TPU v7x, 32 devices: a whole 2x2x4 slice. The times are simulated.
32 devices in a mesh: fsdp: 8 (over z, x), tp: 4 (over y, core).
Axes of the slice: x: 2, y: 2, z: 4, core: 2. Of those that a mesh axis runs over, the one named last changes fastest.
Arguments:
- hidden: bfloat16 [8192, 1536], P(('fsdp', 'tp')), may hold values from -6 to 6
- segment_ids: int32 [8, 1024], P('fsdp'), may hold values from 0 to 4, as said below
- cotangent: bfloat16 [8192, 1536], P(('fsdp', 'tp')), may hold values from -6 to 6
- norm_gain: bfloat16 [2, 1536], P(None, ('fsdp', 'tp')), may hold values from 0.25 to 1.75
- in_zx: bfloat16 [2, 1536, 2, 3072], P(None, 'fsdp', None, 'tp'), may hold values from -0.15625 to 0.15625
- in_dt: bfloat16 [2, 1536, 48], P(None, 'fsdp', 'tp'), may hold values from -0.15625 to 0.15625
- in_bc: bfloat16 [2, 1536, 256], P(None, ('fsdp', 'tp')), may hold values from -0.15625 to 0.15625
- conv_x: bfloat16 [2, 3072, 4], P(None, 'tp'), may hold values from -3 to 3
- conv_x_bias: bfloat16 [2, 3072], P(None, 'tp'), may hold values from -3 to 3
- conv_bc: bfloat16 [2, 256, 4], P(None, ('fsdp', 'tp')), may hold values from -3 to 3
- conv_bc_bias: bfloat16 [2, 256], P(None, ('fsdp', 'tp')), may hold values from -3 to 3
- dt_bias: bfloat16 [2, 48], P(None, 'tp'), may hold values from -6 to -2
- a_log: bfloat16 [2, 48], P(None, 'tp'), may hold values from 0 to 2.765625
- skip_d: bfloat16 [2, 48], P(None, 'tp'), may hold values from 0.5 to 1.5
- gated_gain: bfloat16 [2, 3072], P(None, 'tp'), may hold values from 0.25 to 1.75
- out_wt: bfloat16 [2, 1536, 3072], P(None, 'fsdp', 'tp'), may hold values from -0.109375 to 0.109375
Outputs:
- out_hidden: float32 [8192, 1536], P(('fsdp', 'tp'))
- grad_hidden: float32 [8192, 1536], P(('fsdp', 'tp'))
- grad_norm_gain: float32 [2, 1536], P(None, ('fsdp', 'tp'))
- grad_in_zx: float32 [2, 1536, 2, 3072], P(None, 'fsdp', None, 'tp')
- grad_in_dt: float32 [2, 1536, 48], P(None, 'fsdp', 'tp')
- grad_in_bc: float32 [2, 1536, 256], P(None, ('fsdp', 'tp'))
- grad_conv_x: float32 [2, 3072, 4], P(None, 'tp')
- grad_conv_x_bias: float32 [2, 3072], P(None, 'tp')
- grad_conv_bc: float32 [2, 256, 4], P(None, ('fsdp', 'tp'))
- grad_conv_bc_bias: float32 [2, 256], P(None, ('fsdp', 'tp'))
- grad_dt_bias: float32 [2, 48], P(None, 'tp')
- grad_a_log: float32 [2, 48], P(None, 'tp')
- grad_skip_d: float32 [2, 48], P(None, 'tp')
- grad_gated_gain: float32 [2, 3072], P(None, 'tp')
- grad_out_wt: float32 [2, 1536, 3072], P(None, 'fsdp', 'tp')
Inputs may be any that keep to these rules, and one draw needn't show every extreme that they name: `segment_ids`: along each sequence the ids never fall, start at 0 and end at 4; a document may span several blocks.
All inputs are finite; a program needn't handle non-finite values.
Results may differ from a plain program's by a relative error of at most 0.017.
Values may be sent and summed in bfloat16 or wider, within the bound.
No kernel may reach another device: no remote copies, remote signals or barrier semaphores. Data moves between devices by JAX's collectives and lax.ppermute only.
A program may use at most 256 MiB of HBM per device.

v0:
```python
from functools import partial

import jax
import jax.numpy as jnp
from jax import lax
from jax.sharding import PartitionSpec as P

BLOCK = 256


EPS = 1e-05
HIGH = lax.Precision.HIGHEST


def rms_norm(values, weight):
    return values * lax.rsqrt(jnp.mean(values * values, -1, keepdims=True) + EPS) * weight


def segment_conv(values, weight, offset_bias, segment):
    length = values.shape[0]
    kernel = weight.shape[1]
    result = jnp.zeros_like(values) + offset_bias[None, :]
    for back_by in range(kernel):
        moved = jnp.pad(values, ((back_by, 0), (0, 0)))[:length]
        moved_seg = jnp.pad(segment, (back_by, 0), constant_values=-1)[:length]
        agree = (moved_seg == segment).astype(values.dtype)
        result = result + moved * agree[:, None] * weight[None, :, kernel - 1 - back_by]
    return result


def block_scan(scaled_x, log_decay, b_rows, c_rows, segment):
    length, heads, width = scaled_x.shape
    blocks = length // BLOCK
    where_tok = jnp.arange(BLOCK)
    causal = where_tok[:, None] >= where_tok[None, :]

    def scan_step(carry, pieces):
        running, before_seg = carry
        piece_x, piece_decay, piece_b, piece_c, piece_seg = pieces
        totals = jnp.cumsum(piece_decay, 0)
        joined = (piece_seg[:, None] == piece_seg[None, :]) & causal
        spread = totals[:, None, :] - totals[None, :, :]
        weights = (
            jnp.exp(jnp.where(joined[:, :, None], spread, 0.0))
            * joined.astype(scaled_x.dtype)[:, :, None]
        )
        scores = jnp.dot(piece_c, piece_b.T, precision=HIGH)
        inside = jnp.einsum("tsh,shp->thp", weights * scores[:, :, None], piece_x, precision=HIGH)
        carried = (piece_seg == before_seg).astype(scaled_x.dtype)
        entering = (
            jnp.einsum("tn,hpn->thp", piece_c, running, precision=HIGH)
            * (jnp.exp(totals) * carried[:, None])[:, :, None]
        )
        last_seg = piece_seg[BLOCK - 1]
        tail_rate = (
            jnp.exp(totals[BLOCK - 1][None, :] - totals)
            * (piece_seg == last_seg).astype(scaled_x.dtype)[:, None]
        )
        keep_old = jnp.exp(totals[BLOCK - 1]) * (last_seg == before_seg).astype(scaled_x.dtype)
        running = running * keep_old[:, None, None] + jnp.einsum(
            "sh,shp,sn->hpn", tail_rate, piece_x, piece_b, precision=HIGH
        )
        return ((running, last_seg), inside + entering)

    initial = (jnp.zeros((heads, width, b_rows.shape[1]), scaled_x.dtype), segment[0])
    pieces = (
        scaled_x.reshape(blocks, BLOCK, heads, width),
        log_decay.reshape(blocks, BLOCK, heads),
        b_rows.reshape(blocks, BLOCK, -1),
        c_rows.reshape(blocks, BLOCK, -1),
        segment.reshape(blocks, BLOCK),
    )
    finished, outputs = lax.scan(jax.checkpoint(scan_step), initial, pieces)
    return outputs.reshape(length, heads, width)


def mixer_local(
    gate_z,
    input_x,
    raw_dt,
    raw_bc,
    conv_w,
    conv_b,
    shared_w,
    shared_b,
    dt_shift,
    log_rate,
    skip_gain,
    segment=None,
):
    heads = dt_shift.shape[0]
    length = input_x.shape[0]
    width = input_x.shape[1] // heads
    states = shared_w.shape[0] // 2
    conv_x_out = jax.nn.silu(segment_conv(input_x, conv_w, conv_b, segment))
    conv_bc_out = jax.nn.silu(segment_conv(raw_bc, shared_w, shared_b, segment))
    step_size = jax.nn.softplus(raw_dt + dt_shift[None, :])
    log_decay = -step_size * jnp.exp(log_rate)[None, :]
    signal = conv_x_out.reshape(length, heads, width)
    scanned = block_scan(
        signal * step_size[:, :, None],
        log_decay,
        conv_bc_out[:, :states],
        conv_bc_out[:, states:],
        segment,
    )
    mixed = scanned + skip_gain[None, :, None] * signal
    return mixed.reshape(length, heads * width) * jax.nn.silu(gate_z)


def contract_last(left, right):
    return lax.dot_general(
        left, right, (((1,), (1,)), ((), ())), preferred_element_type=jnp.float32
    )


def contract_first(left, right):
    return lax.dot_general(
        left, right, (((0,), (0,)), ((), ())), preferred_element_type=jnp.float32
    )


def shards(
    hidden,
    segment_ids,
    cotangent,
    norm_gain,
    in_zx,
    in_dt,
    in_bc,
    conv_x,
    conv_x_bias,
    conv_bc,
    conv_bc_bias,
    dt_bias,
    a_log,
    skip_d,
    gated_gain,
    out_wt,
):
    seg_row = segment_ids[0]
    layers = in_zx.shape[0]
    tp_count = lax.axis_size("tp")
    running = hidden.astype(jnp.float32)
    saved = []
    for depth_at in range(layers):
        w_zx, w_dt, w_out = (
            lax.all_gather(in_zx[depth_at], "fsdp", axis=0, tiled=True),
            lax.all_gather(in_dt[depth_at], "fsdp", axis=0, tiled=True),
            lax.all_gather(out_wt[depth_at], "fsdp", axis=0, tiled=True),
        )
        w_bc, gain_pre, conv_shared, bias_shared = (
            lax.all_gather(in_bc[depth_at], ("fsdp", "tp"), axis=0, tiled=True),
            lax.all_gather(norm_gain[depth_at], ("fsdp", "tp"), axis=0, tiled=True),
            lax.all_gather(conv_bc[depth_at], ("fsdp", "tp"), axis=0, tiled=True),
            lax.all_gather(conv_bc_bias[depth_at], ("fsdp", "tp"), axis=0, tiled=True),
        )
        normed, pull_norm = jax.vjp(rms_norm, running, gain_pre.astype(jnp.float32))
        all_rows = lax.all_gather(normed.astype(jnp.bfloat16), "tp", axis=0, tiled=True)
        gate_input = jnp.einsum("td,dkc->tkc", all_rows, w_zx, preferred_element_type=jnp.float32)
        raw_dt = jnp.dot(all_rows, w_dt, preferred_element_type=jnp.float32)
        raw_bc = jnp.dot(all_rows, w_bc, preferred_element_type=jnp.float32)
        mixed, pull_mix = jax.vjp(
            partial(mixer_local, segment=seg_row),
            gate_input[:, 0],
            gate_input[:, 1],
            raw_dt,
            raw_bc,
            conv_x[depth_at].astype(jnp.float32),
            conv_x_bias[depth_at].astype(jnp.float32),
            conv_shared.astype(jnp.float32),
            bias_shared.astype(jnp.float32),
            dt_bias[depth_at].astype(jnp.float32),
            a_log[depth_at].astype(jnp.float32),
            skip_d[depth_at].astype(jnp.float32),
        )
        squares = lax.psum(jnp.sum(mixed * mixed, -1), "tp")
        inner_width = mixed.shape[1] * tp_count
        norm_scale = lax.rsqrt(squares / inner_width + EPS)
        post_gain = gated_gain[depth_at].astype(jnp.float32)
        gated = (mixed * norm_scale[:, None] * post_gain[None, :]).astype(jnp.bfloat16)
        branch_out = lax.psum_scatter(
            contract_last(gated, w_out), "tp", scatter_dimension=0, tiled=True
        )
        saved.append(
            (
                pull_norm,
                pull_mix,
                all_rows,
                mixed,
                norm_scale,
                gated,
                (w_zx, w_dt, w_out),
                w_bc,
                inner_width,
            )
        )
        running = running + branch_out
    grad_run = cotangent.astype(jnp.float32)
    collected = [[None] * layers for index_at in range(13)]
    for depth_at in reversed(range(layers)):
        pull_norm, pull_mix, all_rows, mixed, norm_scale, gated, kept_weights, w_bc, inner_width = (
            saved[depth_at]
        )
        w_zx, w_dt, w_out = (
            lax.all_gather(in_zx[depth_at], "fsdp", axis=0, tiled=True),
            lax.all_gather(in_dt[depth_at], "fsdp", axis=0, tiled=True),
            lax.all_gather(out_wt[depth_at], "fsdp", axis=0, tiled=True),
        )
        cot_rows = lax.all_gather(grad_run.astype(jnp.bfloat16), "tp", axis=0, tiled=True)
        d_gated = jnp.dot(cot_rows, w_out, preferred_element_type=jnp.float32)
        d_w_out = contract_first(cot_rows, gated)
        post_gain = gated_gain[depth_at].astype(jnp.float32)
        d_post_gain = jnp.sum(d_gated * mixed * norm_scale[:, None], 0)
        d_unit = d_gated * post_gain[None, :]
        cross = lax.psum(jnp.sum(d_unit * mixed, -1), "tp")
        d_mixed = (
            d_unit * norm_scale[:, None] - mixed * (norm_scale**3 * cross / inner_width)[:, None]
        )
        (
            d_gate_z,
            d_input_x,
            d_raw_dt,
            d_raw_bc,
            d_conv_w,
            d_conv_b,
            d_shared_w,
            d_shared_b,
            d_dt_shift,
            d_log_rate,
            d_skip,
        ) = pull_mix(d_mixed)
        d_gate_in = jnp.stack([d_gate_z, d_input_x], 1).astype(jnp.bfloat16)
        d_dt_low = d_raw_dt.astype(jnp.bfloat16)
        d_bc_low = d_raw_bc.astype(jnp.bfloat16)
        d_w_zx = jnp.einsum("td,tkc->dkc", all_rows, d_gate_in, preferred_element_type=jnp.float32)
        d_w_dt = contract_first(all_rows, d_dt_low)
        d_w_bc = contract_first(all_rows, d_bc_low)
        total_back = jnp.einsum("tkc,dkc->td", d_gate_in, w_zx, preferred_element_type=jnp.float32)
        total_back = total_back + contract_last(d_dt_low, w_dt)
        d_normed = lax.psum_scatter(
            (total_back + contract_last(d_bc_low, w_bc)).astype(jnp.bfloat16),
            "tp",
            scatter_dimension=0,
            tiled=True,
        ).astype(jnp.float32)
        d_state, d_pre_gain = pull_norm(d_normed)
        grad_run = grad_run + d_state
        sum_zx, sum_dt, sum_out = (
            lax.psum_scatter(
                d_w_zx.astype(jnp.bfloat16), "fsdp", scatter_dimension=0, tiled=True
            ).astype(jnp.float32),
            lax.psum_scatter(
                d_w_dt.astype(jnp.bfloat16), "fsdp", scatter_dimension=0, tiled=True
            ).astype(jnp.float32),
            lax.psum_scatter(
                d_w_out.astype(jnp.bfloat16), "fsdp", scatter_dimension=0, tiled=True
            ).astype(jnp.float32),
        )
        sum_bc, sum_pre, sum_shared_w, sum_shared_b = (
            lax.psum_scatter(d_w_bc, ("fsdp", "tp"), scatter_dimension=0, tiled=True),
            lax.psum_scatter(d_pre_gain, ("fsdp", "tp"), scatter_dimension=0, tiled=True),
            lax.psum_scatter(d_shared_w, ("fsdp", "tp"), scatter_dimension=0, tiled=True),
            lax.psum_scatter(d_shared_b, ("fsdp", "tp"), scatter_dimension=0, tiled=True),
        )
        sum_conv_w, sum_conv_b, sum_dt_shift, sum_log_rate, sum_skip, sum_post = lax.psum(
            (d_conv_w, d_conv_b, d_dt_shift, d_log_rate, d_skip, d_post_gain), "fsdp"
        )
        layer_grads = (
            sum_pre,
            sum_zx,
            sum_dt,
            sum_bc,
            sum_conv_w,
            sum_conv_b,
            sum_shared_w,
            sum_shared_b,
            sum_dt_shift,
            sum_log_rate,
            sum_skip,
            sum_post,
            sum_out,
        )
        for index_at in range(13):
            collected[index_at][depth_at] = layer_grads[index_at]
    stacked = [jnp.stack(collected[index_at], 0) for index_at in range(13)]
    return (
        running,
        grad_run,
        stacked[0],
        stacked[1],
        stacked[2],
        stacked[3],
        stacked[4],
        stacked[5],
        stacked[6],
        stacked[7],
        stacked[8],
        stacked[9],
        stacked[10],
        stacked[11],
        stacked[12],
    )


def solution(mesh):
    placed = (
        P(("fsdp", "tp"), None),
        P("fsdp", None),
        P(("fsdp", "tp"), None),
        P(None, ("fsdp", "tp")),
        P(None, "fsdp", None, "tp"),
        P(None, "fsdp", "tp"),
        P(None, ("fsdp", "tp"), None),
        P(None, "tp", None),
        P(None, "tp"),
        P(None, ("fsdp", "tp"), None),
        P(None, ("fsdp", "tp")),
        P(None, "tp"),
        P(None, "tp"),
        P(None, "tp"),
        P(None, "tp"),
        P(None, "fsdp", "tp"),
    )
    return jax.shard_map(
        shards,
        mesh=mesh,
        in_specs=placed,
        out_specs=(
            P(("fsdp", "tp"), None),
            P(("fsdp", "tp"), None),
            P(None, ("fsdp", "tp")),
            P(None, "fsdp", None, "tp"),
            P(None, "fsdp", "tp"),
            P(None, ("fsdp", "tp"), None),
            P(None, "tp", None),
            P(None, "tp"),
            P(None, ("fsdp", "tp"), None),
            P(None, ("fsdp", "tp")),
            P(None, "tp"),
            P(None, "tp"),
            P(None, "tp"),
            P(None, "tp"),
            P(None, "fsdp", "tp"),
        ),
        check_vma=False,
    )
```

profile of v0, /device:TPU:0, one launch (start us, length us, event | category | flops | bytes accessed | tf_op | source)
XLA Modules:
  0.0 2126.9 jit_solution(4967290858055655296)
XLA Ops:
  9.6 42.2 %all-reduce.63 = (bf16[1536]{0:T(1024)(128)(2,1)S(1)}, bf16[256]{0:T(256)(128)(2,1)S(1)}, bf16[1536]{0:T(1024)(128)(2,1)}, bf16[256]{0:T(256)(128)(2,1)}) all-reduce(bf16[1536]{0:T(1024)(128)(2,1)S(1)} %dynamic-update-slice, bf16[256]{0:T(256)(128)(2,1)S(1)} %dynamic-update-slice.1, ...), channel_id=2, replica_groups=mesh['fsdp'=8,'tp'=4] {'fsdp','tp'}, use_global_device_ids=true, to_apply=%add.51 | all-reduce | flops 3584 | bytes 14336
  63.6 32.2 %all-gather.1 = bf16[1,1536,12]{2,0,1:T(2,128)(2,1)S(1)} all-gather(bf16[1,192,12]{2,0,1:T(2,128)(2,1)S(1)} %copy.390), channel_id=3, replica_groups=mesh['fsdp'=8,'tp'=4] {'fsdp'}, dimensions={1}, use_global_device_ids=true | all-gather | bytes 41472 | tf_op jit(solution)/shard_map/all_gather | solution.py:149
  99.1 48.6 %all-gather.4 = bf16[1,1536,256]{2,1,0:T(8,128)(2,1)} all-gather(bf16[1,48,256]{2,1,0:T(8,128)(2,1)S(1)} %get-tuple-element.1703), channel_id=6, replica_groups=mesh['fsdp'=8,'tp'=4] {'fsdp','tp'}, dimensions={1}, use_global_device_ids=true | all-gather | bytes 811008 | tf_op jit(solution)/shard_map/all_gather | solution.py:153
  149.0 37.7 %all-gather.5 = bf16[1,256,4]{2,0,1:T(2,128)(2,1)S(1)} all-gather(bf16[1,8,4]{2,0,1:T(2,128)(2,1)S(1)} %copy.392), channel_id=7, replica_groups=mesh['fsdp'=8,'tp'=4] {'fsdp','tp'}, dimensions={1}, use_global_device_ids=true | all-gather | bytes 2112 | tf_op jit(solution)/shard_map/all_gather | solution.py:155
  234.5 140.5 %while.86 = (s32[]{:T(128)}, f32[12,64,128]{2,1,0:T(8,128)S(1)}, s32[]{:T(128)}, f32[4,256,12,64]{1,0,3,2:T(4,128)}, f32[4,12,64,128]{3,2,1,0:T(8,128)}, /*index...) while((s32[]{:T(128)}, f32[12,64,128]{2,1,0:T(8,128)S(1)}, ...), condition=%wide.region_4.6_spmd.clone, body=%wide.region_1.5_spmd.clone.sunk | while | flops 1313515520 | bytes 11072187 | solution.py:73
  405.3 52.8 %reduce-scatter.19.cloned.1.call-done = f32[256,1536]{1,0:T(8,128)} async-done(((f32[1024,1536]{1,0:T(8,128)}), f32[256,1536]{1,0:T(8,128)}) %reduce-scatter.19.cloned.1.call-update) | async-done | bytes 1572880 | tf_op jit(solution)/shard_map/reduce_scatter | solution.py:182
  463.9 34.3 %all-gather.8 = bf16[1,1536,12]{2,0,1:T(2,128)(2,1)S(1)} all-gather(bf16[1,192,12]{2,0,1:T(2,128)(2,1)S(1)} %copy.393), channel_id=10, replica_groups=mesh['fsdp'=8,'tp'=4] {'fsdp'}, dimensions={1}, use_global_device_ids=true | all-gather | bytes 41472 | tf_op jit(solution)/shard_map/all_gather | solution.py:149
  499.7 48.7 %all-gather.11 = bf16[1,1536,256]{2,1,0:T(8,128)(2,1)} all-gather(bf16[1,48,256]{2,1,0:T(8,128)(2,1)S(1)} %copy-done.101), channel_id=13, replica_groups=mesh['fsdp'=8,'tp'=4] {'fsdp','tp'}, dimensions={1}, use_global_device_ids=true | all-gather | bytes 811008 | tf_op jit(solution)/shard_map/all_gather | solution.py:153
  549.1 37.4 %all-gather.12 = bf16[1,256,4]{2,0,1:T(2,128)(2,1)S(1)} all-gather(bf16[1,8,4]{2,0,1:T(2,128)(2,1)S(1)} %copy.395), channel_id=14, replica_groups=mesh['fsdp'=8,'tp'=4] {'fsdp','tp'}, dimensions={1}, use_global_device_ids=true | all-gather | bytes 2112 | tf_op jit(solution)/shard_map/all_gather | solution.py:155
  625.9 132.1 %while.87 = (s32[]{:T(128)}, f32[12,64,128]{2,1,0:T(8,128)S(1)}, s32[]{:T(128)}, f32[4,256,12,64]{1,0,3,2:T(4,128)}, f32[4,12,64,128]{3,2,1,0:T(8,128)}, /*index...) while((s32[]{:T(128)}, f32[12,64,128]{2,1,0:T(8,128)S(1)}, ...), condition=%wide.region_12.14_spmd.clone, body=%wide.region_9.13_spmd.clone.sunk | while | flops 1313515520 | bytes 11072187 | solution.py:73
  637.5 18.0 dynamic_update_slice.145
  811.2 209.0 %while.88 = (s32[]{:T(128)}, f32[12,64,128]{2,1,0:T(8,128)S(1)}, f32[4,256,12,64]{1,0,3,2:T(4,128)}, f32[4,256,12]{1,0,2:T(4,128)}, f32[4,256,128]{2,1,0:T(8,128...) while((s32[]{:T(128)}, f32[12,64,128]{2,1,0:T(8,128)S(1)}, ...), condition=%wide.region_29.31_spmd.clone, body=%wide.region_18.30_spmd.clone.sunk | while | flops 3035048960 | bytes 29864308 | solution.py:73
  1070.0 34.1 %reduce-scatter.23.cloned.1.call-done = bf16[256,1536]{1,0:T(8,128)(2,1)} async-done(((bf16[1024,1536]{1,0:T(8,128)(2,1)}), bf16[256,1536]{1,0:T(8,128)(2,1)}) %reduce-scatter.23.cloned.1.call-update) | async-done | bytes 786448 | tf_op jit(solution)/shard_map/reduce_scatter | solution.py:241
  1113.0 25.1 %all-gather.29.cloned.1.call-done = bf16[1024,1536]{1,0:T(8,128)(2,1)} async-done(((bf16[256,1536]{1,0:T(8,128)(2,1)}), bf16[1024,1536]{1,0:T(8,128)(2,1)}) %all-gather.29.cloned.1.call-update) | async-done | bytes 3145744 | tf_op jit(solution)/shard_map/all_gather | solution.py:210
  1172.3 224.9 %while.89 = (s32[]{:T(128)}, f32[12,64,128]{2,1,0:T(8,128)S(1)}, f32[4,256,12,64]{1,0,3,2:T(4,128)}, f32[4,256,12]{1,0,2:T(4,128)}, f32[4,256,128]{2,1,0:T(8,128...) while((s32[]{:T(128)}, f32[12,64,128]{2,1,0:T(8,128)S(1)}, ...), condition=%wide.region_46.48_spmd.clone, body=%wide.region_35.47_spmd.clone.sunk | while | flops 3035048960 | bytes 29479540 | solution.py:73
  1501.4 38.0 %all-reduce.62 = (f32[1,768,4]{1,2,0:T(4,128)S(1)}, f32[1,768,4]{1,2,0:T(4,128)S(1)}, f32[1,768]{1,0:T(1,128)S(1)}, f32[1,768]{1,0:T(1,128)S(1)}, f32[1,12]{1,0:...) all-reduce(f32[1,768,4]{1,2,0:T(4,128)S(1)} %add_bitcast_fusion.2, ...), channel_id=1, replica_groups=mesh['fsdp'=8,'tp'=4] {'fsdp'}, use_global_device_ids=true, to_apply=%region_69.71 | all-reduce | flops 9288 | bytes 74304 | tf_op jit(solution)/shard_map/psum | solution.py:266
  1543.3 28.2 %reduce-scatter.33.cloned.1.call-done = f32[48,256]{1,0:T(8,128)} async-done(((f32[1536,256]{1,0:T(8,128)}), f32[48,256]{1,0:T(8,128)}) %reduce-scatter.33.cloned.1.call-update) | async-done | bytes 49168 | tf_op jit(solution)/shard_map/reduce_scatter | solution.py:261
  1571.6 101.2 %reduce-scatter.31.cloned.1.call-done = f32[48,256]{1,0:T(8,128)} async-done(((f32[1536,256]{1,0:T(8,128)}), f32[48,256]{1,0:T(8,128)}) %reduce-scatter.31.cloned.1.call-update) | async-done | bytes 49168 | tf_op jit(solution)/shard_map/reduce_scatter | solution.py:261
  1674.2 70.5 %reduce-scatter.37.cloned.1.call-done = bf16[192,768]{1,0:T(8,128)(2,1)} async-done(((bf16[1536,768]{1,0:T(8,128)(2,1)}), bf16[192,768]{1,0:T(8,128)(2,1)}) %reduce-scatter.37.cloned.1.call-update) | async-done | bytes 294928 | tf_op jit(solution)/shard_map/reduce_scatter | solution.py:256
  1744.7 71.6 %reduce-scatter.35.cloned.1.call-done = bf16[192,768]{1,0:T(8,128)(2,1)} async-done(((bf16[1536,768]{1,0:T(8,128)(2,1)}), bf16[192,768]{1,0:T(8,128)(2,1)}) %reduce-scatter.35.cloned.1.call-update) | async-done | bytes 294928 | tf_op jit(solution)/shard_map/reduce_scatter | solution.py:256
  1818.5 37.3 %reduce-scatter.25.cloned.1.call-done = bf16[256,1536]{1,0:T(8,128)(2,1)} async-done(((bf16[1024,1536]{1,0:T(8,128)(2,1)}), bf16[256,1536]{1,0:T(8,128)(2,1)}) %reduce-scatter.25.cloned.1.call-update) | async-done | bytes 786448 | tf_op jit(solution)/shard_map/reduce_scatter | solution.py:241
  1857.6 40.0 %all-reduce.61 = (f32[1536]{0:T(1024)S(1)}, f32[1536]{0:T(1024)S(1)}, f32[256,4]{0,1:T(4,128)S(1)}, f32[256,4]{0,1:T(4,128)S(1)}, f32[256]{0:T(256)S(1)}, /*index=5*/f32[256]{0:T(256)S(1)}) all-reduce(f32[1536]{0:T(1024)S(1)} %copy-done.129, ...), channel_id=21, replica_groups=mesh['fsdp'=8,'tp'=4] {'fsdp','tp'}, use_global_device_ids=true, to_apply=%region_53.55.clone | all-reduce | flops 5632 | bytes 45056
  1921.9 94.6 %reduce-scatter.29.cloned.1.call-done = bf16[192,2,768]{2,0,1:T(8,128)(2,1)} async-done(((bf16[1536,2,768]{2,0,1:T(8,128)(2,1)}), bf16[192,2,768]{2,0,1:T(8,128)(2,1)}) %reduce-scatter.29.cloned.1.call-update) | async-done | bytes 589840 | tf_op jit(solution)/shard_map/reduce_scatter | solution.py:250
  2016.4 98.5 %reduce-scatter.27.cloned.1.call-done = bf16[192,2,768]{2,0,1:T(8,128)(2,1)} async-done(((bf16[1536,2,768]{2,0,1:T(8,128)(2,1)}), bf16[192,2,768]{2,0,1:T(8,128)(2,1)}) %reduce-scatter.27.cloned.1.call-update) | async-done | bytes 589840 | tf_op jit(solution)/shard_map/reduce_scatter | solution.py:250
  (1420 shorter events, 1092.5 us)
Async XLA Ops:
  7.2 184.3 %all-gather.23.cloned.1.call-start = ((), (), s32[]{:S(2)}) async-start(), calls=%async_computation.12 | async-start | bytes 3932160 | tf_op jit(solution)/shard_map/all_gather | solution.py:159
  56.7 149.0 %all-gather.31.cloned.1.call-start = ((), (), s32[]{:S(2)}) async-start(), calls=%async_computation.26 | async-start | bytes 5308416 | tf_op jit(solution)/shard_map/all_gather | solution.py:148
  59.3 335.9 %all-gather.33.cloned.1.call-start = ((), (), s32[]{:S(2)}) async-start(), calls=%async_computation.27 | async-start | bytes 2654208 | tf_op jit(solution)/shard_map/all_gather | solution.py:150
  60.2 397.8 %reduce-scatter.19.cloned.1.call-start = ((), (), s32[]{:S(2)}) async-start(), calls=%async_computation.13 | async-start | bytes 7864320 | tf_op jit(solution)/shard_map/reduce_scatter | solution.py:182
  60.9 559.2 %copy-start.73 = (f32[1024]{0:T(1024)}, f32[1024]{0:T(1024)S(1)}, u32[]{:S(2)}) copy-start(f32[1024]{0:T(1024)S(1)} %get-tuple-element.1709) | copy-start | bytes 12292
  60.9 559.2 %copy-start.76 = (f32[1024]{0:T(1024)}, f32[1024]{0:T(1024)S(1)}, u32[]{:S(2)}) copy-start(f32[1024]{0:T(1024)S(1)} %get-tuple-element.1710) | copy-start | bytes 12292
  61.0 559.2 %copy-start.80 = (f32[1024]{0:T(1024)}, f32[1024]{0:T(1024)S(1)}, u32[]{:S(2)}) copy-start(f32[1024]{0:T(1024)S(1)} %get-tuple-element.1708) | copy-start | bytes 12292
  403.2 184.5 %all-gather.35.cloned.1.call-start = ((), (), s32[]{:S(2)}) async-start(), calls=%async_computation.28 | async-start | bytes 5308416 | tf_op jit(solution)/shard_map/all_gather | solution.py:148
  405.2 182.5 %all-gather.25.cloned.1.call-start = ((), (), s32[]{:S(2)}) async-start(), calls=%async_computation.14 | async-start | bytes 3932160 | tf_op jit(solution)/shard_map/all_gather | solution.py:159
  462.0 316.6 %all-gather.37.cloned.1.call-start = ((), (), s32[]{:S(2)}) async-start(), calls=%async_computation.29 | async-start | bytes 2654208 | tf_op jit(solution)/shard_map/all_gather | solution.py:150
  462.8 315.8 %all-gather.27.cloned.1.call-start = ((), (), s32[]{:S(2)}) async-start(), calls=%async_computation.16 | async-start | bytes 3932160 | tf_op jit(solution)/shard_map/all_gather | solution.py:210
  463.5 640.6 %reduce-scatter.23.cloned.1.call-start = ((), (), s32[]{:S(2)}) async-start(), calls=%async_computation.17 | async-start | bytes 3932160 | tf_op jit(solution)/shard_map/reduce_scatter | solution.py:241
  1070.0 68.2 %all-gather.29.cloned.1.call-start = ((), (), s32[]{:S(2)}) async-start(), calls=%async_computation.18 | async-start | bytes 3932160 | tf_op jit(solution)/shard_map/all_gather | solution.py:210
  1109.5 390.5 %reduce-scatter.41.cloned.1.call-start = ((), (), s32[]{:S(2)}) async-start(), calls=%async_computation.31 | async-start | bytes 442368
  1113.0 428.8 %reduce-scatter.39.cloned.1.call-start = ((), (), s32[]{:S(2)}) async-start(), calls=%async_computation.30 | async-start | bytes 442368
  1407.4 164.1 %reduce-scatter.33.cloned.1.call-start = ((), (), s32[]{:S(2)}) async-start(), calls=%async_computation.23 | async-start | bytes 1622016 | tf_op jit(solution)/shard_map/reduce_scatter | solution.py:261
  1410.8 262.0 %reduce-scatter.31.cloned.1.call-start = ((), (), s32[]{:S(2)}) async-start(), calls=%async_computation.22 | async-start | bytes 1622016 | tf_op jit(solution)/shard_map/reduce_scatter | solution.py:261
  1421.9 322.8 %reduce-scatter.37.cloned.1.call-start = ((), (), s32[]{:S(2)}) async-start(), calls=%async_computation.25 | async-start | bytes 2654208 | tf_op jit(solution)/shard_map/reduce_scatter | solution.py:256
  1429.2 387.1 %reduce-scatter.35.cloned.1.call-start = ((), (), s32[]{:S(2)}) async-start(), calls=%async_computation.24 | async-start | bytes 2654208 | tf_op jit(solution)/shard_map/reduce_scatter | solution.py:256
  1435.7 420.1 %reduce-scatter.25.cloned.1.call-start = ((), (), s32[]{:S(2)}) async-start(), calls=%async_computation.19 | async-start | bytes 3932160 | tf_op jit(solution)/shard_map/reduce_scatter | solution.py:241
  1469.6 447.9 %reduce-scatter.21.cloned.1.call-start = ((), (), s32[]{:S(2)}) async-start(), calls=%async_computation.15 | async-start | bytes 7864320 | tf_op jit(solution)/shard_map/reduce_scatter | solution.py:182
  1477.9 538.5 %reduce-scatter.29.cloned.1.call-start = ((), (), s32[]{:S(2)}) async-start(), calls=%async_computation.21 | async-start | bytes 5308416 | tf_op jit(solution)/shard_map/reduce_scatter | solution.py:250
  1488.5 626.5 %reduce-scatter.27.cloned.1.call-start = ((), (), s32[]{:S(2)}) async-start(), calls=%async_computation.20 | async-start | bytes 5308416 | tf_op jit(solution)/shard_map/reduce_scatter | solution.py:250
  1499.2 418.3 %copy-start.7 = (f32[256,1536]{1,0:T(8,128)S(1)}, f32[256,1536]{1,0:T(8,128)}, u32[]{:S(2)}) copy-start(f32[256,1536]{1,0:T(8,128)} %copy-done.5) | copy-start | bytes 4718596
  (254 other events, 7134.9 us)
Sparse Core Ops, SparseCore 0:
  56.8 28.7 all-gather.22
  88.4 83.2 all-gather.30
  174.4 50.8 all-gather.32
  403.4 54.6 reduce-scatter.18
  460.4 89.2 all-gather.34
  551.7 28.5 all-gather.24
  582.7 52.0 all-gather.36
  636.4 27.0 all-gather.26
  1070.1 33.9 reduce-scatter.22
  1109.6 28.5 all-gather.28
  1141.5 61.3 reduce-scatter.40
  1407.5 62.4 reduce-scatter.38
  1475.3 96.2 reduce-scatter.32
  1576.7 96.0 reduce-scatter.30
  1676.7 68.0 reduce-scatter.36
  1748.1 68.2 reduce-scatter.34
  1818.7 36.9 reduce-scatter.24
  1858.3 59.1 reduce-scatter.20
  1921.1 95.2 reduce-scatter.28
  2019.9 95.0 reduce-scatter.26
where the time goes:
time: 2140 us; the launch traced here: 2130 us
  waiting for transfers between devices  634 us (30%)
  local copies, waits for them, and re-layouts  564 us (26%)
  blocking collectives  386 us (18%)
  matrix products  315 us (15%)
  other arithmetic  183 us (9%)
  loops' own time  25.9 us (1%)
    dynamic_update_slice x56, local copies, waits for them, and re-layouts, block_scan(): finished, outputs = lax.scan(jax.checkpoint(scan_step), initial, pieces)  317 us
    reduce_scatter x2, waiting for transfers between devices, shards(): lax.psum_scatter(d_w_zx.astype(jnp.bfloat16), 'fsdp', scatter_dimension=0...  193 us
    reduce_scatter x2, waiting for transfers between devices, shards(): lax.psum_scatter(d_w_out.astype(jnp.bfloat16), 'fsdp', scatter_dimension=...  142 us
    reduce_scatter x2, waiting for transfers between devices, shards(): lax.psum_scatter(d_w_bc, ('fsdp', 'tp'), scatter_dimension=0, tiled=True)  129 us
    dot_general x24, matrix products, scan_step(): jnp.einsum('tsh,shp->thp', weights * scores[:, :, None], piece_x, precisi...  108 us
    all_gather x2, blocking collectives, shards(): lax.all_gather(in_bc[depth_at], ('fsdp', 'tp'), axis=0, tiled=True)  97.3 us
    unnamed x2, blocking collectives  82.1 us
    all_gather x2, blocking collectives, shards(): lax.all_gather(conv_bc[depth_at], ('fsdp', 'tp'), axis=0, tiled=True)  75.1 us
  transfers between devices with their start and end apart: 20, of which 11 were waited for; matrix products, arithmetic and copies ran while one was open for 35% of the time, Pallas kernels for 0%

commit v1 on v0

v1 whole, which is shorter than its diff:
```python
import jax
import jax.numpy as jnp
from jax import lax
from jax.experimental import pallas as pl
from jax.experimental.pallas import tpu as pltpu
from jax.sharding import PartitionSpec as P

EPS = 1e-05
NEG = -1e30
F32 = jnp.float32
BF16 = jnp.bfloat16
WALK = (0, 2, 4, 6, 7, 5, 3, 1)
HEAD_ROWS = 16
VMEM = 56 * 1024 * 1024


def tp_swap(value, mask):
    size = lax.axis_size("tp")
    return lax.ppermute(value, "tp", [(at, at ^ mask) for at in range(size)])


def tp_gather(value):
    core = tp_swap(value, 1)
    across = tp_swap(value, 2)
    return [value, core, across, tp_swap(across, 1)]


def tp_reduce_own(slots):
    near = tp_swap(jnp.stack([slots[1], slots[3]]), 1)
    far = (slots[2].astype(F32) + near[1].astype(F32)).astype(slots[2].dtype)
    far = tp_swap(far, 2)
    return slots[0].astype(F32) + near[0].astype(F32) + far.astype(F32)


def tp_sum_slots(value):
    near = tp_swap(value, 1)
    value = value + jnp.stack([near[1], near[0], near[3], near[2]])
    far = tp_swap(value, 2)
    return value + jnp.stack([far[2], far[3], far[0], far[1]])


def tp_natural(slots, index):
    odd = (index & 1) == 1
    high = (index & 2) == 2
    pairs = [
        jnp.where(odd, slots[1], slots[0]),
        jnp.where(odd, slots[0], slots[1]),
        jnp.where(odd, slots[3], slots[2]),
        jnp.where(odd, slots[2], slots[3]),
    ]
    return [
        jnp.where(high, pairs[2], pairs[0]),
        jnp.where(high, pairs[3], pairs[1]),
        jnp.where(high, pairs[0], pairs[2]),
        jnp.where(high, pairs[1], pairs[3]),
    ]


def is_walk():
    return lax.axis_size("fsdp") == len(WALK)


def step_ring(value, by):
    size = len(WALK)
    return lax.ppermute(
        value, "fsdp", [(WALK[at], WALK[(at + by) % size]) for at in range(size)]
    )


def fsdp_gather(value):
    if not is_walk():
        return lax.all_gather(value, "fsdp", axis=0, tiled=False)
    half = value.shape[0] // 2
    ahead = behind = value
    slots = {0: value}
    for step in (1, 2, 3):
        behind = step_ring(behind, 1)
        ahead = step_ring(ahead, -1)
        slots[8 - step] = behind
        slots[step] = ahead
    slots[4] = jnp.concatenate(
        [step_ring(behind[:half], 1), step_ring(ahead[half:], -1)], 0
    )
    return jnp.stack([slots[at] for at in range(8)])


def fsdp_reduce(terms):
    if not is_walk():
        return lax.psum_scatter(terms, "fsdp", scatter_dimension=0, tiled=False).astype(F32)
    half = terms.shape[1] // 2
    kind = terms.dtype

    def add(left, right):
        return (left.astype(F32) + right.astype(F32)).astype(kind)

    forth = step_ring(terms[4, :half], 1)
    back = step_ring(terms[4, half:], -1)
    forth = step_ring(
        jnp.concatenate([add(terms[3, :half], forth), terms[3, half:]], 0), 1
    )
    back = step_ring(
        jnp.concatenate([terms[5, :half], add(terms[5, half:], back)], 0), -1
    )
    for step in (2, 1):
        forth = step_ring(add(terms[step], forth), 1)
        back = step_ring(add(terms[8 - step], back), -1)
    return terms[0].astype(F32) + forth.astype(F32) + back.astype(F32)


def fsdp_sum(value):
    if not is_walk():
        return lax.psum(value, "fsdp")

    def swap(item, mask):
        return lax.ppermute(item, "fsdp", [(at, at ^ mask) for at in range(8)])

    value = value + swap(value, 1)
    return value + swap(value, 2) + swap(value, 4) + swap(value, 6)


def walk_place():
    index = lax.axis_index("fsdp")
    place = jnp.zeros((), jnp.int32)
    for at, owner in enumerate(WALK):
        place = jnp.where(index == owner, at, place)
    return place


def to_walk(blocks, place):
    if not is_walk():
        return blocks
    ordered = [blocks[owner] for owner in WALK]
    for bit in (1, 2, 4):
        turn = (place & bit) == bit
        ordered = [jnp.where(turn, ordered[(at + bit) % 8], ordered[at]) for at in range(8)]
    return ordered


def from_walk(blocks, place):
    if not is_walk():
        return blocks
    for bit in (1, 2, 4):
        turn = (place & bit) == bit
        blocks = [jnp.where(turn, blocks[(at - bit) % 8], blocks[at]) for at in range(8)]
    natural = [None] * 8
    for at, owner in enumerate(WALK):
        natural[owner] = blocks[at]
    return natural


def columns_to_walk(value, place):
    count = lax.axis_size("fsdp")
    return jnp.concatenate(to_walk(jnp.split(value, count, 1), place), 1)


def columns_from_walk(value, place):
    count = lax.axis_size("fsdp")
    return jnp.concatenate(from_walk(jnp.split(value, count, 1), place), 1)


def dot(left, right):
    return jnp.dot(left, right, preferred_element_type=F32)


def dot_t(left, right):
    return lax.dot_general(left, right, (((1,), (1,)), ((), ())), preferred_element_type=F32)


def shifted_sum(value, sign):
    width = value.shape[1]
    lane = lax.broadcasted_iota(jnp.int32, value.shape, 1)
    by = 1
    while by < width:
        if sign > 0:
            value = value + jnp.where(lane >= by, pltpu.roll(value, by, 1), 0.0)
        else:
            value = value + jnp.where(lane < width - by, pltpu.roll(value, width - by, 1), 0.0)
        by *= 2
    return value


def conv_parts(cur, prev, weight, bias, marks):
    rows = cur.shape[0]
    ext = jnp.concatenate([prev, cur], 0)
    pre = bias + cur * weight[3:4]
    moved = []
    for back in (1, 2, 3):
        item = ext[8 - back : 8 - back + rows]
        moved.append(item)
        pre = pre + item * marks[back - 1] * weight[3 - back : 4 - back]
    return pre, moved


def rates(u, bias, rate, seg_rows):
    u = u + bias
    dt = jnp.maximum(u, 0.0) + jnp.log1p(jnp.exp(-jnp.abs(u)))
    log_dt = jnp.where(u < -15.0, u, jnp.log(dt))
    a = -dt * rate
    total = shifted_sum(a, 1)
    last = total[:, -1:]
    less = total - log_dt
    enter = jnp.exp(total) * seg_rows[1:2]
    tail = jnp.exp(last - less) * seg_rows[2:3]
    return u, dt, a, total, less, enter, tail


def as_columns(first, enter, tail):
    enter_hi = enter.astype(BF16).astype(F32)
    tail_hi = tail.astype(BF16).astype(F32)
    rest = jnp.zeros((128 - 5 * HEAD_ROWS, enter.shape[1]), F32)
    stacked = jnp.concatenate(
        [first, enter_hi, tail_hi, enter - enter_hi, tail - tail_hi, rest], 0
    )
    return stacked.T


def pair_masks(rows):
    lane = lax.broadcasted_iota(jnp.int32, (rows, 128), 1)
    return lane < 64, lane >= 64


def mix_forward(
    t_ref, x_ref, bc_ref, u_ref, sc_ref, sr_ref, cw_ref, cb_ref, bw_ref, bb_ref,
    db_ref, rate_ref, skip_ref, spread_ref, y_ref, state_ref, held, x_tail, bc_tail,
):
    del t_ref
    rows = x_ref.shape[1]
    pairs = x_ref.shape[2] // 128

    @pl.when(pl.program_id(0) == 0)
    def _():
        held[...] = jnp.zeros_like(held)
        x_tail[...] = jnp.zeros_like(x_tail)
        bc_tail[...] = jnp.zeros_like(bc_tail)

    sc = sc_ref[0]
    sr = sr_ref[0]
    marks = [sc[:, at : at + 1] for at in range(3)]
    x = x_ref[0]
    pre, _ = conv_parts(x, x_tail[...], cw_ref[...], cb_ref[...], marks)
    xc = pre * jax.nn.sigmoid(pre)
    x_tail[...] = x[rows - 8 :]
    raw = bc_ref[0]
    pre_bc, _ = conv_parts(raw, bc_tail[...], bw_ref[...], bb_ref[...], marks)
    bc = (pre_bc * jax.nn.sigmoid(pre_bc)).astype(BF16)
    bc_tail[...] = raw[rows - 8 :]
    states = bc.shape[1] // 2
    b_rows, c_rows = bc[:, :states], bc[:, states:]

    _, _, _, total, less, enter, tail = rates(u_ref[0], db_ref[...], rate_ref[...], sr)
    cols = as_columns(total, enter, tail)
    cols_low = cols.astype(BF16)
    enter_x = dot(cols_low, spread_ref[0])
    tail_x = dot(cols_low, spread_ref[1])

    at_t = lax.broadcasted_iota(jnp.int32, (rows, rows), 0)
    at_s = lax.broadcasted_iota(jnp.int32, (rows, rows), 1)
    bar = jnp.where((sc[:, 3:4] == sr[0:1]) & (at_t >= at_s), 0.0, NEG)
    scores = dot_t(c_rows, b_rows)
    state = held[...]
    state_ref[0] = state
    entering = dot(c_rows, state.astype(BF16)) * enter_x
    xl = xc.astype(BF16)
    low_mask, high_mask = pair_masks(rows)
    zero = jnp.zeros((rows, 128), BF16)
    for pair in range(pairs):
        span = slice(pair * 128, pair * 128 + 128)
        part = xl[:, span]
        acc = entering[:, span] + xc[:, span] * skip_ref[:, span]
        for side, mask in ((0, low_mask), (1, high_mask)):
            head = 2 * pair + side
            weights = jnp.exp(cols[:, head : head + 1] - less[head : head + 1] + bar) * scores
            acc = acc + dot(weights.astype(BF16), jnp.where(mask, part, zero))
        y_ref[0, :, span] = acc
    keep = enter_x[rows - 1 : rows]
    held[...] = state * keep + dot(
        b_rows.astype(F32).T.astype(BF16), (xc * tail_x).astype(BF16)
    )


def mix_backward(
    t_ref, x_ref, xp_ref, bc_ref, bp_ref, u_ref, sc_ref, sr_ref, y_ref, dy_ref, state_ref,
    cw_ref, cb_ref, bw_ref, bb_ref, db_ref, rate_ref, skip_ref, spread_ref, heads_ref,
    dx_ref, dbc_ref, du_ref, gx_ref, gbc_ref, gh_ref, held, x_next, bc_next,
):
    del t_ref
    rows = x_ref.shape[1]
    width = x_ref.shape[2]
    pairs = width // 128

    @pl.when(pl.program_id(0) == 0)
    def _():
        held[...] = jnp.zeros_like(held)
        x_next[...] = jnp.zeros_like(x_next)
        bc_next[...] = jnp.zeros_like(bc_next)
        gx_ref[...] = jnp.zeros_like(gx_ref)
        gbc_ref[...] = jnp.zeros_like(gbc_ref)
        gh_ref[...] = jnp.zeros_like(gh_ref)

    sc = sc_ref[0]
    sr = sr_ref[0]
    marks = [sc[:, at : at + 1] for at in range(3)]
    x = x_ref[0]
    pre, x_moved = conv_parts(x, xp_ref[0], cw_ref[...], cb_ref[...], marks)
    sig = jax.nn.sigmoid(pre)
    xc = pre * sig
    raw = bc_ref[0]
    pre_bc, bc_moved = conv_parts(raw, bp_ref[0], bw_ref[...], bb_ref[...], marks)
    sig_bc = jax.nn.sigmoid(pre_bc)
    bc = (pre_bc * sig_bc).astype(BF16)
    states = bc.shape[1] // 2
    b_rows, c_rows = bc[:, :states], bc[:, states:]

    u, dt, a, total, less, enter, tail = rates(u_ref[0], db_ref[...], rate_ref[...], sr)
    cols = as_columns(less, enter, tail)
    cols_low = cols.astype(BF16)
    enter_x = dot(cols_low, spread_ref[0])
    tail_x = dot(cols_low, spread_ref[1])
    keep = enter_x[rows - 1 : rows]

    at_s = lax.broadcasted_iota(jnp.int32, (rows, rows), 0)
    at_t = lax.broadcasted_iota(jnp.int32, (rows, rows), 1)
    bar = jnp.where((sc[:, 3:4] == sr[0:1]) & (at_t >= at_s), 0.0, NEG)
    scores = dot_t(b_rows, c_rows)

    dy = dy_ref[0]
    dyl = dy.astype(BF16)
    xl = xc.astype(BF16)
    state = state_ref[0]
    d_state = held[...]
    d_state_low = d_state.astype(BF16)
    entered = (dy * enter_x).astype(BF16)
    dc = dot_t(entered, state.astype(BF16))
    db = dot_t((xc * tail_x).astype(BF16), d_state_low)
    dx_tail = dot(b_rows, d_state_low) * tail_x
    x_round = xl.astype(F32)
    last_terms = jnp.sum(x_round * dx_tail, 0, keepdims=True) + keep * jnp.sum(
        state * d_state, 0, keepdims=True
    )
    held[...] = keep * d_state + dot(c_rows.astype(F32).T.astype(BF16), entered)

    low_mask, high_mask = pair_masks(rows)
    zero = jnp.zeros((rows, 128), BF16)
    d_scores = jnp.zeros((rows, rows), F32)
    d_scan = []
    for pair in range(pairs):
        span = slice(pair * 128, pair * 128 + 128)
        part, grad = xl[:, span], dyl[:, span]
        acc = dx_tail[:, span]
        for side, mask in ((0, low_mask), (1, high_mask)):
            head = 2 * pair + side
            decay = jnp.exp(total[head : head + 1] - cols[:, head : head + 1] + bar)
            weights = (decay * scores).astype(BF16)
            d_scores = d_scores + decay * dot_t(jnp.where(mask, part, zero), grad)
            acc = acc + dot(weights, jnp.where(mask, grad, zero))
        d_scan.append(acc)
    d_scan = jnp.concatenate(d_scan, 1)
    db = db + dot(d_scores.astype(BF16), c_rows)
    dc = dc + dot(d_scores.T.astype(BF16), b_rows)

    skip = skip_ref[...]
    from_x = x_round * d_scan
    from_t = dyl.astype(F32) * (y_ref[0] - skip * xc) - from_x
    row_at = lax.broadcasted_iota(jnp.int32, (rows, width), 0)
    from_t = from_t + jnp.where(row_at == rows - 1, last_terms, 0.0)

    def per_head(value):
        high = value.astype(BF16)
        return dot_t(heads_ref[...], high) + dot_t(
            heads_ref[...], (value - high.astype(F32)).astype(BF16)
        )

    q = per_head(from_x)
    da = shifted_sum(per_head(from_t), -1)
    slope = jax.nn.sigmoid(u)
    ratio = jnp.where(u < -15.0, 1.0, slope / dt)
    du = q * ratio - da * rate_ref[...] * slope
    du_ref[0] = du
    gh_ref[0] += jnp.sum(du, 1, keepdims=True)
    gh_ref[1] += jnp.sum(da * a, 1, keepdims=True)

    def conv_back(d_out, cur, moved, weight, carried, grads):
        grads[3:4] += jnp.sum(d_out * cur, 0, keepdims=True)
        grads[4:5] += jnp.sum(d_out, 0, keepdims=True)
        result = d_out * weight[3:4]
        for back in (1, 2, 3):
            kept = d_out * marks[back - 1]
            grads[3 - back : 4 - back] += jnp.sum(kept * moved[back - 1], 0, keepdims=True)
            ext = jnp.concatenate([kept, carried[back - 1]], 0)
            result = result + ext[back : back + rows] * weight[3 - back : 4 - back]
            carried[back - 1] = kept[:8]
        return result

    gx_ref[5:6] += jnp.sum(dy * xc, 0, keepdims=True)
    d_pre = (d_scan + skip * dy) * (sig * (1.0 + pre * (1.0 - sig)))
    dx_ref[0] = conv_back(d_pre, x, x_moved, cw_ref[...], x_next, gx_ref).astype(BF16)
    d_bc = jnp.concatenate([db, dc], 1) * (sig_bc * (1.0 + pre_bc * (1.0 - sig_bc)))
    dbc_ref[0] = conv_back(d_bc, raw, bc_moved, bw_ref[...], bc_next, gbc_ref).astype(BF16)


def whole_spec(shape):
    return pl.BlockSpec(shape, lambda at, t: (0,) * len(shape))


def run_forward(place, x, bc, u, seg_cols, seg_rows, small):
    blocks, rows, width = x.shape
    wide = bc.shape[2]
    states = wide // 2

    def slot(shape):
        return pl.BlockSpec((1,) + shape, lambda at, t: (at ^ t[0], 0, 0))

    def straight(shape):
        return pl.BlockSpec((1,) + shape, lambda at, t: (at, 0, 0))

    spec = pltpu.PrefetchScalarGridSpec(
        num_scalar_prefetch=1,
        grid=(blocks,),
        in_specs=[
            slot((rows, width)), slot((rows, wide)), slot((HEAD_ROWS, rows)),
            straight((rows, 8)), straight((8, rows)),
        ] + [whole_spec(item.shape) for item in small],
        out_specs=[slot((rows, width)), straight((states, width))],
        scratch_shapes=[
            pltpu.VMEM((states, width), F32),
            pltpu.VMEM((8, width), F32),
            pltpu.VMEM((8, wide), F32),
        ],
    )
    return pl.pallas_call(
        mix_forward,
        grid_spec=spec,
        out_shape=[
            jax.ShapeDtypeStruct((blocks, rows, width), F32),
            jax.ShapeDtypeStruct((blocks, states, width), F32),
        ],
        compiler_params=pltpu.CompilerParams(
            dimension_semantics=("arbitrary",), vmem_limit_bytes=VMEM
        ),
        cost_estimate=pl.CostEstimate(flops=3 * 10**9, bytes_accessed=10**7, transcendentals=4 * 10**6),
        name="mix_forward",
    )(place, x, bc, u, seg_cols, seg_rows, *small)


def run_backward(place, x, bc, u, seg_cols, seg_rows, y, dy, state, small, heads_of):
    blocks, rows, width = x.shape
    wide = bc.shape[2]
    states = wide // 2
    last = blocks - 1

    def slot(shape):
        return pl.BlockSpec((1,) + shape, lambda at, t: ((last - at) ^ t[0], 0, 0))

    def before(shape):
        return pl.BlockSpec(
            (1,) + shape,
            lambda at, t: (jnp.maximum(last - at - 1, 0) ^ t[0], rows // 8 - 1, 0),
        )

    def straight(shape):
        return pl.BlockSpec((1,) + shape, lambda at, t: (last - at, 0, 0))

    spec = pltpu.PrefetchScalarGridSpec(
        num_scalar_prefetch=1,
        grid=(blocks,),
        in_specs=[
            slot((rows, width)), before((8, width)), slot((rows, wide)), before((8, wide)),
            slot((HEAD_ROWS, rows)), straight((rows, 8)), straight((8, rows)),
            slot((rows, width)), slot((rows, width)), straight((states, width)),
        ] + [whole_spec(item.shape) for item in small] + [whole_spec(heads_of.shape)],
        out_specs=[
            slot((rows, width)), slot((rows, wide)), slot((HEAD_ROWS, rows)),
            whole_spec((8, width)), whole_spec((8, wide)), whole_spec((2, HEAD_ROWS, 128)),
        ],
        scratch_shapes=[
            pltpu.VMEM((states, width), F32),
            pltpu.VMEM((3, 8, width), F32),
            pltpu.VMEM((3, 8, wide), F32),
        ],
    )
    return pl.pallas_call(
        mix_backward,
        grid_spec=spec,
        out_shape=[
            jax.ShapeDtypeStruct((blocks, rows, width), BF16),
            jax.ShapeDtypeStruct((blocks, rows, wide), BF16),
            jax.ShapeDtypeStruct((blocks, HEAD_ROWS, rows), F32),
            jax.ShapeDtypeStruct((8, width), F32),
            jax.ShapeDtypeStruct((8, wide), F32),
            jax.ShapeDtypeStruct((2, HEAD_ROWS, 128), F32),
        ],
        compiler_params=pltpu.CompilerParams(
            dimension_semantics=("arbitrary",), vmem_limit_bytes=VMEM
        ),
        cost_estimate=pl.CostEstimate(flops=8 * 10**9, bytes_accessed=2 * 10**7, transcendentals=5 * 10**6),
        name="mix_backward",
    )(place, x, x, bc, bc, u, seg_cols, seg_rows, y, dy, state, *small, heads_of)


def segment_tables(segment, blocks):
    rows = segment.shape[0] // blocks
    marks = [
        jnp.concatenate([jnp.zeros((back,), F32), (segment[back:] == segment[:-back]).astype(F32)])
        for back in (1, 2, 3)
    ]
    cut = segment.reshape(blocks, rows)
    ends = cut[:, -1]
    before = jnp.concatenate([cut[:1, 0], ends[:-1]])
    carried = (cut == before[:, None]).astype(F32)
    is_last = (cut == ends[:, None]).astype(F32)
    ids = cut.astype(F32)
    nothing = jnp.zeros_like(ids)
    cols = jnp.stack(
        [item.reshape(blocks, rows) for item in marks] + [ids] + [nothing] * 4, 2
    )
    lines = jnp.stack([ids, carried, is_last] + [nothing] * 5, 1)
    return cols, lines


def head_tables(heads, width):
    owner = jnp.arange(width)[None, :] // (width // heads)
    at = jnp.arange(128)[:, None]
    spread_enter = (at == owner + HEAD_ROWS) | (at == owner + 3 * HEAD_ROWS)
    spread_tail = (at == owner + 2 * HEAD_ROWS) | (at == owner + 4 * HEAD_ROWS)
    spread = jnp.stack([spread_enter, spread_tail]).astype(BF16)
    return spread, (at[:HEAD_ROWS] == owner).astype(BF16)


def head_column(value):
    return jnp.pad(value.astype(F32), (0, HEAD_ROWS - value.shape[0]))[:, None]


def norm_scale_of(values):
    return lax.rsqrt(jnp.mean(values * values, -1, keepdims=True) + EPS)


def shards(
    hidden, segment_ids, cotangent, norm_gain, in_zx, in_dt, in_bc, conv_x, conv_x_bias,
    conv_bc, conv_bc_bias, dt_bias, a_log, skip_d, gated_gain, out_wt,
):
    layers = in_zx.shape[0]
    count = lax.axis_size("fsdp")
    tp_count = lax.axis_size("tp")
    tp_at = lax.axis_index("tp")
    place = walk_place()
    slot_at = tp_at.astype(jnp.int32)[None]
    own, features = hidden.shape
    deep = in_zx.shape[1]
    width = in_zx.shape[3]
    heads = in_dt.shape[2]
    wide = in_bc.shape[2]
    bc_deep = in_bc.shape[1]
    shared = conv_bc.shape[1]
    taps = conv_bc.shape[2]
    inner = width * tp_count

    start = columns_to_walk(hidden, place)
    all_start = jnp.stack(tp_gather(start))
    seg_cols, seg_rows = segment_tables(segment_ids[0], tp_count)
    spread, heads_of = head_tables(heads, width)

    w_x, w_z, w_o, w_dt, w_bc, gains, small = [], [], [], [], [], [], []
    for k in range(layers):
        tiny = jnp.concatenate(
            [norm_gain[k], conv_bc[k].reshape(-1), conv_bc_bias[k]], 0
        )
        tiny = jnp.pad(tiny, (0, wide - tiny.shape[0]))[None]
        pack = jnp.concatenate([in_bc[k], tiny], 0)
        x_all = fsdp_gather(in_zx[k, :, 1])
        pack_all = fsdp_gather(pack)
        dt_all = fsdp_gather(in_dt[k])
        z_all = fsdp_gather(in_zx[k, :, 0])
        o_all = fsdp_gather(out_wt[k])
        pack_all = jnp.stack(tp_natural(tp_gather(pack_all), tp_at), 1)
        w_x.append(x_all.reshape(features, width))
        w_z.append(z_all.reshape(features, width))
        w_o.append(o_all.reshape(features, width))
        w_dt.append(dt_all.reshape(features, heads))
        w_bc.append(pack_all[:, :, :bc_deep].reshape(features, wide))
        tiny = pack_all[:, :, bc_deep]
        gains.append(tiny[:, :, :bc_deep].reshape(1, features).astype(F32))
        rest = tiny[:, :, bc_deep:]
        rest = jnp.stack(from_walk([rest[at] for at in range(count)], place))
        taps_bc = rest[:, :, : shared * taps].reshape(wide, taps).astype(F32)
        bias_bc = rest[:, :, shared * taps : shared * (taps + 1)].reshape(1, wide).astype(F32)
        small.append(
            (
                conv_x[k].astype(F32).T,
                conv_x_bias[k].astype(F32)[None],
                taps_bc.T,
                bias_bc,
                head_column(dt_bias[k]),
                jnp.exp(head_column(a_log[k])),
                jnp.repeat(skip_d[k].astype(F32), width // heads)[None],
                spread,
            )
        )

    def project(rows, weight):
        return lax.dot_general(
            rows, weight, (((2,), (0,)), ((), ())), preferred_element_type=F32
        )

    def step_inputs(rows, weight):
        result = lax.dot_general(
            weight, rows, (((0,), (2,)), ((), ())), preferred_element_type=F32
        )
        result = jnp.swapaxes(result, 0, 1)
        return jnp.pad(result, ((0, 0), (0, HEAD_ROWS - heads), (0, 0)))

    running = start.astype(F32)
    saved = []
    for k in range(layers):
        if k == 0:
            wide_start = all_start.astype(F32)
            rows = (wide_start * norm_scale_of(wide_start) * gains[0]).astype(BF16)
        else:
            rows = (running * norm_scale_of(running) * gains[k]).astype(BF16)
            rows = jnp.stack(tp_gather(rows))
        raw_x = project(rows, w_x[k])
        raw_bc = project(rows, w_bc[k])
        raw_u = step_inputs(rows, w_dt[k])
        y, state = run_forward(slot_at, raw_x, raw_bc, raw_u, seg_cols, seg_rows, small[k])
        z = project(rows, w_z[k])
        v = y * jax.nn.silu(z)
        squares = jnp.sum(v * v, -1)
        gain = gated_gain[k].astype(F32)
        entry = dict(rows=rows, x=raw_x, bc=raw_bc, u=raw_u, y=y, z=z, v=v, state=state, h=running)
        partial = lax.dot_general(
            (v * gain).astype(BF16), w_o[k], (((2,), (1,)), ((), ())), preferred_element_type=F32
        ).astype(BF16)
        branch = tp_reduce_own([partial[at] for at in range(tp_count)])
        if k < layers - 1:
            scale = lax.rsqrt(tp_sum_slots(squares) / inner + EPS)
            entry["scale"] = scale
            entry["branch"] = branch
            running = running + branch * scale[0][:, None]
        else:
            entry["squares"] = squares
            entry["branch"] = branch
        saved.append(entry)

    grad_run = columns_to_walk(cotangent, place).astype(F32)
    collected = [[None] * layers for _ in range(13)]
    for k in reversed(range(layers)):
        item = saved[k]
        rows, v, z, y = item["rows"], item["v"], item["z"], item["y"]
        gain = gated_gain[k].astype(F32)
        grad_low = grad_run.astype(BF16)
        if k < layers - 1:
            cross_own = jnp.sum(grad_low.astype(F32) * item["branch"], -1)
            cross = jnp.stack(tp_gather(cross_own))
            scale = item["scale"]
        cot = jnp.stack(tp_gather(grad_low))
        d_gated = project(cot, w_o[k])
        d_unit = d_gated * gain
        if k == layers - 1:
            sums = jnp.stack([item["squares"], jnp.sum(d_unit * v, -1)], 1)
            sums = tp_sum_slots(sums)
            scale = lax.rsqrt(sums[:, 0] / inner + EPS)
            cross = sums[:, 1]
            running = running + item["branch"] * scale[0][:, None]
        gated = (v * scale[:, :, None] * gain).astype(BF16)
        d_w_o = lax.dot_general(
            cot, gated, (((0, 1), (0, 1)), ((), ())), preferred_element_type=F32
        ).astype(BF16)
        sum_o = fsdp_reduce(d_w_o.reshape(count, deep, width))
        d_gain = jnp.sum(d_gated * v * scale[:, :, None], (0, 1))
        dv = d_unit * scale[:, :, None] - v * (scale**3 * cross / inner)[:, :, None]
        sig_z = jax.nn.sigmoid(z)
        dy = dv * (z * sig_z)
        dz = (dv * y * (sig_z * (1.0 + z * (1.0 - sig_z)))).astype(BF16)

        def weight_grad(grad):
            return lax.dot_general(
                rows, grad, (((0, 1), (0, 1)), ((), ())), preferred_element_type=F32
            )

        sum_z = fsdp_reduce(weight_grad(dz).astype(BF16).reshape(count, deep, width))
        dx, dbc, du, gx, gbc, gh = run_backward(
            slot_at, item["x"], item["bc"], item["u"], seg_cols, seg_rows, y, dy,
            item["state"], small[k], heads_of,
        )
        du_low = du[:, :heads].astype(BF16)

        def back(grad, weight):
            return lax.dot_general(
                grad, weight, (((2,), (1,)), ((), ())), preferred_element_type=F32
            )

        total = back(dz, w_z[k]) + back(dx, w_x[k]) + back(dbc, w_bc[k])
        total = total + lax.dot_general(
            du_low, w_dt[k], (((1,), (1,)), ((), ())), preferred_element_type=F32
        )
        d_gain_pre = jnp.sum(total * rows.astype(F32), (0, 1)) / gains[k][0]
        total = total.astype(BF16)
        d_normed = tp_reduce_own([total[at] for at in range(tp_count)])
        sum_x = fsdp_reduce(weight_grad(dx).astype(BF16).reshape(count, deep, width))
        h = item["h"]
        inv = norm_scale_of(h)
        scaled = d_normed * gains[k]
        grad_run = (
            grad_run
            + inv * scaled
            - h * (inv**3 * (jnp.sum(scaled * h, -1, keepdims=True) / features))
        )

        d_w_bc = weight_grad(dbc).reshape(count, tp_count, bc_deep, wide)
        d_w_dt = lax.dot_general(
            rows, du_low, (((0, 1), (0, 2)), ((), ())), preferred_element_type=F32
        )
        d_tiny = jnp.concatenate(
            [
                d_gain_pre.reshape(count, tp_count, bc_deep),
                jnp.stack(
                    to_walk(
                        list(
                            jnp.concatenate(
                                [
                                    gbc[:4].T.reshape(count, tp_count, shared * taps),
                                    gbc[4].reshape(count, tp_count, shared),
                                ],
                                2,
                            )
                        ),
                        place,
                    )
                ),
            ],
            2,
        )
        d_tiny = jnp.pad(d_tiny, ((0, 0), (0, 0), (0, wide - d_tiny.shape[2])))
        d_pack = jnp.concatenate([d_w_bc, d_tiny[:, :, None]], 2)
        d_slots = tp_natural([d_pack[:, at] for at in range(tp_count)], tp_at)
        d_pack = tp_reduce_own(d_slots)
        d_pack = jnp.concatenate(
            [d_pack.reshape(count, -1), d_w_dt.reshape(count, -1)], 1
        )
        d_pack = fsdp_reduce(d_pack)
        cut = (bc_deep + 1) * wide
        sum_pack = d_pack[:cut].reshape(bc_deep + 1, wide)
        sum_dt = d_pack[cut:].reshape(deep, heads)
        tiny = sum_pack[bc_deep]
        sum_pre = tiny[:bc_deep]
        sum_bc_w = tiny[bc_deep : bc_deep + shared * taps].reshape(shared, taps)
        sum_bc_b = tiny[bc_deep + shared * taps : bc_deep + shared * (taps + 1)]

        flat = jnp.concatenate([gx[:6], d_gain[None]], 0).reshape(-1, 128)
        flat = jnp.concatenate([flat, gh[0, :, 0:1].T.repeat(8, 1), gh[1, :, 0:1].T.repeat(8, 1)], 0)
        flat = fsdp_sum(flat)
        lines = width // 128
        sums = flat[: 7 * lines].reshape(7, width)
        layer_grads = (
            sum_pre,
            jnp.stack([sum_z, sum_x], 1),
            sum_dt,
            sum_pack[:bc_deep],
            sums[:4].T,
            sums[4],
            sum_bc_w,
            sum_bc_b,
            flat[7 * lines].reshape(-1, 8)[:heads, 0],
            flat[7 * lines + 1].reshape(-1, 8)[:heads, 0],
            jnp.sum(sums[5].reshape(heads, -1), 1),
            sums[6],
            sum_o,
        )
        for at in range(13):
            collected[at][k] = layer_grads[at]
    stacked = [jnp.stack(entry, 0) for entry in collected]
    return (
        columns_from_walk(running, place),
        columns_from_walk(grad_run, place),
        *stacked,
    )


def solution(mesh):
    tokens = P(("fsdp", "tp"), None)
    split = P(None, ("fsdp", "tp"))
    rows = P(None, ("fsdp", "tp"), None)
    weights = (
        split,
        P(None, "fsdp", None, "tp"),
        P(None, "fsdp", "tp"),
        rows,
        P(None, "tp", None),
        P(None, "tp"),
        rows,
        split,
        P(None, "tp"),
        P(None, "tp"),
        P(None, "tp"),
        P(None, "tp"),
        P(None, "fsdp", "tp"),
    )
    return jax.shard_map(
        shards,
        mesh=mesh,
        in_specs=(tokens, P("fsdp", None), tokens) + weights,
        out_specs=(tokens, tokens) + weights,
        check_vma=False,
    )
```

time: 2140 us -> 899 us (0.42)
  local copies, waits for them, and re-layouts: 564 us -> 123 us
  blocking collectives: 386 us -> 0 us
  waiting for transfers between devices: 634 us -> 282 us
  matrix products: 315 us -> 125 us
  starting transfers between devices: 1.29 us -> 185 us
  other arithmetic: 183 us -> 88.3 us
  Pallas kernels: 0 us -> 82.1 us
  loops' own time: 25.9 us -> 0 us
    reduce_scatter x10 -> x0, waiting for transfers between devices: 607 us -> none  [the longest x2 193 us: shards(): lax.psum_scatter(d_w_zx.astype(jnp.bfloat16), 'fsdp', scatter_dimension=0...]
    dynamic_update_slice x56 -> x0, local copies, waits for them, and re-layouts: 317 us -> none  [block_scan(): finished, outputs = lax.scan(jax.checkpoint(scan_step), initial, pieces)]
    ppermute x0 -> x189, waiting for transfers between devices: none -> 282 us  [the longest x144 176 us: step_ring(): lax.ppermute(value, 'fsdp', [(WALK[at], WALK[(at + by) % size]) for at in...]
    all_gather x6 -> x0, blocking collectives: 239 us -> none  [the longest x2 97.3 us: shards(): lax.all_gather(in_bc[depth_at], ('fsdp', 'tp'), axis=0, tiled=True)]
    dot_general x136 -> x30, matrix products: 315 us -> 125 us  [the longest x8 35.4 us: project(): lax.dot_general(rows, weight, (((2,), (0,)), ((), ())), preferred_element...]
    ppermute x0 -> x189, starting transfers between devices: none -> 185 us  [the longest x144 152 us: step_ring(): lax.ppermute(value, 'fsdp', [(WALK[at], WALK[(at + by) % size]) for at in...]
    unnamed x2 -> x0, blocking collectives: 82.1 us -> none
    pallas_call x0 -> x4, Pallas kernels: none -> 82.1 us  [the longest x2 56.9 us: run_backward(): pl.pallas_call(mix_backward, grid_spec=spec, out_shape=[jax.ShapeDtypeStr...]
  transfers between devices with their start and end apart: 20 -> 189, of which waited for: 11 -> 78; matrix products, arithmetic and copies ran while one was open for 35% -> 27% of each run, Pallas kernels for 0% -> 3%
where the time goes in v1:
time: 899 us; the launch traced here: 889 us
  waiting for transfers between devices  282 us (31%)
  starting transfers between devices  185 us (21%)
  matrix products  125 us (14%)
  local copies, waits for them, and re-layouts  123 us (14%)
  other arithmetic  88.3 us (10%)
  Pallas kernels  82.1 us (9%)
    ppermute x144, waiting for transfers between devices, step_ring(): lax.ppermute(value, 'fsdp', [(WALK[at], WALK[(at + by) % size]) for at in...  176 us
    ppermute x144, starting transfers between devices, step_ring(): lax.ppermute(value, 'fsdp', [(WALK[at], WALK[(at + by) % size]) for at in...  152 us
    ppermute x37, waiting for transfers between devices, tp_swap(): return lax.ppermute(value, 'tp', [(at, at ^ mask) for at in range(size)])  104 us
    pallas_call x2, Pallas kernels, run_backward(): pl.pallas_call(mix_backward, grid_spec=spec, out_shape=[jax.ShapeDtypeStr...  56.9 us
    unnamed x353, local copies, waits for them, and re-layouts  41.1 us
    dot_general x8, matrix products, project(): lax.dot_general(rows, weight, (((2,), (0,)), ((), ())), preferred_element...  35.4 us
    dot_general x6, matrix products, back(): lax.dot_general(grad, weight, (((2,), (1,)), ((), ())), preferred_element...  26.4 us
    pallas_call x2, Pallas kernels, run_forward(): pl.pallas_call(mix_forward, grid_spec=spec, out_shape=[jax.ShapeDtypeStru...  25.2 us
  transfers between devices with their start and end apart: 189, of which 78 were waited for; matrix products, arithmetic and copies ran while one was open for 27% of the time, Pallas kernels for 3%

profile of v1, /device:TPU:0, one launch (start us, length us, event | category | flops | bytes accessed | tf_op | source)
XLA Modules:
  0.0 888.8 jit_solution(16707889131899772216)
XLA Ops:
  160.0 5.2 collective-permute-done.91
  263.3 9.6 %collective-permute-done.99 = bf16[256,1536]{1,0:T(8,128)(2,1)} collective-permute-done((bf16[256,1536]{1,0:T(8,128)(2,1)}, bf16[256,1536]{1,0:T(8,128)(2,1)}, u32[]{:S(2)}, u32[]{:S(2)}) %collective-permute-start.99) | collective-permute-done | bytes 786464 | tf_op jit(solution)/shard_map/ppermute | solution.py:19
  288.9 12.6 %mix_forward.2 = (f32[4,256,768]{2,1,0:T(8,128)}, f32[4,128,768]{2,1,0:T(8,128)}) custom-call(s32[1]{0:T(128)} %bitcast.t_ref, f32[4,256,768]{2,1,0:T(8,128)} %fusion.154.x_ref.xp_ref, f32[4,256,256]{2,1,0:T(8,128)} %fusion.155.bc_ref.bp_ref, f32[4,16,256]{2,1,0:T(8,128)} %pad.47.u_ref, f32[4,256,8]{2,1,0:T(8,128)} %stack.596.sc_ref, ...), custom_call_target="tpu_custom_call" | custom-call | flops 3000000000 | bytes 10000000 | tf_op jit(solution)/shard_map/mix_forward/pallas_call | solution.py:430
  301.6 6.8 multiply_reduce_fusion.6
  325.7 17.6 %collective-permute-done.49 = f32[4,256]{1,0:T(4,128)S(1)} collective-permute-done((f32[4,256]{1,0:T(4,128)S(1)}, f32[4,256]{1,0:T(4,128)S(1)}, u32[]{:S(2)}, u32[]{:S(2)}) %collective-permute-start.49) | collective-permute-done | bytes 4128 | tf_op jit(solution)/shard_map/ppermute | solution.py:19
  351.2 13.7 %collective-permute-done.62 = bf16[256,1536]{1,0:T(8,128)(2,1)S(1)} collective-permute-done((bf16[256,1536]{1,0:T(8,128)(2,1)S(1)}, bf16[256,1536]{1,0:T(8,128)(2,1)S(1)}, u32[]{:S(2)}, u32[]{:S(2)}) %collective-permute-start.62) | collective-permute-done | bytes 786464 | tf_op jit(solution)/shard_map/ppermute | solution.py:19
  375.9 12.6 %mix_forward.3 = (f32[4,256,768]{2,1,0:T(8,128)}, f32[4,128,768]{2,1,0:T(8,128)}) custom-call(s32[1]{0:T(128)} %bitcast.t_ref, f32[4,256,768]{2,1,0:T(8,128)} %fusion.156.x_ref.xp_ref, f32[4,256,256]{2,1,0:T(8,128)} %fusion.157.bc_ref.bp_ref, f32[4,16,256]{2,1,0:T(8,128)} %pad.52.u_ref, f32[4,256,8]{2,1,0:T(8,128)} %stack.596.sc_ref, ...), custom_call_target="tpu_custom_call" | custom-call | flops 3000000000 | bytes 10000000 | tf_op jit(solution)/shard_map/mix_forward/pallas_call | solution.py:430
  406.2 6.2 bitcast_convert_fusion
  415.9 28.2 %mix_backward.2 = (bf16[4,256,768]{2,1,0:T(8,128)(2,1)}, bf16[4,256,256]{2,1,0:T(8,128)(2,1)}, f32[4,16,256]{2,1,0:T(8,128)}, f32[8,768]{1,0:T(8,128)}, f32[8,256]{1,0:T(8,128)}, /*index=5*/f32[2,16,128]{2,1,0:T(8,128)}) custom-call(s32[1]{0:T(128)} %bitcast.t_ref, f32[4,256,768]{2,1,0:T(8,128)} %fusion.156.x_ref.xp_ref, ...), custom_call_target="tpu_custom_call" | custom-call | flops 8000000000 | bytes 20000000 | tf_op jit(solution)/shard_map/mix_backward/pallas_call | solution.py:481
  481.9 9.1 %multiply_reduce_fusion = (f32[1536]{0:T(1024)S(1)}, bf16[4,256,1536]{2,1,0:T(8,128)(2,1)}) fusion(bf16[4,256,1536]{2,1,0:T(8,128)(2,1)S(1)} %pad_maximum_fusion.1, bf16[1536,12,1]{0,1,2:T(8,128)(2,1)S(1)} %reshape.1041, f32[4,16,256]{2,1,0:T(8,128)S(1)} %copy-done.74, f32[4,256,1536]{2,1,0:T(8,128)} %fusion.161, f32[4,256,1536]{2,1,0:T(8,128)} %fusion.159, ...), kind=kOutput, calls=%fused_computation.5 | convolution fusion | flops 48757248 | bytes 25253888 | tf_op jit(solution)/shard_map/dot_general | solution.py:692
  528.5 5.2 collective-permute-done.158
  534.9 5.2 collective-permute-done.150
  564.1 5.9 collective-permute-done.124
  607.7 14.5 %collective-permute-done.104 = bf16[256,1536]{1,0:T(8,128)(2,1)S(1)} collective-permute-done((bf16[256,1536]{1,0:T(8,128)(2,1)S(1)}, bf16[256,1536]{1,0:T(8,128)(2,1)S(1)}, u32[]{:S(2)}, u32[]{:S(2)}) %collective-permute-start.104) | collective-permute-done | bytes 786464 | tf_op jit(solution)/shard_map/ppermute | solution.py:19
  622.7 9.9 %collective-permute-done.97 = bf16[256,1536]{1,0:T(8,128)(2,1)S(1)} collective-permute-done((bf16[256,1536]{1,0:T(8,128)(2,1)S(1)}, bf16[256,1536]{1,0:T(8,128)(2,1)S(1)}, u32[]{:S(2)}, u32[]{:S(2)}) %collective-permute-start.97) | collective-permute-done | bytes 786464 | tf_op jit(solution)/shard_map/ppermute | solution.py:19
  641.7 6.8 collective-permute-done.106
  651.2 7.0 bitcast_convert_fusion.1
  658.3 7.0 multiply_convert_fusion.2
  665.3 28.7 %mix_backward.3 = (bf16[4,256,768]{2,1,0:T(8,128)(2,1)}, bf16[4,256,256]{2,1,0:T(8,128)(2,1)}, f32[4,16,256]{2,1,0:T(8,128)}, f32[8,768]{1,0:T(8,128)}, f32[8,256]{1,0:T(8,128)}, /*index=5*/f32[2,16,128]{2,1,0:T(8,128)}) custom-call(s32[1]{0:T(128)} %bitcast.t_ref, f32[4,256,768]{2,1,0:T(8,128)} %fusion.154.x_ref.xp_ref, ...), custom_call_target="tpu_custom_call" | custom-call | flops 8000000000 | bytes 20000000 | tf_op jit(solution)/shard_map/mix_backward/pallas_call | solution.py:481
  730.4 9.1 %multiply_reduce_fusion.1 = (f32[1536]{0:T(1024)S(1)}, bf16[4,256,1536]{2,1,0:T(8,128)(2,1)}) fusion(bf16[4,256,1536]{2,1,0:T(8,128)(2,1)S(1)} %copy-done.1, bf16[1536,12,1]{0,1,2:T(8,128)(2,1)S(1)} %copy-done.51, f32[4,16,256]{2,1,0:T(8,128)S(1)} %copy-done.73, f32[4,256,1536]{2,1,0:T(8,128)} %fusion.164, f32[4,256,1536]{2,1,0:T(8,128)} %fusion.162, ...), kind=kOutput, calls=%fused_computation.6 | convolution fusion | flops 48757248 | bytes 25253888 | tf_op jit(solution)/shard_map/dot_general | solution.py:692
  781.4 5.9 collective-permute-done.142
  787.7 5.9 collective-permute-done.134
  847.4 5.4 collective-permute-done.176
  869.3 13.4 %collective-permute-done.112 = bf16[256,1536]{1,0:T(8,128)(2,1)S(1)} collective-permute-done((bf16[256,1536]{1,0:T(8,128)(2,1)}, bf16[256,1536]{1,0:T(8,128)(2,1)S(1)}, u32[]{:S(2)}, u32[]{:S(2)}) %collective-permute-start.112) | collective-permute-done | bytes 786464 | tf_op jit(solution)/shard_map/ppermute | solution.py:19
  (1136 shorter events, 633.6 us)
Async XLA Ops:
  4.5 79.8 %collective-permute-start.3 = (bf16[49,256]{1,0:T(8,128)(2,1)}, bf16[49,256]{1,0:T(8,128)(2,1)}, u32[]{:S(2)}, u32[]{:S(2)}) collective-permute-start(bf16[49,256]{1,0:T(8,128)(2,1)} %pad_maximum_fusion.45), channel_id=1, source_target_pairs={{0,4},{8,0},{16,8},{24,16},{28,24},{20,28},{12,20},{4,12},{1,5},{9... | collective-permute-start | bytes 75272 | tf_op jit(solution)/shard_map/ppermute | solution.py:65
  7.4 80.2 %collective-permute-start.6 = (bf16[49,256]{1,0:T(8,128)(2,1)}, bf16[49,256]{1,0:T(8,128)(2,1)}, u32[]{:S(2)}, u32[]{:S(2)}) collective-permute-start(bf16[49,256]{1,0:T(8,128)(2,1)} %pad_maximum_fusion.45), channel_id=1, source_target_pairs={{0,8},{8,16},{16,24},{24,28},{28,20},{20,12},{12,4},{4,0},{1,9},{9... | collective-permute-start | bytes 75272 | tf_op jit(solution)/shard_map/ppermute | solution.py:65
  8.9 52.7 %collective-permute-start.75 = (bf16[192,12]{0,1:T(8,128)(2,1)}, bf16[192,12]{0,1:T(8,128)(2,1)}, u32[]{:S(2)}, u32[]{:S(2)}) collective-permute-start(bf16[192,12]{0,1:T(8,128)(2,1)} %get-tuple-element.417), channel_id=1, source_target_pairs={{0,8},{8,16},{16,24},{24,28},{28,20},{20,12},{12,4},{4,0},{1,9},{9... | collective-permute-start | bytes 13832 | tf_op jit(solution)/shard_map/ppermute | solution.py:65
  11.0 46.8 %collective-permute-start.72 = (bf16[192,12]{0,1:T(8,128)(2,1)}, bf16[192,12]{0,1:T(8,128)(2,1)}, u32[]{:S(2)}, u32[]{:S(2)}) collective-permute-start(bf16[192,12]{0,1:T(8,128)(2,1)} %get-tuple-element.417), channel_id=1, source_target_pairs={{0,4},{8,0},{16,8},{24,16},{28,24},{20,28},{12,20},{4,12},{1,5},{9... | collective-permute-start | bytes 13832 | tf_op jit(solution)/shard_map/ppermute | solution.py:65
  11.6 52.1 %collective-permute-start.25 = (bf16[192,12]{0,1:T(8,128)(2,1)}, bf16[192,12]{0,1:T(8,128)(2,1)}, u32[]{:S(2)}, u32[]{:S(2)}) collective-permute-start(bf16[192,12]{0,1:T(8,128)(2,1)} %get-tuple-element.421), channel_id=1, source_target_pairs={{0,8},{8,16},{16,24},{24,28},{28,20},{20,12},{12,4},{4,0},{1,9},{9... | collective-permute-start | bytes 13832 | tf_op jit(solution)/shard_map/ppermute | solution.py:65
  82.1 61.3 %collective-permute-start.17 = (bf16[192,768]{1,0:T(8,128)(2,1)}, bf16[192,768]{1,0:T(8,128)(2,1)}, u32[]{:S(2)}, u32[]{:S(2)}) collective-permute-start(bf16[192,768]{1,0:T(8,128)(2,1)} %bitcast.658), channel_id=1, source_target_pairs={{0,8},{8,16},{16,24},{24,28},{28,20},{20,12},{12,4},{4,0},{1,9},{9... | collective-permute-start | bytes 884744 | tf_op jit(solution)/shard_map/ppermute | solution.py:65
  84.3 31.7 %collective-permute-start.14 = (bf16[192,768]{1,0:T(8,128)(2,1)}, bf16[192,768]{1,0:T(8,128)(2,1)S(1)}, u32[]{:S(2)}, u32[]{:S(2)}) collective-permute-start(bf16[192,768]{1,0:T(8,128)(2,1)} %bitcast.658), channel_id=1, source_target_pairs={{0,4},{8,0},{16,8},{24,16},{28,24},{20,28},{12,20},{4,12},{1,5},{9... | collective-permute-start | bytes 884744 | tf_op jit(solution)/shard_map/ppermute | solution.py:65
  146.3 33.4 %collective-permute-start.15 = (bf16[192,768]{1,0:T(8,128)(2,1)}, bf16[192,768]{1,0:T(8,128)(2,1)}, u32[]{:S(2)}, u32[]{:S(2)}) collective-permute-start(bf16[192,768]{1,0:T(8,128)(2,1)} %copy-done.57), channel_id=1, source_target_pairs={{0,4},{8,0},{16,8},{24,16},{28,24},{20,28},{12,20},{4,12},{1,5},{9... | collective-permute-start | bytes 884744 | tf_op jit(solution)/shard_map/ppermute | solution.py:65
  241.0 36.7 %collective-permute-start = (bf16[256,1536]{1,0:T(8,128)(2,1)S(1)}, bf16[256,1536]{1,0:T(8,128)(2,1)S(1)}, u32[]{:S(2)}, u32[]{:S(2)}) collective-permute-start(bf16[256,1536]{1,0:T(8,128)(2,1)S(1)} %concatenate.169), channel_id=1, source_target_pairs={{0,1},{1,0},{2,3},{3,2},{4,5},{5,4},{6,7},{7,6},{8,9},{9,8},{10,11... | collective-permute-start | bytes 2359304 | tf_op jit(solution)/shard_map/ppermute | solution.py:19
  263.2 129.7 %collective-permute-start.98 = (bf16[256,1536]{1,0:T(8,128)(2,1)}, bf16[256,1536]{1,0:T(8,128)(2,1)}, u32[]{:S(2)}, u32[]{:S(2)}) collective-permute-start(bf16[256,1536]{1,0:T(8,128)(2,1)} %concatenate.188), channel_id=1, source_target_pairs={{0,1},{1,0},{2,3},{3,2},{4,5},{5,4},{6,7},{7,6},{8,9},{9,8},{10,11... | collective-permute-start | bytes 2359304 | tf_op jit(solution)/shard_map/ppermute | solution.py:19
  272.9 120.0 %collective-permute-start.100 = (bf16[256,1536]{1,0:T(8,128)(2,1)}, bf16[256,1536]{1,0:T(8,128)(2,1)}, u32[]{:S(2)}, u32[]{:S(2)}) collective-permute-start(bf16[256,1536]{1,0:T(8,128)(2,1)} %collective-permute-done.99), channel_id=1, source_target_pairs={{0,1},{1,0},{2,3},{3,2},{4,5},{5,4},{6,7},{7,6},{8,9},{9,8},{10,11... | collective-permute-start | bytes 2359304 | tf_op jit(solution)/shard_map/ppermute | solution.py:19
  273.4 41.4 %collective-permute-start.86 = (bf16[96,768]{1,0:T(8,128)(2,1)}, bf16[96,768]{1,0:T(8,128)(2,1)}, u32[]{:S(2)}, u32[]{:S(2)}) collective-permute-start(bf16[96,768]{1,0:T(8,128)(2,1)} %slice.1235), channel_id=1, source_target_pairs={{0,8},{8,16},{16,24},{24,28},{28,20},{20,12},{12,4},{4,0},{1,9},{9... | collective-permute-start | bytes 442376 | tf_op jit(solution)/shard_map/ppermute | solution.py:65
  277.7 37.5 %collective-permute-start.87 = (bf16[96,768]{1,0:T(8,128)(2,1)}, bf16[96,768]{1,0:T(8,128)(2,1)}, u32[]{:S(2)}, u32[]{:S(2)}) collective-permute-start(bf16[96,768]{1,0:T(8,128)(2,1)} %slice.1236), channel_id=1, source_target_pairs={{0,4},{8,0},{16,8},{24,16},{28,24},{20,28},{12,20},{4,12},{1,5},{9... | collective-permute-start | bytes 442376 | tf_op jit(solution)/shard_map/ppermute | solution.py:65
  474.0 38.1 %collective-permute-start.181 = (bf16[96,768]{1,0:T(8,128)(2,1)}, bf16[96,768]{1,0:T(8,128)(2,1)}, u32[]{:S(2)}, u32[]{:S(2)}) collective-permute-start(bf16[96,768]{1,0:T(8,128)(2,1)} %get-tuple-element.288), channel_id=1, source_target_pairs={{0,8},{8,16},{16,24},{24,28},{28,20},{20,12},{12,4},{4,0},{1,9},{9... | collective-permute-start | bytes 442376 | tf_op jit(solution)/shard_map/ppermute | solution.py:65
  474.3 39.0 %collective-permute-start.185 = (bf16[96,768]{1,0:T(8,128)(2,1)}, bf16[96,768]{1,0:T(8,128)(2,1)}, u32[]{:S(2)}, u32[]{:S(2)}) collective-permute-start(bf16[96,768]{1,0:T(8,128)(2,1)} %get-tuple-element.289), channel_id=1, source_target_pairs={{0,4},{8,0},{16,8},{24,16},{28,24},{20,28},{12,20},{4,12},{1,5},{9... | collective-permute-start | bytes 442376 | tf_op jit(solution)/shard_map/ppermute | solution.py:65
  513.3 39.9 %collective-permute-start.123 = (f32[2,8,49,256]{3,1,2,0:T(8,128)S(1)}, f32[2,8,49,256]{3,1,2,0:T(8,128)S(1)}, u32[]{:S(2)}, u32[]{:S(2)}) collective-permute-start(f32[2,8,49,256]{3,1,2,0:T(8,128)S(1)} %pad_maximum_fusion.11), channel_id=1, source_target_pairs={{0,1},{1,0},{2,3},{3,2},{4,5},{5,4},{6,7},{7,6},{8,9},{9,8},{10,11... | collective-permute-start | bytes 2408456 | tf_op jit(solution)/shard_map/ppermute | solution.py:19
  541.2 60.5 %collective-permute-start.96 = (bf16[2,256,1536]{2,1,0:T(8,128)(2,1)S(1)}, bf16[2,256,1536]{2,1,0:T(8,128)(2,1)S(1)}, u32[]{:S(2)}, u32[]{:S(2)}) collective-permute-start(bf16[2,256,1536]{2,1,0:T(8,128)(2,1)S(1)} %copy-done.39), channel_id=1, source_target_pairs={{0,1},{1,0},{2,3},{3,2},{4,5},{5,4},{6,7},{7,6},{8,9},{9,8},{10,11... | collective-permute-start | bytes 4718600 | tf_op jit(solution)/shard_map/ppermute | solution.py:19
  546.4 54.2 %collective-permute-start.103 = (bf16[2,256,1536]{2,1,0:T(8,128)(2,1)}, bf16[2,256,1536]{2,1,0:T(8,128)(2,1)S(1)}, u32[]{:S(2)}, u32[]{:S(2)}) collective-permute-start(bf16[2,256,1536]{2,1,0:T(8,128)(2,1)} %pad_maximum_fusion.7), channel_id=1, source_target_pairs={{0,1},{1,0},{2,3},{3,2},{4,5},{5,4},{6,7},{7,6},{8,9},{9,8},{10,11... | collective-permute-start | bytes 4718600 | tf_op jit(solution)/shard_map/ppermute | solution.py:19
  605.4 32.4 %collective-permute-start.128 = (f32[14848]{0:T(1024)S(1)}, f32[14848]{0:T(1024)S(1)}, u32[]{:S(2)}, u32[]{:S(2)}) collective-permute-start(f32[14848]{0:T(1024)S(1)} %add.558), channel_id=1, source_target_pairs={{0,8},{8,16},{16,24},{24,28},{28,20},{20,12},{12,4},{4,0},{1,9},{9... | collective-permute-start | bytes 178184 | tf_op jit(solution)/shard_map/ppermute | solution.py:65
  722.5 43.4 %collective-permute-start.173 = (bf16[96,768]{1,0:T(8,128)(2,1)}, bf16[96,768]{1,0:T(8,128)(2,1)}, u32[]{:S(2)}, u32[]{:S(2)}) collective-permute-start(bf16[96,768]{1,0:T(8,128)(2,1)} %get-tuple-element.280), channel_id=1, source_target_pairs={{0,8},{8,16},{16,24},{24,28},{28,20},{20,12},{12,4},{4,0},{1,9},{9... | collective-permute-start | bytes 442376 | tf_op jit(solution)/shard_map/ppermute | solution.py:65
  724.5 41.6 %collective-permute-start.177 = (bf16[96,768]{1,0:T(8,128)(2,1)}, bf16[96,768]{1,0:T(8,128)(2,1)}, u32[]{:S(2)}, u32[]{:S(2)}) collective-permute-start(bf16[96,768]{1,0:T(8,128)(2,1)} %get-tuple-element.281), channel_id=1, source_target_pairs={{0,4},{8,0},{16,8},{24,16},{28,24},{20,28},{12,20},{4,12},{1,5},{9... | collective-permute-start | bytes 442376 | tf_op jit(solution)/shard_map/ppermute | solution.py:65
  766.2 47.0 %collective-permute-start.113 = (f32[2,8,49,256]{3,1,2,0:T(8,128)S(1)}, f32[2,8,49,256]{3,1,2,0:T(8,128)S(1)}, u32[]{:S(2)}, u32[]{:S(2)}) collective-permute-start(f32[2,8,49,256]{3,1,2,0:T(8,128)S(1)} %pad_maximum_fusion.10), channel_id=1, source_target_pairs={{0,1},{1,0},{2,3},{3,2},{4,5},{5,4},{6,7},{7,6},{8,9},{9,8},{10,11... | collective-permute-start | bytes 2408456 | tf_op jit(solution)/shard_map/ppermute | solution.py:19
  806.4 36.5 %collective-permute-start.144 = (bf16[192,768]{1,0:T(8,128)(2,1)S(1)}, bf16[192,768]{1,0:T(8,128)(2,1)S(1)}, u32[]{:S(2)}, u32[]{:S(2)}) collective-permute-start(bf16[192,768]{1,0:T(8,128)(2,1)S(1)} %get-tuple-element.300), channel_id=1, source_target_pairs={{0,8},{8,16},{16,24},{24,28},{28,20},{20,12},{12,4},{4,0},{1,9},{9... | collective-permute-start | bytes 884744 | tf_op jit(solution)/shard_map/ppermute | solution.py:65
  812.8 32.3 %collective-permute-start.136 = (bf16[192,768]{1,0:T(8,128)(2,1)S(1)}, bf16[192,768]{1,0:T(8,128)(2,1)S(1)}, u32[]{:S(2)}, u32[]{:S(2)}) collective-permute-start(bf16[192,768]{1,0:T(8,128)(2,1)S(1)} %get-tuple-element.292), channel_id=1, source_target_pairs={{0,8},{8,16},{16,24},{24,28},{28,20},{20,12},{12,4},{4,0},{1,9},{9... | collective-permute-start | bytes 884744 | tf_op jit(solution)/shard_map/ppermute | solution.py:65
  (307 other events, 4215.3 us)

commit v2 on v1

v2 whole, which is shorter than its diff:
```python
from functools import partial

import jax
import jax.numpy as jnp
import numpy as np
from jax import lax
from jax.experimental import pallas as pl
from jax.experimental.pallas import tpu as pltpu
from jax.sharding import PartitionSpec as P

EPS = 1e-05
NEG = -1e30
F32 = jnp.float32
BF16 = jnp.bfloat16
WALK = (0, 2, 4, 6, 7, 5, 3, 1)
HEAD_ROWS = 16
VMEM = 56 * 1024 * 1024


def permute(value, axis, mask):
    size = lax.axis_size(axis)
    return lax.ppermute(value, axis, [(at, at ^ mask) for at in range(size)])


def tp_gather(value):
    across = permute(value, "tp", 2)
    core = permute(value, "tp", 1)
    return [value, core, across, permute(across, "tp", 1)]


def tp_reduce(send, keep):
    near = permute(send, "tp", 1)
    far = (keep[1].astype(F32) + near[1].astype(F32)).astype(keep.dtype)
    far = permute(far, "tp", 2)
    return keep[0].astype(F32) + near[0].astype(F32) + far.astype(F32)


def tp_sum_slots(value):
    near = permute(value, "tp", 1)
    value = value + jnp.stack([near[1], near[0], near[3], near[2]])
    far = permute(value, "tp", 2)
    return value + jnp.stack([far[2], far[3], far[0], far[1]])


def is_walk():
    return lax.axis_size("fsdp") == len(WALK)


def placement(tp_at):
    size = lax.axis_size("fsdp")
    if not is_walk():
        owners = jnp.arange(size, dtype=jnp.int32)
    else:
        all_owners = [[WALK[(WALK.index(f) + k) % size] for k in range(size)] for f in range(size)]
        owners = pick(jnp.array(all_owners, jnp.int32), lax.axis_index("fsdp"), 0)
    return jnp.concatenate([tp_at[None], owners])


def step_ring(value, by):
    size = len(WALK)
    return lax.ppermute(
        value, "fsdp", [(WALK[at], WALK[(at + by) % size]) for at in range(size)]
    )


def ring_pair(behind, ahead):
    return step_ring(behind, 1), step_ring(ahead, -1)


def ring_last(behind, ahead):
    half = behind.shape[0] // 2
    return step_ring(behind[:half], 1), step_ring(ahead[half:], -1)


def walk_weight(own, steps):
    arrays = [own]
    rows = own.shape[0]
    meta = [(0, 0, rows, 0, 0, True)]
    for at, (behind, ahead) in enumerate(steps):
        arrays += [behind, ahead]
        if at < 3:
            meta.append((len(arrays) - 2, 0, rows, 7 - at, 0, True))
            meta.append((len(arrays) - 1, 0, rows, 1 + at, 0, True))
        else:
            meta.append((len(arrays) - 2, 0, rows // 2, 4, 0, True))
            meta.append((len(arrays) - 1, 0, rows // 2, 4, rows // 2, True))
    return arrays, tuple(meta)


def natural_weight(array, count, deep, stride):
    return [array], tuple((0, at * stride, deep, at, 0, False) for at in range(count))


def after(value, *earlier):
    return lax.optimization_barrier((value,) + earlier)[0]


class RingGather:
    def __init__(self, own):
        self.own = own
        self.steps = []

    def step(self, *earlier):
        if not is_walk():
            return
        behind, ahead = self.steps[-1] if self.steps else (self.own, self.own)
        if earlier:
            behind, ahead, *_ = lax.optimization_barrier((behind, ahead) + earlier)
        go = ring_last if len(self.steps) == 3 else ring_pair
        self.steps.append(go(behind, ahead))

    def last(self):
        return self.steps[-1] if self.steps else ()

    def weight(self):
        if is_walk():
            return walk_weight(self.own, self.steps)
        whole = lax.all_gather(self.own, "fsdp", axis=0, tiled=True)
        deep = self.own.shape[0]
        return natural_weight(whole, lax.axis_size("fsdp"), deep, deep)


def double(value, axis, mask, dim):
    other = permute(value, axis, mask)
    second = (lax.axis_index(axis) & mask) != 0
    low = jnp.where(second, other, value)
    high = jnp.where(second, value, other)
    return jnp.concatenate([low, high], dim)


def plus(left, right):
    return (left.astype(F32) + right.astype(F32)).astype(left.dtype)


def pick(value, at, axis):
    return lax.dynamic_index_in_dim(value, at, axis, keepdims=False, allow_negative_indices=False)


def two_parts(value):
    high = value.astype(BF16)
    return jnp.concatenate([high, (value - high.astype(F32)).astype(BF16)], 0)


def joined(parts):
    half = parts.shape[0] // 2
    return parts[:half].astype(F32) + parts[half:].astype(F32)


class SmallSum:
    def __init__(self, terms, own, vector):
        index = lax.axis_index("tp")
        self.core, self.y = index & 1, index >> 1
        self.terms = terms.reshape((terms.shape[0], 2, 2) + terms.shape[2:])
        self.own, self.vector = own, vector
        self.wide = vector.shape[1]

    def over_core(self):
        return permute(pick(self.terms, 1 - self.core, 2), "tp", 1)

    def over_y(self, got):
        self.terms = plus(pick(self.terms, self.core, 2), got)
        return permute(pick(self.terms, 1 - self.y, 1), "tp", 2)

    def over_x(self, got):
        terms = plus(pick(self.terms, self.y, 1), got)
        self.terms = terms = jnp.concatenate([terms, self.own], 1)
        self.rows = rows = terms.shape[1]
        if not is_walk():
            return ()
        index = lax.axis_index("fsdp")
        self.x, self.z = index & 1, index >> 1
        self.terms = terms = terms.reshape((4, 2) + terms.shape[1:])
        got = pick(terms, 1 - self.x, 1).reshape(4 * rows, self.wide)
        return permute(jnp.concatenate([got, two_parts(self.vector)], 0), "fsdp", 1)

    def over_z(self, got):
        if not is_walk():
            return ()
        rows, terms = self.rows, self.terms
        self.vector = self.vector + joined(got[4 * rows :])
        got = got[: 4 * rows].reshape(4, rows, self.wide)
        mine = pick(terms, self.x, 1)
        self.total = pick(mine, self.z, 0).astype(F32) + pick(got, self.z, 0).astype(F32)
        sent = two_parts(self.vector)
        parts = []
        for mask in (3, 2, 1):
            part = plus(pick(mine, self.z ^ mask, 0), pick(got, self.z ^ mask, 0))
            parts.append(permute(jnp.concatenate([part, sent], 0), "fsdp", 2 * mask))
        return tuple(parts)

    def result(self, parts):
        if not is_walk():
            own = lax.psum_scatter(self.terms, "fsdp", scatter_dimension=0, tiled=False)
            return own.astype(F32), lax.psum(self.vector, "fsdp")
        total, vector = self.total, self.vector
        for part in parts:
            total = total + part[: self.rows].astype(F32)
            vector = vector + joined(part[self.rows :])
        return total, vector


class RingSum:
    def __init__(self, terms, table):
        self.terms = terms
        self.table = table
        self.at = 0
        self.sent = ()
        self.first = 0


def ring_payload(steps, firsts, which, t_ref, *refs):
    del t_ref
    terms, refs = refs[: 2 * len(steps)], refs[2 * len(steps) :]
    forth_out, back_out = refs[-2:]
    row = 0
    for at, step in enumerate(steps):
        ahead, behind = terms[2 * at][0], terms[2 * at + 1][0]
        deep = ahead.shape[0]
        half = deep // 2
        if step == 0:
            forth_out[row : row + half] = ahead[:half]
            back_out[row : row + half] = behind[half:]
            row += half
            continue
        count = half if step == 1 else deep
        span = pl.ds(firsts[at], count)
        forth = refs[2 * which[at]][span, :].astype(F32)
        back = refs[2 * which[at] + 1][span, :].astype(F32)
        if step == 1:
            forth_out[row : row + half] = (ahead[:half].astype(F32) + forth).astype(BF16)
            forth_out[row + half : row + deep] = ahead[half:]
            back_out[row : row + half] = behind[:half]
            back_out[row + half : row + deep] = (behind[half:].astype(F32) + back).astype(BF16)
        else:
            forth_out[row : row + deep] = (ahead.astype(F32) + forth).astype(BF16)
            back_out[row : row + deep] = (behind.astype(F32) + back).astype(BF16)
        row += deep


def ring_final(firsts, which, t_ref, *refs):
    del t_ref
    count = len(firsts)
    terms, outs = refs[:count], refs[-count:]
    arrived = refs[count:-count]
    for at in range(count):
        deep = outs[at].shape[0]
        span = pl.ds(firsts[at], deep)
        outs[at][...] = (
            terms[at][0].astype(F32)
            + arrived[2 * which[at]][span, :].astype(F32)
            + arrived[2 * which[at] + 1][span, :].astype(F32)
        )


def term_spec(terms, slot):
    return pl.BlockSpec((1,) + terms.shape[1:], lambda at, t: (t[1 + slot], 0, 0))


def arrivals(rings):
    pairs, which = [], []
    for ring in rings:
        if not ring.sent:
            which.append(0)
            continue
        known = [at for at, pair in enumerate(pairs) if pair[0] is ring.sent[0]]
        which.append(known[0] if known else len(pairs))
        if not known:
            pairs.append(ring.sent)
    return [item for pair in pairs for item in pair], tuple(which)


def ring_step(rings, *earlier):
    if not is_walk():
        return ()
    arrived, which = arrivals(rings)
    if earlier and arrived:
        arrived = list(lax.optimization_barrier(tuple(arrived) + tuple(earlier))[: len(arrived)])
    table = rings[0].table
    if earlier and not arrived:
        table = after(table, *earlier)
    ins, in_specs, rows = [], [], 0
    firsts = []
    deep, width = rings[0].terms.shape[1:]
    for ring in rings:
        slots = ((4, 4), (3, 5), (2, 6), (1, 7))[ring.at]
        ins += [ring.terms, ring.terms]
        in_specs += [term_spec(ring.terms, slots[0]), term_spec(ring.terms, slots[1])]
        firsts.append(ring.first)
        ring.first = rows
        rows += deep if ring.at else deep // 2
    ins += arrived
    in_specs += [whole_spec(item.shape) for item in arrived]
    out = jax.ShapeDtypeStruct((rows, width), BF16)
    steps = tuple(ring.at for ring in rings)
    body = partial(ring_payload, steps, tuple(firsts), which)
    forth, back = call(
        body, table, 1, ins, in_specs, [out, out], [whole_spec(out.shape)] * 2, [], 10**6, "ring_payload"
    )
    sent = ring_pair(forth, back)
    for ring in rings:
        ring.sent = sent
        ring.at += 1
    return forth, back


def ring_pin(rings, *values):
    arrived, _ = arrivals(rings)
    if not arrived:
        return values
    olds = {id(item): at for at, item in enumerate(arrived)}
    done = lax.optimization_barrier(tuple(arrived) + tuple(values))
    for ring in rings:
        if ring.sent:
            ring.sent = tuple(done[olds[id(item)]] for item in ring.sent)
    return done[len(arrived) :]


def ring_results(rings):
    if not is_walk():
        return [
            lax.psum_scatter(ring.terms, "fsdp", scatter_dimension=0, tiled=False).astype(F32)
            for ring in rings
        ]
    arrived, which = arrivals(rings)
    ins = [ring.terms for ring in rings] + arrived
    in_specs = [term_spec(ring.terms, 0) for ring in rings]
    in_specs += [whole_spec(item.shape) for item in arrived]
    outs = [jax.ShapeDtypeStruct(ring.terms.shape[1:], F32) for ring in rings]
    out_specs = [whole_spec(item.shape) for item in outs]
    body = partial(ring_final, tuple(ring.first for ring in rings), which)
    return call(body, rings[0].table, 1, ins, in_specs, outs, out_specs, [], 10**6, "ring_final")


def dot(left, right):
    return jnp.dot(left, right, preferred_element_type=F32)


def dot_t(left, right):
    return lax.dot_general(left, right, (((1,), (1,)), ((), ())), preferred_element_type=F32)


def shifted_sum(value, sign):
    width = value.shape[1]
    lane = lax.broadcasted_iota(jnp.int32, value.shape, 1)
    by = 1
    while by < width:
        if sign > 0:
            value = value + jnp.where(lane >= by, pltpu.roll(value, by, 1), 0.0)
        else:
            value = value + jnp.where(lane < width - by, pltpu.roll(value, width - by, 1), 0.0)
        by *= 2
    return value


def conv_parts(cur, prev, weight, bias, marks):
    rows = cur.shape[0]
    ext = jnp.concatenate([prev, cur], 0)
    pre = bias + cur * weight[3:4]
    moved = []
    for back in (1, 2, 3):
        item = ext[8 - back : 8 - back + rows]
        moved.append(item)
        pre = pre + item * marks[back - 1] * weight[3 - back : 4 - back]
    return pre, moved


def rates(u, params, seg_rows):
    u = u + params[:, 0:1]
    rate = jnp.exp(params[:, 1:2])
    dt = jnp.maximum(u, 0.0) + jnp.log1p(jnp.exp(-jnp.abs(u)))
    log_dt = jnp.where(u < -15.0, u, jnp.log(dt))
    a = -dt * rate
    total = shifted_sum(a, 1)
    last = total[:, -1:]
    less = total - log_dt
    enter = jnp.exp(total) * seg_rows[1:2]
    tail = jnp.exp(last - less) * seg_rows[2:3]
    return u, dt, a, rate, total, less, enter, tail


def as_columns(first, enter, tail, lines):
    enter_hi = enter.astype(BF16).astype(F32)
    tail_hi = tail.astype(BF16).astype(F32)
    rest = jnp.zeros((128 - 5 * HEAD_ROWS - 8, enter.shape[1]), F32)
    stacked = jnp.concatenate(
        [first, enter_hi, tail_hi, enter - enter_hi, tail - tail_hi, lines, rest], 0
    )
    return stacked.T


SEG = 5 * HEAD_ROWS


def pair_masks(rows):
    lane = lax.broadcasted_iota(jnp.int32, (rows, 128), 1)
    return lane < 64, lane >= 64


def start_weight(arrays, meta, column, width, deep, table, goal, sems):
    copies = []
    for at, (array, source, rows, slot, first, by_walk) in enumerate(meta):
        row = slot * deep + first
        if by_walk:
            row = pl.multiple_of(table[1 + slot] * deep + first, 32)
        copy = pltpu.make_async_copy(
            arrays[array].at[pl.ds(source, rows), pl.ds(column * width, width)],
            goal.at[pl.ds(row, rows)],
            sems.at[at],
        )
        copy.start()
        copies.append(copy)
    return copies


def wait_all(copies):
    for copy in copies:
        copy.wait()


def scan_block(x, raw, raw_u, sr, cp, bp, hp, spread_ref, y_ref, state_ref, held, x_tail, bc_tail):
    rows = x.shape[0]
    pairs = x.shape[1] // 128
    _, _, _, _, total, less, enter, tail = rates(raw_u, hp, sr)
    cols = as_columns(total, enter, tail, sr)
    marks = [cols[:, SEG + at : SEG + at + 1] for at in (3, 4, 5)]
    pre, _ = conv_parts(x, x_tail[...], cp, cp[4:5], marks)
    xc = pre * jax.nn.sigmoid(pre)
    x_tail[...] = x[rows - 8 :]
    pre_bc, _ = conv_parts(raw, bc_tail[...], bp, bp[4:5], marks)
    bc = (pre_bc * jax.nn.sigmoid(pre_bc)).astype(BF16)
    bc_tail[...] = raw[rows - 8 :]
    states = bc.shape[1] // 2
    b_rows, c_rows = bc[:, :states], bc[:, states:]

    cols_low = cols.astype(BF16)
    enter_x = dot(cols_low, spread_ref[0])
    tail_x = dot(cols_low, spread_ref[1])

    at_t = lax.broadcasted_iota(jnp.int32, (rows, rows), 0)
    at_s = lax.broadcasted_iota(jnp.int32, (rows, rows), 1)
    bar = jnp.where((cols[:, SEG : SEG + 1] == sr[0:1]) & (at_t >= at_s), 0.0, NEG)
    scores = dot_t(c_rows, b_rows)
    state = held[...]
    state_ref[0] = state
    entering = dot(c_rows, state.astype(BF16)) * enter_x
    xl = xc.astype(BF16)
    low_mask, high_mask = pair_masks(rows)
    zero = jnp.zeros((rows, 128), BF16)
    for pair in range(pairs):
        span = slice(pair * 128, pair * 128 + 128)
        part = xl[:, span]
        acc = entering[:, span] + xc[:, span] * cp[5:6, span]
        for side, mask in ((0, low_mask), (1, high_mask)):
            head = 2 * pair + side
            weights = jnp.exp(cols[:, head : head + 1] - less[head : head + 1] + bar) * scores
            acc = acc + dot(weights.astype(BF16), jnp.where(mask, part, zero))
        y_ref[0, :, span] = acc
    keep = enter_x[rows - 1 : rows]
    held[...] = state * keep + dot(
        b_rows.astype(F32).T.astype(BF16), (xc * tail_x).astype(BF16)
    )


def mix_backward(is_first, t_ref, *refs):
    (
        x_ref, xp_ref, bc_ref, bcp_ref, u_ref, sr_ref, y_ref, dy_ref, state_ref,
        cp_ref, bp_ref, hp_ref, spread_ref, heads_ref,
    ) = refs[:14]
    dx_ref, dbc_ref, du_ref, *carried = refs[-9:]
    gx_ref, gbc_ref, gh_ref, held, x_next, bc_next = carried
    rows = x_ref.shape[1]
    width = x_ref.shape[2]
    pairs = width // 128

    @pl.when(pl.program_id(0) == 0)
    def _():
        for at, ref in enumerate(carried):
            if is_first:
                ref[...] = refs[14][...] if at == 0 else jnp.zeros_like(ref)
            else:
                ref[...] = refs[17 + at][...]

    sr = sr_ref[0]
    cp, bp = cp_ref[0], bp_ref[...]
    u, dt, a, rate, total, less, enter, tail = rates(u_ref[0], hp_ref[0], sr)
    cols = as_columns(less, enter, tail, sr)
    marks = [cols[:, SEG + at : SEG + at + 1] for at in (3, 4, 5)]
    x = x_ref[0].astype(F32)
    pre, x_moved = conv_parts(x, xp_ref[0][8:].astype(F32), cp, cp[4:5], marks)
    sig = jax.nn.sigmoid(pre)
    xc = pre * sig
    raw = bc_ref[0]
    pre_bc, bc_moved = conv_parts(raw, bcp_ref[0], bp, bp[4:5], marks)
    sig_bc = jax.nn.sigmoid(pre_bc)
    bc = (pre_bc * sig_bc).astype(BF16)
    states = bc.shape[1] // 2
    b_rows, c_rows = bc[:, :states], bc[:, states:]

    cols_low = cols.astype(BF16)
    enter_x = dot(cols_low, spread_ref[0])
    tail_x = dot(cols_low, spread_ref[1])
    keep = enter_x[rows - 1 : rows]

    at_s = lax.broadcasted_iota(jnp.int32, (rows, rows), 0)
    at_t = lax.broadcasted_iota(jnp.int32, (rows, rows), 1)
    bar = jnp.where((cols[:, SEG : SEG + 1] == sr[0:1]) & (at_t >= at_s), 0.0, NEG)
    scores = dot_t(b_rows, c_rows)

    dyl = dy_ref[0]
    dy = dyl.astype(F32)
    xl = xc.astype(BF16)
    state = state_ref[0]
    d_state = held[...]
    d_state_low = d_state.astype(BF16)
    entered = (dy * enter_x).astype(BF16)
    dc = dot_t(entered, state.astype(BF16))
    db = dot_t((xc * tail_x).astype(BF16), d_state_low)
    dx_tail = dot(b_rows, d_state_low) * tail_x
    x_round = xl.astype(F32)
    last_terms = jnp.sum(x_round * dx_tail, 0, keepdims=True) + keep * jnp.sum(
        state * d_state, 0, keepdims=True
    )
    held[...] = keep * d_state + dot(c_rows.astype(F32).T.astype(BF16), entered)

    low_mask, high_mask = pair_masks(rows)
    zero = jnp.zeros((rows, 128), BF16)
    d_scores = jnp.zeros((rows, rows), F32)
    d_scan = []
    for pair in range(pairs):
        span = slice(pair * 128, pair * 128 + 128)
        part, grad = xl[:, span], dyl[:, span]
        acc = dx_tail[:, span]
        for side, mask in ((0, low_mask), (1, high_mask)):
            head = 2 * pair + side
            decay = jnp.exp(total[head : head + 1] - cols[:, head : head + 1] + bar)
            weights = (decay * scores).astype(BF16)
            d_scores = d_scores + decay * dot_t(jnp.where(mask, part, zero), grad)
            acc = acc + dot(weights, jnp.where(mask, grad, zero))
        d_scan.append(acc)
    d_scan = jnp.concatenate(d_scan, 1)
    db = db + dot(d_scores.astype(BF16), c_rows)
    dc = dc + dot(d_scores.T.astype(BF16), b_rows)

    skip = cp[5:6]
    from_x = x_round * d_scan
    from_t = dy * (y_ref[0] - skip * xc) - from_x
    row_at = lax.broadcasted_iota(jnp.int32, (rows, width), 0)
    from_t = from_t + jnp.where(row_at == rows - 1, last_terms, 0.0)

    def per_head(value):
        high = value.astype(BF16)
        return dot_t(heads_ref[...], high) + dot_t(
            heads_ref[...], (value - high.astype(F32)).astype(BF16)
        )

    q = per_head(from_x)
    da = shifted_sum(per_head(from_t), -1)
    slope = jax.nn.sigmoid(u)
    ratio = jnp.where(u < -15.0, 1.0, slope / dt)
    du = q * ratio - da * rate * slope
    du_ref[0] = du
    gh_ref[0] += jnp.sum(du, 1, keepdims=True)
    gh_ref[1] += jnp.sum(da * a, 1, keepdims=True)
    both = jnp.concatenate([gh_ref[0], gh_ref[1], jnp.zeros((128 - 2 * HEAD_ROWS, 128), F32)], 0)
    gx_ref[7:8, 0:128] = both.T[0:1]

    def conv_back(d_out, cur, moved, weight, carried, grads):
        grads[3:4] += jnp.sum(d_out * cur, 0, keepdims=True)
        grads[4:5] += jnp.sum(d_out, 0, keepdims=True)
        result = d_out * weight[3:4]
        for back in (1, 2, 3):
            kept = d_out * marks[back - 1]
            grads[3 - back : 4 - back] += jnp.sum(kept * moved[back - 1], 0, keepdims=True)
            ext = jnp.concatenate([kept, carried[back - 1]], 0)
            result = result + ext[back : back + rows] * weight[3 - back : 4 - back]
            carried[back - 1] = kept[:8]
        return result

    gx_ref[5:6] += jnp.sum(dy * xc, 0, keepdims=True)
    d_pre = (d_scan + skip * dy) * (sig * (1.0 + pre * (1.0 - sig)))
    dx_ref[0] = conv_back(d_pre, x, x_moved, cp, x_next, gx_ref).astype(BF16)
    d_bc = jnp.concatenate([db, dc], 1) * (sig_bc * (1.0 + pre_bc * (1.0 - sig_bc)))
    dbc_ref[0] = conv_back(d_bc, raw, bc_moved, bp, bc_next, gbc_ref).astype(BF16)


def input_backward(n_x, meta_x, n_z, meta_z, cols_xz, t_ref, *refs):
    dx_ref, dz_ref, dbc_ref, du_ref, rows_ref, wbc_ref, wdt_ref = refs[:7]
    x_parts, z_parts = refs[7 : 7 + n_x], refs[7 + n_x : 7 + n_x + n_z]
    send_ref, keep_ref, gdt_ref, gn_ref, wx, wz, sem_x, sem_z = refs[7 + n_x + n_z :]
    step = pl.program_id(0)
    width = wx.shape[1]
    deep = wx.shape[0] // (t_ref.shape[0] - 1)

    @pl.when(step == 0)
    def _():
        copies = start_weight(x_parts, meta_x, cols_xz[0], width, deep, t_ref, wx, sem_x)
        copies += start_weight(z_parts, meta_z, cols_xz[1], width, deep, t_ref, wz, sem_z)
        wait_all(copies)
        gdt_ref[...] = jnp.zeros_like(gdt_ref)
        gn_ref[...] = jnp.zeros_like(gn_ref)

    normed = rows_ref[0]
    du = du_ref[0]
    gdt_ref[...] += dot(du.astype(BF16), normed)
    total = dot_t(dz_ref[0], wz[...]) + dot_t(dx_ref[0], wx[...]) + dot_t(dbc_ref[0], wbc_ref[...])
    du_cols = jnp.concatenate([du, jnp.zeros((128 - du.shape[0], du.shape[1]), F32)], 0).T
    total = total + dot(du_cols.astype(BF16), wdt_ref[...])
    gn_ref[...] += jnp.sum(total * normed.astype(F32), 0, keepdims=True)
    out = total.astype(BF16)

    @pl.when(step < 2)
    def _():
        send_ref[0] = out

    @pl.when(step >= 2)
    def _():
        keep_ref[0] = out


def project_scan(n_x, meta_x, col_x, with_norm, t_ref, *refs):
    slots, refs = refs[:4], refs[4:]
    gain_ref, wbc_ref, wdt_ref, sr_ref, cp_ref, bp_ref, hp_ref, spread_ref = refs[:8]
    refs = refs[8:]
    x_parts, refs = refs[:n_x], refs[n_x:]
    rows_ref, x_ref, bc_ref, u_ref, y_ref, state_ref = refs[:6]
    held, x_tail, bc_tail, wx, r_s, x_s, bc_s, u_s, sem_x = refs[6:]
    step = pl.program_id(0)
    blocks = x_s.shape[0]
    deep = wx.shape[0] // (t_ref.shape[0] - 1)

    def weights():
        return start_weight(x_parts, meta_x, col_x, wx.shape[1], deep, t_ref, wx, sem_x)

    for at in range(4):

        @pl.when(step == at)
        def _():
            copies = weights() if at == 0 else []
            value = slots[at][...]
            if with_norm:
                value = value.astype(F32)
                scale = lax.rsqrt(jnp.mean(value * value, -1, keepdims=True) + EPS)
                value = (value * scale * gain_ref[...]).astype(BF16)
            r_s[...] = value
            wait_all(copies)

    @pl.when(step < blocks)
    def _():
        value = r_s[...]
        rows_ref[0] = value
        x = dot(value, wx[...])
        bc = dot(value, wbc_ref[...])
        u = dot_t(wdt_ref[...][:HEAD_ROWS], value)
        x = x.astype(BF16)
        x_ref[0], bc_ref[0], u_ref[0] = x, bc, u
        x_s[step], bc_s[step], u_s[step] = x.astype(F32), bc, u

    @pl.when(step == blocks)
    def _():
        held[...] = jnp.zeros_like(held)
        x_tail[...] = jnp.zeros_like(x_tail)
        bc_tail[...] = jnp.zeros_like(bc_tail)

    @pl.when(step >= blocks)
    def _():
        slot = (step - blocks) ^ t_ref[0]
        scan_block(
            x_s[slot], bc_s[slot], u_s[slot], sr_ref[0], cp_ref[0], bp_ref[...], hp_ref[0], spread_ref,
            y_ref, state_ref, held, x_tail, bc_tail,
        )


def lane_columns(columns, rows):
    lane = lax.broadcasted_iota(jnp.int32, (rows, 128), 1)
    result = jnp.zeros((rows, 128), F32)
    for at, column in enumerate(columns):
        result = jnp.where(lane == at, column, result)
    return result


def three_parts(value):
    high = value.astype(BF16).astype(F32)
    rest = value - high
    middle = rest.astype(BF16).astype(F32)
    return [high, middle, rest - middle]


def gate_forward(n_z, meta_z, n_o, meta_o, cols_zo, is_last, t_ref, *refs):
    rows_ref, y_ref, gain_ref = refs[:3]
    refs = refs[3:]
    cots = ()
    if is_last:
        cots, refs = refs[:4], refs[4:]
    z_parts, refs = refs[:n_z], refs[n_z:]
    o_parts, refs = refs[:n_o], refs[n_o:]
    z_ref, send_ref, keep_ref = refs[:3]
    refs = refs[3:]
    if is_last:
        cot_ref, dg_ref, sums_ref = refs[:3]
        refs = refs[3:]
    wz, wo, sem_z, sem_o = refs
    step = pl.program_id(0)
    width = wz.shape[1]
    deep = wz.shape[0] // (t_ref.shape[0] - 1)

    @pl.when(step == 0)
    def _():
        copies = start_weight(z_parts, meta_z, cols_zo[0], width, deep, t_ref, wz, sem_z)
        copies += start_weight(o_parts, meta_o, cols_zo[1], width, deep, t_ref, wo, sem_o)
        wait_all(copies)

    z = dot(rows_ref[0], wz[...]).astype(BF16)
    z_ref[0] = z
    z = z.astype(F32)
    v = y_ref[0] * (z * jax.nn.sigmoid(z))
    gain = gain_ref[0][6:7]
    squares = jnp.sum(v * v, -1, keepdims=True)
    scaled = v * gain
    part = dot_t(scaled.astype(BF16), wo[...]).astype(BF16)
    features = wz.shape[0]
    rows = z.shape[0]

    def put(ref):
        ref[0, :, :features] = part
        if not is_last:
            ref[0, :, features:] = lane_columns(three_parts(squares), rows).astype(BF16)

    @pl.when(step < 2)
    def _():
        put(send_ref)

    @pl.when(step >= 2)
    def _():
        put(keep_ref)

    if is_last:
        for at, slot in enumerate((1, 3, 0, 2)):

            @pl.when(step == at)
            def _():
                cot_ref[0] = cots[slot][...]

        d_gated = dot(cot_ref[0], wo[...])
        dg_ref[0] = d_gated.astype(BF16)
        cross = jnp.sum(d_gated * scaled, -1, keepdims=True)
        sums_ref[0] = lane_columns([squares, cross], rows).T[:8]


def gate_backward(n_o, meta_o, col_o, is_last, inner, t_ref, *refs):
    z_ref, y_ref, gain_ref = refs[:3]
    refs = refs[3:]
    if is_last:
        dg_ref, sums_ref = refs[:2]
        refs = refs[2:]
        dy_ref, dz_ref, gated_ref, gg_ref = refs
    else:
        cots, refs = refs[:4], refs[4:]
        o_parts, refs = refs[:n_o], refs[n_o:]
        dy_ref, dz_ref, gated_ref, gg_ref, cot_ref, wo, extra_s, sem_o = refs
    step = pl.program_id(0)

    @pl.when(step == 0)
    def _():
        gg_ref[...] = jnp.zeros_like(gg_ref)
        if not is_last:
            deep = wo.shape[0] // (t_ref.shape[0] - 1)
            wait_all(
                start_weight(o_parts, meta_o, col_o, wo.shape[1], deep, t_ref, wo, sem_o)
            )

    if is_last:
        d_gated = dg_ref[0].astype(F32)
        sums = sums_ref[0]
        cols = jnp.concatenate([sums, jnp.zeros((120, sums.shape[1]), F32)], 0).T
        scale = lax.rsqrt(cols[:, 0:1] / inner + EPS)
        cross = cols[:, 1:2]
    else:
        features = wo.shape[0]
        for at in range(4):

            @pl.when(step == at)
            def _():
                cot_ref[0] = cots[at][:, :features]
                extra_s[...] = cots[at][:, features:].astype(F32)

        d_gated = dot(cot_ref[0], wo[...])
        extra = extra_s[...]
        scale = extra[:, 0:1] + extra[:, 1:2] + extra[:, 2:3]
        cross = extra[:, 3:4] + extra[:, 4:5] + extra[:, 5:6]
    z, y, gain = z_ref[0].astype(F32), y_ref[0], gain_ref[0][6:7]
    sig = jax.nn.sigmoid(z)
    silu = z * sig
    v = y * silu
    normed = v * scale
    gated_ref[0] = (normed * gain).astype(BF16)
    gg_ref[6:7] += jnp.sum(d_gated * normed, 0, keepdims=True)
    dv = d_gated * gain * scale - v * (scale * scale * scale * cross / inner)
    dy_ref[0] = (dv * silu).astype(BF16)
    dz_ref[0] = (dv * y * (sig * (1.0 + z * (1.0 - sig)))).astype(BF16)


def layer_spec(array, k):
    return pl.BlockSpec((1,) + array.shape[1:], lambda at, t: (k,) + (0,) * (array.ndim - 1))


def whole_spec(shape):
    return pl.BlockSpec(shape, lambda at, t: (0,) * len(shape))


ANY = pl.BlockSpec(memory_space=pl.ANY)


def call(body, table, grid, ins, in_specs, outs, out_specs, scratch, flops, name, aliases=None):
    size = sum(item.size * item.dtype.itemsize for item in list(ins) + list(outs))
    return pl.pallas_call(
        body,
        grid_spec=pltpu.PrefetchScalarGridSpec(
            num_scalar_prefetch=1,
            grid=(grid,),
            in_specs=in_specs,
            out_specs=out_specs,
            scratch_shapes=scratch,
        ),
        out_shape=outs,
        compiler_params=pltpu.CompilerParams(
            dimension_semantics=("arbitrary",), vmem_limit_bytes=VMEM
        ),
        cost_estimate=pl.CostEstimate(flops=flops, bytes_accessed=size, transcendentals=0),
        name=name,
        input_output_aliases=aliases or {},
    )(table, *ins)


def run_project(k, table, slots, gain, w_bc, w_dt, lines, params, bc_params, spread, weight, col, norm):
    blocks = len(slots)
    rows, features = slots[0].shape
    wide = w_bc.shape[1]
    chan, head = params
    width = chan.shape[2]
    states = wide // 2
    last = blocks - 1

    def early(shape):
        return pl.BlockSpec((1,) + shape, lambda at, t: (jnp.minimum(at, last), 0, 0))

    def block(shape):
        return pl.BlockSpec((1,) + shape, lambda at, t: (jnp.maximum(at - blocks, 0), 0, 0))

    def slot(shape):
        return pl.BlockSpec((1,) + shape, lambda at, t: (jnp.maximum(at - blocks, 0) ^ t[0], 0, 0))

    ins = [*slots, gain, w_bc, w_dt, lines, chan, bc_params, head, spread, *weight[0]]
    in_specs = [whole_spec(item.shape) for item in slots]
    in_specs += [whole_spec(item.shape) for item in (gain, w_bc, w_dt)]
    in_specs += [block((8, rows)), layer_spec(chan, k), whole_spec(bc_params.shape)]
    in_specs += [layer_spec(head, k), whole_spec(spread.shape)] + [ANY] * len(weight[0])
    outs = [
        jax.ShapeDtypeStruct((blocks, rows, features), BF16),
        jax.ShapeDtypeStruct((blocks, rows, width), BF16),
        jax.ShapeDtypeStruct((blocks, rows, wide), F32),
        jax.ShapeDtypeStruct((blocks, HEAD_ROWS, rows), F32),
        jax.ShapeDtypeStruct((blocks, rows, width), F32),
        jax.ShapeDtypeStruct((blocks, states, width), F32),
    ]
    out_specs = [
        early((rows, features)), early((rows, width)), early((rows, wide)),
        early((HEAD_ROWS, rows)), slot((rows, width)), block((states, width)),
    ]
    scratch = [
        pltpu.VMEM((states, width), F32),
        pltpu.VMEM((8, width), F32),
        pltpu.VMEM((8, wide), F32),
        pltpu.VMEM((features, width), BF16),
        pltpu.VMEM((rows, features), BF16),
        pltpu.VMEM((blocks, rows, width), F32),
        pltpu.VMEM((blocks, rows, wide), F32),
        pltpu.VMEM((blocks, HEAD_ROWS, rows), F32),
        pltpu.SemaphoreType.DMA((len(weight[1]),)),
    ]
    body = partial(project_scan, len(weight[0]), weight[1], col, norm)
    return call(body, table, 2 * blocks, ins, in_specs, outs, out_specs, scratch, 10**10, "project_scan")


def run_gate_forward(k, table, rows, y, chan, cots, w_z, w_o, cols):
    blocks, count, features = rows.shape
    width = y.shape[2]
    is_last = cots is not None
    extra = 0 if is_last else 128

    def slot(shape):
        return pl.BlockSpec((1,) + shape, lambda at, t: (2 * at + 1 - 5 * (at // 2), 0, 0))

    cots = cots or []
    ins = [rows, y, chan, *cots, *w_z[0], *w_o[0]]
    in_specs = [slot((count, features)), slot((count, width)), layer_spec(chan, k)]
    in_specs += [whole_spec(item.shape) for item in cots] + [ANY] * (len(w_z[0]) + len(w_o[0]))
    half = jax.ShapeDtypeStruct((2, count, features + extra), BF16)
    outs = [jax.ShapeDtypeStruct((blocks, count, width), BF16), half, half]
    out_specs = [
        slot((count, width)),
        pl.BlockSpec((1, count, features + extra), lambda at, t: (jnp.minimum(at, 1), 0, 0)),
        pl.BlockSpec((1, count, features + extra), lambda at, t: (jnp.maximum(at - 2, 0), 0, 0)),
    ]
    if is_last:
        outs += [
            jax.ShapeDtypeStruct((blocks, count, features), BF16),
            jax.ShapeDtypeStruct((blocks, count, width), BF16),
            jax.ShapeDtypeStruct((blocks, 8, count), F32),
        ]
        out_specs += [slot((count, features)), slot((count, width)), slot((8, count))]
    scratch = [
        pltpu.VMEM((features, width), BF16),
        pltpu.VMEM((features, width), BF16),
        pltpu.SemaphoreType.DMA((len(w_z[1]),)),
        pltpu.SemaphoreType.DMA((len(w_o[1]),)),
    ]
    body = partial(gate_forward, len(w_z[0]), w_z[1], len(w_o[0]), w_o[1], cols, is_last)
    return call(body, table, blocks, ins, in_specs, outs, out_specs, scratch, 6 * 10**9, "gate_forward")


def run_gate_backward(k, table, z, y, chan, known, cots, w_o, col, inner):
    blocks, count, width = z.shape
    is_last = cots is None

    def slot(shape):
        return pl.BlockSpec((1,) + shape, lambda at, t: (at, 0, 0))

    ins = [z, y, chan]
    in_specs = [slot((count, width)), slot((count, width)), layer_spec(chan, k)]
    outs = [
        jax.ShapeDtypeStruct((blocks, count, width), BF16),
        jax.ShapeDtypeStruct((blocks, count, width), BF16),
        jax.ShapeDtypeStruct((blocks, count, width), BF16),
        jax.ShapeDtypeStruct((8, width), F32),
    ]
    out_specs = [slot((count, width))] * 3 + [whole_spec((8, width))]
    scratch = []
    if is_last:
        ins += list(known)
        in_specs += [slot((count, width)), slot((8, count))]
    else:
        features = cots[0].shape[1] - 128
        ins += [*cots, *w_o[0]]
        in_specs += [whole_spec(item.shape) for item in cots] + [ANY] * len(w_o[0])
        outs.append(jax.ShapeDtypeStruct((blocks, count, features), BF16))
        out_specs.append(slot((count, features)))
        scratch = [
            pltpu.VMEM((features, width), BF16),
            pltpu.VMEM((count, 128), F32),
            pltpu.SemaphoreType.DMA((len(w_o[1]),)),
        ]
    body = partial(gate_backward, len(w_o[0]), w_o[1], col, is_last, inner)
    return call(body, table, blocks, ins, in_specs, outs, out_specs, scratch, 3 * 10**9, "gate_backward")


def run_mix_backward(k, table, x, bc, u, lines, y, dy, state, params, bc_params, spread, heads_of, gg, top, steps, before):
    blocks, rows, width = x.shape
    wide = bc.shape[2]
    states = wide // 2
    chan, head = params

    def slot(shape):
        return pl.BlockSpec((1,) + shape, lambda at, t: ((top - at) ^ t[0], 0, 0))

    def earlier(shape):
        return pl.BlockSpec(
            (1,) + shape,
            lambda at, t: (jnp.maximum(top - at - 1, 0) ^ t[0], rows // shape[0] - 1, 0),
        )

    def straight(shape):
        return pl.BlockSpec((1,) + shape, lambda at, t: (top - at, 0, 0))

    ins = [x, x, bc, bc, u, lines, y, dy, state, chan, bc_params, head, spread, heads_of]
    in_specs = [
        slot((rows, width)), earlier((16, width)), slot((rows, wide)), earlier((8, wide)),
        slot((HEAD_ROWS, rows)), straight((8, rows)),
        slot((rows, width)), slot((rows, width)), straight((states, width)),
        layer_spec(chan, k), whole_spec(bc_params.shape), layer_spec(head, k),
        whole_spec(spread.shape), whole_spec(heads_of.shape),
    ]
    outs = [
        jax.ShapeDtypeStruct((blocks, rows, width), BF16),
        jax.ShapeDtypeStruct((blocks, rows, wide), BF16),
        jax.ShapeDtypeStruct((blocks, HEAD_ROWS, rows), F32),
        jax.ShapeDtypeStruct((8, width), F32),
        jax.ShapeDtypeStruct((8, wide), F32),
        jax.ShapeDtypeStruct((2, HEAD_ROWS, 128), F32),
        jax.ShapeDtypeStruct((states, width), F32),
        jax.ShapeDtypeStruct((3, 8, width), F32),
        jax.ShapeDtypeStruct((3, 8, wide), F32),
    ]
    out_specs = [slot((rows, width)), slot((rows, wide)), slot((HEAD_ROWS, rows))]
    out_specs += [whole_spec(item.shape) for item in outs[3:]]
    aliases = {}
    if before:
        aliases = {1 + len(ins) + at: at for at in range(3)}
        ins += list(before)
        in_specs += [ANY] * 3 + [whole_spec(item.shape) for item in outs[3:]]
    else:
        ins.append(gg)
        in_specs.append(whole_spec(gg.shape))
    body = partial(mix_backward, not before)
    return call(body, table, steps, ins, in_specs, outs, out_specs, [], 2 * 10**9 * steps, "mix_backward", aliases)


def run_input_backward(table, dx, dz, dbc, du, normed, w_bc, w_dt, w_x, w_z, cols):
    blocks, rows, width = dx.shape
    features = normed.shape[2]
    wide = dbc.shape[2]

    def slot(shape):
        return pl.BlockSpec((1,) + shape, lambda at, t: (2 * at + 1 - 5 * (at // 2), 0, 0))

    ins = [dx, dz, dbc, du, normed, w_bc, w_dt, *w_x[0], *w_z[0]]
    in_specs = [slot((rows, width)), slot((rows, width)), slot((rows, wide)), slot((HEAD_ROWS, rows))]
    in_specs += [slot((rows, features)), whole_spec(w_bc.shape), whole_spec(w_dt.shape)]
    in_specs += [ANY] * (len(w_x[0]) + len(w_z[0]))
    half = jax.ShapeDtypeStruct((2, rows, features), BF16)
    outs = [
        half, half,
        jax.ShapeDtypeStruct((HEAD_ROWS, features), F32),
        jax.ShapeDtypeStruct((1, features), F32),
    ]
    out_specs = [
        pl.BlockSpec((1, rows, features), lambda at, t: (jnp.minimum(at, 1), 0, 0)),
        pl.BlockSpec((1, rows, features), lambda at, t: (jnp.maximum(at - 2, 0), 0, 0)),
        whole_spec((HEAD_ROWS, features)), whole_spec((1, features)),
    ]
    scratch = [
        pltpu.VMEM((features, width), BF16),
        pltpu.VMEM((features, width), BF16),
        pltpu.SemaphoreType.DMA((len(w_x[1]),)),
        pltpu.SemaphoreType.DMA((len(w_z[1]),)),
    ]
    body = partial(input_backward, len(w_x[0]), w_x[1], len(w_z[0]), w_z[1], cols)
    return call(body, table, blocks, ins, in_specs, outs, out_specs, scratch, 7 * 10**9, "input_backward")


def segment_lines(segment, blocks):
    rows = segment.shape[0] // blocks
    cut = segment.reshape(blocks, rows)
    ends = cut[:, -1:]
    before = jnp.concatenate([cut[:1, :1], ends[:-1]], 0)
    kinds = [cut.astype(F32), (cut == before).astype(F32), (cut == ends).astype(F32)]
    for back in (1, 2, 3):
        earlier = jnp.pad(segment, (back, 0), constant_values=-1)[: segment.shape[0]]
        kinds.append((segment == earlier).astype(F32).reshape(blocks, rows))
    at = jnp.arange(8)[None, :, None]
    lines = jnp.zeros((blocks, 8, rows), F32)
    for index, kind in enumerate(kinds):
        lines = jnp.where(at == index, kind[:, None], lines)
    return lines


def head_tables(heads, width):
    owner = np.arange(width)[None, :] // (width // heads)
    at = np.arange(128)[:, None]
    spread_enter = (at == owner + HEAD_ROWS) | (at == owner + 3 * HEAD_ROWS)
    spread_tail = (at == owner + 2 * HEAD_ROWS) | (at == owner + 4 * HEAD_ROWS)
    spread = np.stack([spread_enter, spread_tail]).astype(np.float32)
    owners = (at[:HEAD_ROWS] == owner).astype(np.float32)
    return jnp.asarray(spread, BF16), jnp.asarray(owners, BF16)


def norm_scale_of(values):
    return lax.rsqrt(jnp.mean(values * values, -1, keepdims=True) + EPS)


def shards(
    hidden, segment_ids, cotangent, norm_gain, in_zx, in_dt, in_bc, conv_x, conv_x_bias,
    conv_bc, conv_bc_bias, dt_bias, a_log, skip_d, gated_gain, out_wt,
):
    layers = in_zx.shape[0]
    count = lax.axis_size("fsdp")
    tp_count = lax.axis_size("tp")
    tp_at = lax.axis_index("tp").astype(jnp.int32)
    own, features = hidden.shape
    deep = in_zx.shape[1]
    width = in_zx.shape[3]
    heads = in_dt.shape[2]
    wide = in_bc.shape[2]
    bc_deep = in_bc.shape[1]
    shared = conv_bc.shape[1]
    taps = conv_bc.shape[2]
    inner = width * tp_count
    dt_lines = -(-deep * heads // wide)
    dt_rest = dt_lines * wide - deep * heads
    lines = -(-(bc_deep + dt_lines + 1) // 16) * 16
    table = placement(tp_at)

    packs, weights, wholes = [], [], []
    for k in range(layers):
        tiny = [conv_bc[k].reshape(-1), conv_bc_bias[k]]
        tiny = jnp.concatenate(tiny + ([norm_gain.reshape(-1)] if k == 0 else []))
        tiny = jnp.pad(tiny, (0, wide - tiny.shape[0]))[None]
        dt = jnp.pad(in_dt[k].T.reshape(-1), (0, dt_rest)).reshape(dt_lines, wide)
        pack = jnp.concatenate([in_bc[k], dt, tiny], 0)
        packs.append(jnp.pad(pack, ((0, lines - pack.shape[0]), (0, 0))))

    ring_x = RingGather(in_zx[0, :, 1])
    over = permute(hidden, "tp", 2)
    beside = permute(hidden, "tp", 1)
    ring_x.step()
    walk = is_walk()
    pack = double(packs[0][None, None, None, None, None], "tp", 2, 3)
    for k in range(1, layers):
        whole = lax.all_gather(packs[k], ("fsdp", "tp"), axis=0, tiled=False)
        packs[k] = whole.reshape((count, tp_count) + packs[k].shape)

    def whole_of(k, source, out):
        return jnp.concatenate([source[k, :, 1], source[k, :, 0], out[k]], 1)

    if walk:
        steps = ring_x.steps
        in_zx_late, out_wt_late, *steps[0] = lax.optimization_barrier((in_zx, out_wt) + tuple(steps[0]))
        ring_zo = RingGather(jnp.concatenate([in_zx_late[0, :, 0], out_wt_late[0]], 1))
        ring_x.step(pack)
        pack = double(after(pack, *steps[0]), "fsdp", 4, 0)
        ring_x.step(pack)
        ring_zo.step(*steps[1])
        pack = double(after(pack, *steps[1]), "fsdp", 2, 1)
        ring_x.step(pack)
        pack = double(after(pack, *steps[2]), "fsdp", 1, 2)
        ring_zo.step(pack, *steps[3])
        over = after(over, pack)
    else:
        in_zx_late, out_wt_late = in_zx, out_wt
        ring_zo = RingGather(jnp.concatenate([in_zx[0, :, 0], out_wt[0]], 1))
        pack = lax.all_gather(pack[0], "fsdp", axis=0, tiled=False)[:, None]
    packs[0] = pack = double(pack, "tp", 1, 4).reshape(count, tp_count, lines, wide)
    slots = [hidden, beside, over, permute(over, "tp", 1)]
    cot_over = permute(after(cotangent, pack), "tp", 2)
    cot_beside = permute(after(cotangent, pack), "tp", 1)
    table = after(table, pack, *ring_zo.last())
    ring_zo.step(table)

    lines_of = segment_lines(segment_ids[0], tp_count)
    spread, heads_of = head_tables(heads, width)
    w_bc, w_dt, gains, bc_params = [], [], [], []
    skips = jnp.repeat(skip_d, width // heads, axis=1)
    chan = jnp.stack([conv_x_bias, skips, gated_gain], 1)
    chan = jnp.concatenate([jnp.swapaxes(conv_x, 1, 2), chan], 1)
    chan = jnp.pad(chan, ((0, 0), (0, 1), (0, 0))).astype(F32)
    head = jnp.pad(jnp.stack([dt_bias, a_log], 2), ((0, 0), (0, HEAD_ROWS - heads), (0, 126)))
    params = (chan, head.astype(F32))

    def unpack(k):
        part = packs[k]
        w_bc.append(part[:, :, :bc_deep].reshape(features, wide))
        dt = pick(part[:, :, bc_deep : bc_deep + dt_lines], tp_at, 1)
        dt = dt.reshape(count, -1)[:, : heads * deep]
        dt = dt.reshape(count, heads, deep).swapaxes(0, 1).reshape(heads, features)
        w_dt.append(jnp.pad(dt, ((0, 128 - heads), (0, 0))))
        tiny = part[:, :, bc_deep + dt_lines]
        if k == 0:
            first = shared * (taps + 1)
            every = tiny[:, :, first : first + layers * bc_deep]
            every = every.reshape(features // bc_deep, layers, bc_deep).swapaxes(0, 1)
            gains.extend(every.reshape(layers, 1, features).astype(F32))
        taps_bc = tiny[:, :, : shared * taps].reshape(wide, taps).astype(F32)
        bias_bc = tiny[:, :, shared * taps : shared * (taps + 1)].reshape(1, wide).astype(F32)
        bc_params.append(jnp.pad(jnp.concatenate([taps_bc.T, bias_bc], 0), ((0, 3), (0, 0))))

    running = hidden.astype(F32)
    saved = []
    for k in range(layers):
        if k:
            normed = (running * norm_scale_of(running) * gains[k]).astype(BF16)
            over = permute(normed, "tp", 2)
            beside = permute(normed, "tp", 1)
            if walk:
                ring_all.step(normed)
                over, *ring_all.steps[2] = lax.optimization_barrier((over,) + tuple(ring_all.steps[2]))
                ring_all.step()
            slots = [normed, beside, over, permute(over, "tp", 1)]
        unpack(k)
        w_x = ring_x.weight() if k == 0 else ring_all.weight()
        rows, x, bc, u, y, state = run_project(
            k, table, slots, gains[k], w_bc[k], w_dt[k], lines_of, params, bc_params[k], spread, w_x, 0, k == 0
        )
        if k == 0:
            y, cot_over, *_ = lax.optimization_barrier((y, cot_over) + tuple(ring_zo.last()))
            ring_zo.step(y)
            cots_last = [cotangent, cot_beside, cot_over, permute(cot_over, "tp", 1)]
            w_zo, cols_zo = ring_zo.weight(), (0, 1)
        else:
            w_zo, cols_zo = w_x, (1, 2)
        weights.append((w_x, w_zo, cols_zo))
        entry = dict(rows=rows, x=x, bc=bc, u=u, y=y, state=state, h=running)
        is_last = k == layers - 1
        if not is_last:
            next_ring = RingGather(whole_of(k + 1, in_zx_late, out_wt_late))
            next_ring.step(*(ring_zo.last() if k == 0 else (y,)))
        z, send, keep, *more = run_gate_forward(
            k, table, rows, y, chan, cots_last if is_last else None, w_zo, w_zo, cols_zo
        )
        if not is_last and walk:
            send, z, *next_ring.steps[0] = lax.optimization_barrier((send, z) + tuple(next_ring.steps[0]))
        entry["z"] = z
        entry["near"] = near = permute(send, "tp", 1)
        if not is_last:
            ring_all = next_ring
            going = plus(keep[1], near[1])
            far = permute(going, "tp", 2)
            if walk:
                ring_all.step(going)
                far, *ring_all.steps[1] = lax.optimization_barrier((far,) + tuple(ring_all.steps[1]))
        else:
            cot, d_gated, sums = more
            sums = tp_sum_slots(sums)
            far = permute(plus(keep[1], near[1]), "tp", 2)
            entry.update(cot=cot, d_gated=d_gated, sums=sums, far=far, parts=keep[0].astype(F32) + near[0].astype(F32))
        if not is_last:
            branch = keep[0].astype(F32) + near[0].astype(F32) + far.astype(F32)
            squares = jnp.sum(branch[:, features:], -1, keepdims=True)
            branch = branch[:, :features]
            scale = lax.rsqrt(squares / inner + EPS)
            entry.update(branch=branch, scale=scale)
            running = running + branch * scale
        saved.append(entry)

    grad_run = cotangent.astype(F32)
    parts = [None] * layers

    def small_sum(parts):
        d_bc, g_norm, gbc, g_dt, gx = (jnp.stack(item) for item in zip(*parts))
        room = (layers, count, tp_count)
        d_norm = (g_norm / jnp.stack(gains)).reshape(room + (bc_deep,))
        d_conv = gbc[:, : taps + 1].reshape((layers, taps + 1) + room[1:] + (shared,))
        d_conv = d_conv.transpose(0, 2, 3, 1, 4).reshape(room + ((taps + 1) * shared,))
        d_tiny = jnp.concatenate([d_norm, d_conv], 3).astype(BF16)
        d_tiny = jnp.pad(d_tiny, ((0, 0), (0, 0), (0, 0), (0, wide - d_tiny.shape[3])))
        d_pack = jnp.concatenate([d_bc.reshape(room + (bc_deep, wide)), d_tiny[:, :, :, None]], 3)
        d_pack = d_pack.transpose(1, 2, 0, 3, 4).reshape(count, tp_count, -1, wide)
        d_dt = g_dt[:, :heads].reshape(layers, heads, count, deep).transpose(2, 0, 1, 3)
        d_dt = jnp.pad(d_dt.reshape(count, layers, -1), ((0, 0), (0, 0), (0, dt_rest))).astype(BF16)
        return SmallSum(d_pack, d_dt.reshape(count, -1, wide), gx.reshape(-1, wide))

    sums_of = [None] * layers
    for k in reversed(range(layers)):
        item = saved[k]
        rows, z, y = item["rows"], item["z"], item["y"]
        w_x, w_zo, cols_zo = weights[k]
        if k == layers - 1:
            cot = item["cot"]
            dy, dz, gated, g_gain = run_gate_backward(
                k, table, z, y, chan, (item["d_gated"], item["sums"]), None, w_zo, cols_zo[1], inner
            )
        else:
            low = grad_run.astype(BF16)
            cross = jnp.sum(low.astype(F32) * item["branch"], -1, keepdims=True)
            extra = three_parts(item["scale"]) + three_parts(cross)
            extra = jnp.concatenate(extra, 1).astype(BF16)
            low = jnp.concatenate([low, jnp.pad(extra, ((0, 0), (0, 128 - 6)))], 1)
            cots = tp_gather(low)
            if walk:
                later_rings = sums_of[k + 1]
                (low_now,) = ring_pin(later_rings, low)
                sums_of[k + 1] = later_rings[:2] + (ring_results(later_rings[:2]), later_rings[2])
                last_x = later_rings[2]
                ring_step([last_x], low_now)
                (cots[2],) = ring_pin([last_x], cots[2])
                ring_step([last_x])
            dy, dz, gated, g_gain, cot = run_gate_backward(
                k, table, z, y, chan, None, cots, w_zo, cols_zo[1], inner
            )
            if walk:
                (dy,) = ring_pin([last_x], dy)

        def weight_grad(left, right):
            result = lax.dot_general(
                left, right, (((0, 1), (0, 1)), ((), ())), preferred_element_type=F32
            )
            return result.astype(BF16)

        ring_o = RingSum(weight_grad(cot, gated).reshape(count, deep, width), table)
        ring_z = RingSum(weight_grad(rows, dz).reshape(count, deep, width), table)
        early = [ring_o, ring_z]
        dy = after(dy, *ring_step(early, dy), ring_o.terms, ring_z.terms)
        if k == layers - 1:
            dy = after(dy, saved[k]["near"])
        splits = (tp_count // 2, tp_count - tp_count // 2)
        done, top = None, tp_count - 1
        for steps in splits:
            done = run_mix_backward(
                k, table, item["x"], item["bc"], item["u"], lines_of, y, dy, item["state"], params,
                bc_params[k], spread, heads_of, g_gain, top, steps, done,
            )
            top -= steps
            if top >= 0:
                done = list(done)
                (done[6],) = ring_pin(early, done[6])
                done[6] = after(done[6], *ring_step(early))
        dx, dbc, du, gx, gbc, gh = done[:6]
        (dx,) = ring_pin(early, dx)
        if k == layers - 1:
            dx, far = lax.optimization_barrier((dx, item["far"]))
            scale = lax.rsqrt(item["sums"][0, 0] / inner + EPS)[:, None]
            running = running + (item["parts"] + far.astype(F32)) * scale
        every = [ring_o, ring_z]
        if k == 0:
            ring_x = RingSum(weight_grad(rows, dx).reshape(count, deep, width), table)
            every.append(ring_x)
            sent = ring_step(every)
            dx_now = after(dx, *sent) if walk else dx
        else:
            dx_now = dx
        send, keep, g_dt, g_norm = run_input_backward(
            table, dx_now, dz, dbc, du, rows, w_bc[k], w_dt[k], w_x, w_zo, (0, cols_zo[0])
        )
        parts[k] = [weight_grad(rows, dbc), g_norm, gbc, g_dt, gx]
        if k == 0:
            (send,) = ring_pin(every, send)
            near = permute(send, "tp", 1)
            small = small_sum(parts)
            near, small.terms = lax.optimization_barrier((near, small.terms))
            going = plus(keep[1], near[1])
            far = permute(going, "tp", 2)
            ring_step(every, going)
            got = small.over_core()
            got, far = ring_pin(every, got, far)
            ring_step([ring_x], far)
            got = small.over_y(got)
            (got,) = ring_pin([ring_x], got)
            ring_step([ring_x])
            got = small.over_x(got)
            if walk:
                (got,) = ring_pin([ring_x], got)
            got = small.over_z(got)
        else:
            near = permute(send, "tp", 1)
            ring_x = RingSum(weight_grad(rows, dx).reshape(count, deep, width), table)
            every.append(ring_x)
            going, ring_x.terms = lax.optimization_barrier((plus(keep[1], near[1]), ring_x.terms))
            far = permute(going, "tp", 2)
            ring_step(every, going)
            (far,) = ring_pin(every, far)
            ring_step(every, far)
        sums_of[k] = (ring_o, ring_z, ring_x)
        if k == 0 or not walk:
            sums_of[k] = (ring_o, ring_z, ring_results([ring_o, ring_z]), ring_x)
        d_normed = keep[0].astype(F32) + near[0].astype(F32) + far.astype(F32)
        h = item["h"]
        inv = norm_scale_of(h)
        scaled = d_normed * gains[k]
        grad_run = (
            grad_run
            + inv * scaled
            - h * (inv**3 * (jnp.sum(scaled * h, -1, keepdims=True) / features))
        )

    d_pack, vector = small.result(got)
    d_dt = d_pack[layers * (bc_deep + 1) :].reshape(layers, -1)[:, : heads * deep]
    d_pack = d_pack[: layers * (bc_deep + 1)].reshape(layers, -1, wide)
    vector = vector.reshape(layers, 8, width)
    tiny = d_pack[:, bc_deep]
    conv = tiny[:, bc_deep : bc_deep + (taps + 1) * shared].reshape(layers, taps + 1, shared)
    zx, out = [], []
    for k in range(layers):
        _, _, (sum_o, sum_z), last_x = sums_of[k]
        zx.append(jnp.stack([sum_z, ring_results([last_x])[0]], 1))
        out.append(sum_o)
    return (
        running,
        grad_run,
        tiny[:, :bc_deep],
        jnp.stack(zx),
        d_dt.reshape(layers, heads, deep).swapaxes(1, 2),
        d_pack[:, :bc_deep],
        vector[:, :taps].swapaxes(1, 2),
        vector[:, taps],
        conv[:, :taps].swapaxes(1, 2),
        conv[:, taps],
        vector[:, 7, :heads],
        vector[:, 7, HEAD_ROWS : HEAD_ROWS + heads],
        jnp.sum(vector[:, 5].reshape(layers, heads, -1), 2),
        vector[:, 6],
        jnp.stack(out),
    )


def solution(mesh):
    tokens = P(("fsdp", "tp"), None)
    split = P(None, ("fsdp", "tp"))
    rows = P(None, ("fsdp", "tp"), None)
    weights = (
        split,
        P(None, "fsdp", None, "tp"),
        P(None, "fsdp", "tp"),
        rows,
        P(None, "tp", None),
        P(None, "tp"),
        rows,
        split,
        P(None, "tp"),
        P(None, "tp"),
        P(None, "tp"),
        P(None, "tp"),
        P(None, "fsdp", "tp"),
    )
    return jax.shard_map(
        shards,
        mesh=mesh,
        in_specs=(tokens, P("fsdp", None), tokens) + weights,
        out_specs=(tokens, tokens) + weights,
        check_vma=False,
    )
```

time: 899 us -> 636 us (0.71)
  Pallas kernels: 82.1 us -> 246 us
  waiting for transfers between devices: 282 us -> 163 us
  starting transfers between devices: 185 us -> 88 us
  matrix products: 125 us -> 36 us
  local copies, waits for them, and re-layouts: 123 us -> 40.7 us
  other arithmetic: 88.3 us -> 42.7 us
  between operations: 3.69 us -> 16 us
    pallas_call x4 -> x28, Pallas kernels: 82.1 us -> 246 us  [call(): pl.pallas_call(body, grid_spec=pltpu.PrefetchScalarGridSpec(num_scalar_pr...]
    ppermute x144 -> x48, waiting for transfers between devices: 176 us -> 78.3 us  [step_ring(): lax.ppermute(value, 'fsdp', [(WALK[at], WALK[(at + by) % size]) for at in...]
    dot_general x30 -> x8, matrix products: 125 us -> 36 us  [weight_grad(): lax.dot_general(left, right, (((0, 1), (0, 1)), ((), ())), preferred_elem...]
    ppermute x144 -> x48, starting transfers between devices: 152 us -> 63.1 us  [step_ring(): lax.ppermute(value, 'fsdp', [(WALK[at], WALK[(at + by) % size]) for at in...]
    unnamed x353 -> x209, local copies, waits for them, and re-layouts: 41.1 us -> 14.6 us
    ppermute x45 -> x33, waiting for transfers between devices: 107 us -> 82.6 us  [permute(): return lax.ppermute(value, axis, [(at, at ^ mask) for at in range(size)])]
    another operation x51 -> x18, local copies, waits for them, and re-layouts: 19.6 us -> 4.5 us  [the longest x3 2.6 us: unpack(): gains.extend(every.reshape(layers, 1, features).astype(F32))]
    squeeze x12 -> x9, local copies, waits for them, and re-layouts: 16.4 us -> 1.81 us  [the longest x3 1.69 us: pick(): lax.dynamic_index_in_dim(value, at, axis, keepdims=False, allow_negative_...]
  transfers between devices with their start and end apart: 189 -> 82, of which waited for: 78 -> 38; matrix products, arithmetic and copies ran while one was open for 27% -> 13% of each run, Pallas kernels for 3% -> 31%
where the time goes in v2:
time: 636 us; the launch traced here: 632 us
  Pallas kernels  246 us (39%)
  waiting for transfers between devices  163 us (26%)
  starting transfers between devices  88 us (14%)
  other arithmetic  42.7 us (7%)
  local copies, waits for them, and re-layouts  40.7 us (6%)
  matrix products  36 us (6%)
  between operations  16 us (3%)
    pallas_call x28, Pallas kernels, call(): pl.pallas_call(body, grid_spec=pltpu.PrefetchScalarGridSpec(num_scalar_pr...  246 us
    ppermute x33, waiting for transfers between devices, permute(): return lax.ppermute(value, axis, [(at, at ^ mask) for at in range(size)])  82.6 us
    ppermute x48, waiting for transfers between devices, step_ring(): lax.ppermute(value, 'fsdp', [(WALK[at], WALK[(at + by) % size]) for at in...  78.3 us
    ppermute x48, starting transfers between devices, step_ring(): lax.ppermute(value, 'fsdp', [(WALK[at], WALK[(at + by) % size]) for at in...  63.1 us
    dot_general x8, matrix products, weight_grad(): lax.dot_general(left, right, (((0, 1), (0, 1)), ((), ())), preferred_elem...  36 us
    ppermute x33, starting transfers between devices, permute(): return lax.ppermute(value, axis, [(at, at ^ mask) for at in range(size)])  24.8 us
    unnamed x209, local copies, waits for them, and re-layouts  14.6 us
  transfers between devices with their start and end apart: 82, of which 38 were waited for; matrix products, arithmetic and copies ran while one was open for 13% of the time, Pallas kernels for 31%

profile of v2, /device:TPU:0, one launch (start us, length us, event | category | flops | bytes accessed | tf_op | source)
XLA Modules:
  0.0 631.7 jit_solution(13777123338661721770)
XLA Ops:
  45.8 6.2 collective-permute-done.9
  57.8 6.6 %collective-permute-done.13.refs_19_.refs_14_ = bf16[96,768]{1,0:T(8,128)(2,1)S(1)} collective-permute-done((bf16[96,768]{1,0:T(8,128)(2,1)S(1)}, bf16[96,768]{1,0:T(8,128)(2,1)S(1)}, u32[]{:S(2)}, u32[]{:S(2)}) %collective-permute-start.13) | collective-permute-done | bytes 147488 | tf_op jit(solution)/shard_map/ppermute | solution.py:61
  82.8 23.9 %project_scan.2 = (bf16[4,256,1536]{2,1,0:T(8,128)(2,1)}, bf16[4,256,768]{2,1,0:T(8,128)(2,1)}, f32[4,256,256]{2,1,0:T(8,128)}, f32[4,16,256]{2,1,0:T(8,128)}, f...) custom-call(s32[9]{0:T(128)} %pad_add_fusion.t_ref, bf16[256,1536]{1,0:T(8,128)(2,1)} %refs_0_.1, ...), custom_call_target="tpu_custom_call" | custom-call | flops 10000000000 | bytes 17741824 | tf_op jit(solution)/shard_map/project_scan/pallas_call | solution.py:815
  109.0 6.1 collective-permute-done.23.refs_10_.refs_19_.refs_14_.refs_23_
  119.0 13.7 %gate_forward.2 = (bf16[4,256,768]{2,1,0:T(8,128)(2,1)}, bf16[2,256,1664]{2,1,0:T(8,128)(2,1)}, bf16[2,256,1664]{2,1,0:T(8,128)(2,1)}) custom-call(s32[9]{0:T(128)} %pad_add_fusion.t_ref, bf16[4,256,1536]{2,1,0:T(8,128)(2,1)} %get-tuple-element.234.refs_0_.refs_4_, f32[4,256,768]{2,1,0:T(8,128)} %get-tuple-element.239.refs_1_.refs_6_, ...), custom_call_target="tpu_custom_call" | custom-call | flops 6000000000 | bytes 20758528 | tf_op jit(solution)/shard_map/gate_forward/pallas_call | solution.py:815
  148.3 18.7 %collective-permute-done.28 = bf16[256,1664]{1,0:T(8,128)(2,1)} collective-permute-done((bf16[256,1664]{1,0:T(8,128)(2,1)}, bf16[256,1664]{1,0:T(8,128)(2,1)}, u32[]{:S(2)}, u32[]{:S(2)}) %collective-permute-start.28) | collective-permute-done | bytes 852000 | tf_op jit(solution)/shard_map/ppermute | solution.py:22
  175.2 18.1 %collective-permute-done.32.refs_2_ = bf16[256,1536]{1,0:T(8,128)(2,1)} collective-permute-done((bf16[256,1536]{1,0:T(8,128)(2,1)}, bf16[256,1536]{1,0:T(8,128)(2,1)}, u32[]{:S(2)}, u32[]{:S(2)}) %collective-permute-start.32) | collective-permute-done | bytes 786464 | tf_op jit(solution)/shard_map/ppermute | solution.py:22
  210.1 23.1 %project_scan.3 = (bf16[4,256,1536]{2,1,0:T(8,128)(2,1)}, bf16[4,256,768]{2,1,0:T(8,128)(2,1)}, f32[4,256,256]{2,1,0:T(8,128)}, f32[4,16,256]{2,1,0:T(8,128)}, f...) custom-call(s32[9]{0:T(128)} %pad_add_fusion.t_ref, bf16[256,1536]{1,0:T(8,128)(2,1)} %multiply_convert_fusion.refs_0_, ...), custom_call_target="tpu_custom_call" | custom-call | flops 10000000000 | bytes 22460416 | tf_op jit(solution)/shard_map/project_scan/pallas_call | solution.py:815
  234.2 18.8 %gate_forward.3 = (bf16[4,256,768]{2,1,0:T(8,128)(2,1)}, bf16[2,256,1536]{2,1,0:T(8,128)(2,1)}, bf16[2,256,1536]{2,1,0:T(8,128)(2,1)}, bf16[4,256,1536]{2,1,0:T(...) custom-call(s32[9]{0:T(128)} %pad_add_fusion.t_ref, ...), custom_call_target="tpu_custom_call" | custom-call | flops 6000000000 | bytes 33112064 | tf_op jit(solution)/shard_map/gate_forward/pallas_call | solution.py:815
  260.5 7.9 %gate_backward.2 = (bf16[4,256,768]{2,1,0:T(8,128)(2,1)}, bf16[4,256,768]{2,1,0:T(8,128)(2,1)}, bf16[4,256,768]{2,1,0:T(8,128)(2,1)}, f32[8,768]{1,0:T(8,128)}) custom-call(s32[9]{0:T(128)} %pad_add_fusion.t_ref, bf16[4,256,768]{2,1,0:T(8,128)(2,1)} %get-tuple-element.266.refs_0_, f32[4,256,768]{2,1,0:T(8,128)} %get-tuple-element.261.refs_1_.refs_6_, ...), custom_call_target="tpu_custom_call" | custom-call | flops 3000000000 | bytes 11116544 | tf_op jit(solution)/shard_map/gate_backward/pallas_call | solution.py:815
  281.9 12.5 %collective-permute-start.44 = (bf16[192,768]{1,0:T(8,128)(2,1)}, bf16[192,768]{1,0:T(8,128)(2,1)S(1)}, u32[]{:S(2)}, u32[]{:S(2)}) collective-permute-start(bf16[192,768]{1,0:T(8,128)(2,1)} %get-tuple-element.274), channel_id=1, source_target_pairs={{0,4},{8,0},{16,8},{24,16},{28,24},{20,28},{12,20},{4,12},{1,5},{9... | collective-permute-start | bytes 884744 | tf_op jit(solution)/shard_map/ppermute | solution.py:61
  296.2 16.0 %mix_backward.4 = (bf16[4,256,768]{2,1,0:T(8,128)(2,1)}, bf16[4,256,256]{2,1,0:T(8,128)(2,1)}, f32[4,16,256]{2,1,0:T(8,128)}, f32[8,768]{1,0:T(8,128)}, f32[8,25...) custom-call(s32[9]{0:T(128)} %pad_add_fusion.t_ref, ...), custom_call_target="tpu_custom_call" | custom-call | flops 4000000000 | bytes 14852096 | tf_op jit(solution)/shard_map/mix_backward/pallas_call | solution.py:815
  318.4 16.3 %mix_backward.5 = (bf16[4,256,768]{2,1,0:T(8,128)(2,1)}, bf16[4,256,256]{2,1,0:T(8,128)(2,1)}, f32[4,16,256]{2,1,0:T(8,128)}, f32[8,768]{1,0:T(8,128)}, f32[8,25...) custom-call(s32[9]{0:T(128)} %pad_add_fusion.t_ref, ...), custom_call_target="tpu_custom_call", output_to_operand_aliasing={{0}: (15, {}), {1}: (16, {}), {2}: (17, {})} | custom-call | flops 4000000000 | bytes 17530880 | tf_op jit(solution)/shard_map/mix_backward/pallas_call | solution.py:815
  334.8 15.1 %input_backward.2 = (bf16[2,256,1536]{2,1,0:T(8,128)(2,1)}, bf16[2,256,1536]{2,1,0:T(8,128)(2,1)}, f32[16,1536]{1,0:T(8,128)}, f32[1,1536]{1,0:T(1,128)}) custom-call(s32[9]{0:T(128)} %pad_add_fusion.t_ref, bf16[4,256,768]{2,1,0:T(8,128)(2,1)} %get-tuple-element.300.refs_0_, bf16[4,256,768]{2,1,0:T(8,128)(2,1)} %get-tuple-element.270.refs_1_, ...), custom_call_target="tpu_custom_call" | custom-call | flops 7000000000 | bytes 25466880 | tf_op jit(solution)/shard_map/input_backward/pallas_call | solution.py:815
  364.4 15.7 %collective-permute-done.49.refs_6_ = bf16[480,768]{1,0:T(8,128)(2,1)S(1)} collective-permute-done((bf16[480,768]{1,0:T(8,128)(2,1)}, bf16[480,768]{1,0:T(8,128)(2,1)S(1)}, u32[]{:S(2)}, u32[]{:S(2)}) %collective-permute-start.49) | collective-permute-done | bytes 737312 | tf_op jit(solution)/shard_map/ppermute | solution.py:61
  395.1 12.2 %collective-permute-done.57.refs_5_ = bf16[256,1664]{1,0:T(8,128)(2,1)S(1)} collective-permute-done((bf16[256,1664]{1,0:T(8,128)(2,1)S(1)}, bf16[256,1664]{1,0:T(8,128)(2,1)S(1)}, u32[]{:S(2)}, u32[]{:S(2)}) %collective-permute-start.57) | collective-permute-done | bytes 852000 | tf_op jit(solution)/shard_map/ppermute | solution.py:22
  407.2 6.2 collective-permute-done.53.refs_2_
  433.3 10.9 %gate_backward.3 = (bf16[4,256,768]{2,1,0:T(8,128)(2,1)}, bf16[4,256,768]{2,1,0:T(8,128)(2,1)}, bf16[4,256,768]{2,1,0:T(8,128)(2,1)}, f32[8,768]{1,0:T(8,128)}, bf16[4,256,1536]{2,1,0:T(8,128)(2,1)}) custom-call(s32[9]{0:T(128)} %pad_add_fusion.t_ref, bf16[4,256,768]{2,1,0:T(8,128)(2,1)} %get-tuple-element.314.refs_0_, ...), custom_call_target="tpu_custom_call" | custom-call | flops 3000000000 | bytes 20783104 | tf_op jit(solution)/shard_map/gate_backward/pallas_call | solution.py:815
  444.3 6.6 %bitcast_convert_fusion.1 = bf16[1536,768]{1,0:T(8,128)(2,1)} fusion(bf16[4,256,1536]{2,1,0:T(8,128)(2,1)} %get-tuple-element.234.refs_0_.refs_4_, bf16[4,256,768]{2,1,0:T(8,128)(2,1)} %get-tuple-element.330.refs_1_), kind=kOutput, calls=%fused_computation.1 | convolution fusion | flops 2417098752 | bytes 7077888 | tf_op jit(solution)/shard_map/dot_general | solution.py:1272
  460.1 15.9 %mix_backward.6 = (bf16[4,256,768]{2,1,0:T(8,128)(2,1)}, bf16[4,256,256]{2,1,0:T(8,128)(2,1)}, f32[4,16,256]{2,1,0:T(8,128)}, f32[8,768]{1,0:T(8,128)}, f32[8,25...) custom-call(s32[9]{0:T(128)} %pad_add_fusion.t_ref, ...), custom_call_target="tpu_custom_call" | custom-call | flops 4000000000 | bytes 14852096 | tf_op jit(solution)/shard_map/mix_backward/pallas_call | solution.py:815
  483.8 16.4 %mix_backward.7 = (bf16[4,256,768]{2,1,0:T(8,128)(2,1)}, bf16[4,256,256]{2,1,0:T(8,128)(2,1)}, f32[4,16,256]{2,1,0:T(8,128)}, f32[8,768]{1,0:T(8,128)}, f32[8,25...) custom-call(s32[9]{0:T(128)} %pad_add_fusion.t_ref, ...), custom_call_target="tpu_custom_call", output_to_operand_aliasing={{0}: (15, {}), {1}: (16, {}), {2}: (17, {})} | custom-call | flops 4000000000 | bytes 17530880 | tf_op jit(solution)/shard_map/mix_backward/pallas_call | solution.py:815
  512.7 14.7 %input_backward.3 = (bf16[2,256,1536]{2,1,0:T(8,128)(2,1)}, bf16[2,256,1536]{2,1,0:T(8,128)(2,1)}, f32[16,1536]{1,0:T(8,128)}, f32[1,1536]{1,0:T(1,128)}) custom-call(s32[9]{0:T(128)} %pad_add_fusion.t_ref, bf16[4,256,768]{2,1,0:T(8,128)(2,1)} %get-tuple-element.367.refs_0_, bf16[4,256,768]{2,1,0:T(8,128)(2,1)} %get-tuple-element.330.refs_1_, ...), custom_call_target="tpu_custom_call" | custom-call | flops 7000000000 | bytes 18388992 | tf_op jit(solution)/shard_map/input_backward/pallas_call | solution.py:815
  552.8 11.5 %collective-permute-done.71 = bf16[256,1536]{1,0:T(8,128)(2,1)S(1)} collective-permute-done((bf16[256,1536]{1,0:T(8,128)(2,1)}, bf16[256,1536]{1,0:T(8,128)(2,1)S(1)}, u32[]{:S(2)}, u32[]{:S(2)}) %collective-permute-start.71) | collective-permute-done | bytes 786464 | tf_op jit(solution)/shard_map/ppermute | solution.py:22
  564.3 6.4 %collective-permute-done.68.refs_2_ = bf16[576,768]{1,0:T(8,128)(2,1)S(1)} collective-permute-done((bf16[576,768]{1,0:T(8,128)(2,1)}, bf16[576,768]{1,0:T(8,128)(2,1)S(1)}, u32[]{:S(2)}, u32[]{:S(2)}) %collective-permute-start.68) | collective-permute-done | bytes 884768 | tf_op jit(solution)/shard_map/ppermute | solution.py:61
  (587 shorter events, 296.1 us)
Async XLA Ops:
  7.3 194.4 %all-gather.3.cloned.1.call-start = ((), (), s32[]{:S(2)}) async-start(), calls=%async_computation | async-start | bytes 1081344 | tf_op jit(solution)/shard_map/all_gather | solution.py:1108
  15.6 38.7 %collective-permute-start.18 = (bf16[256,1536]{1,0:T(8,128)(2,1)S(1)}, bf16[256,1536]{1,0:T(8,128)(2,1)}, u32[]{:S(2)}, u32[]{:S(2)}) collective-permute-start(bf16[256,1536]{1,0:T(8,128)(2,1)S(1)} %copy-done.1), channel_id=1, source_target_pairs={{0,2},{1,3},{2,0},{3,1},{4,6},{5,7},{6,4},{7,5},{8,10},{9,11},{10,... | collective-permute-start | bytes 2359304 | tf_op jit(solution)/shard_map/ppermute | solution.py:22
  43.7 21.2 %collective-permute-start.11 = (bf16[192,1536]{1,0:T(8,128)(2,1)S(1)}, bf16[192,1536]{1,0:T(8,128)(2,1)}, u32[]{:S(2)}, u32[]{:S(2)}) collective-permute-start(bf16[192,1536]{1,0:T(8,128)(2,1)S(1)} %pad_maximum_fusion.5.refs_3_.refs_12_.refs_7_.refs_16_), channel_id=1, source_target_pairs={{0,8},{8,16},{16,24},{24,28},{28,20},{20,12},{12,4},{4,0},{1,9},{9... | collective-permute-start | bytes 1769480 | tf_op jit(solution)/shard_map/ppermute | solution.py:61
  72.7 34.0 %collective-permute-start.20 = (bf16[256,1536]{1,0:T(8,128)(2,1)}, bf16[256,1536]{1,0:T(8,128)(2,1)S(1)}, u32[]{:S(2)}, u32[]{:S(2)}) collective-permute-start(bf16[256,1536]{1,0:T(8,128)(2,1)} %refs_3_.1), channel_id=1, source_target_pairs={{0,2},{1,3},{2,0},{3,1},{4,6},{5,7},{6,4},{7,5},{8,10},{9,11},{10,... | collective-permute-start | bytes 2359304 | tf_op jit(solution)/shard_map/ppermute | solution.py:22
  80.6 26.0 %collective-permute-start.21 = (bf16[192,1536]{1,0:T(8,128)(2,1)}, bf16[192,1536]{1,0:T(8,128)(2,1)S(1)}, u32[]{:S(2)}, u32[]{:S(2)}) collective-permute-start(bf16[192,1536]{1,0:T(8,128)(2,1)} %collective-permute-done.15.refs_6_.refs_15_.refs_10_.refs_19_), channel_id=1, source_target_pairs={{0,8},{8,16},{16,24},{24,28},{28,20},{20,12},{12,4},{4,0},{1,9},{9... | collective-permute-start | bytes 1769480 | tf_op jit(solution)/shard_map/ppermute | solution.py:61
  82.8 23.9 %collective-permute-start.22 = (bf16[192,1536]{1,0:T(8,128)(2,1)}, bf16[192,1536]{1,0:T(8,128)(2,1)S(1)}, u32[]{:S(2)}, u32[]{:S(2)}) collective-permute-start(bf16[192,1536]{1,0:T(8,128)(2,1)} %collective-permute-done.16.refs_7_.refs_16_.refs_11_.refs_20_), channel_id=1, source_target_pairs={{0,4},{8,0},{16,8},{24,16},{28,24},{20,28},{12,20},{4,12},{1,5},{9... | collective-permute-start | bytes 1769480 | tf_op jit(solution)/shard_map/ppermute | solution.py:61
  144.0 23.0 %collective-permute-start.29 = (bf16[192,2304]{1,0:T(8,128)(2,1)S(1)}, bf16[192,2304]{1,0:T(8,128)(2,1)S(1)}, u32[]{:S(2)}, u32[]{:S(2)}) collective-permute-start(bf16[192,2304]{1,0:T(8,128)(2,1)S(1)} %collective-permute-done.25.refs_13_.refs_8_.refs_17_), channel_id=1, source_target_pairs={{0,8},{8,16},{16,24},{24,28},{28,20},{20,12},{12,4},{4,0},{1,9},{9... | collective-permute-start | bytes 2654216 | tf_op jit(solution)/shard_map/ppermute | solution.py:61
  144.5 23.4 %collective-permute-start.30 = (bf16[192,2304]{1,0:T(8,128)(2,1)S(1)}, bf16[192,2304]{1,0:T(8,128)(2,1)}, u32[]{:S(2)}, u32[]{:S(2)}) collective-permute-start(bf16[192,2304]{1,0:T(8,128)(2,1)S(1)} %collective-permute-done.26.refs_14_.refs_9_.refs_18_), channel_id=1, source_target_pairs={{0,4},{8,0},{16,8},{24,16},{28,24},{20,28},{12,20},{4,12},{1,5},{9... | collective-permute-start | bytes 2654216 | tf_op jit(solution)/shard_map/ppermute | solution.py:61
  146.0 21.0 %collective-permute-start.28 = (bf16[256,1664]{1,0:T(8,128)(2,1)}, bf16[256,1664]{1,0:T(8,128)(2,1)}, u32[]{:S(2)}, u32[]{:S(2)}) collective-permute-start(bf16[256,1664]{1,0:T(8,128)(2,1)} %fusion.12), channel_id=1, source_target_pairs={{0,2},{1,3},{2,0},{3,1},{4,6},{5,7},{6,4},{7,5},{8,10},{9,11},{10,... | collective-permute-start | bytes 2555912 | tf_op jit(solution)/shard_map/ppermute | solution.py:22
  171.7 23.0 %collective-permute-start.33 = (bf16[192,2304]{1,0:T(8,128)(2,1)S(1)}, bf16[192,2304]{1,0:T(8,128)(2,1)S(1)}, u32[]{:S(2)}, u32[]{:S(2)}) collective-permute-start(bf16[192,2304]{1,0:T(8,128)(2,1)S(1)} %copy-done.17), channel_id=1, source_target_pairs={{0,8},{8,16},{16,24},{24,28},{28,20},{20,12},{12,4},{4,0},{1,9},{9... | collective-permute-start | bytes 2654216 | tf_op jit(solution)/shard_map/ppermute | solution.py:61
  172.2 23.4 %collective-permute-start.34 = (bf16[192,2304]{1,0:T(8,128)(2,1)}, bf16[192,2304]{1,0:T(8,128)(2,1)S(1)}, u32[]{:S(2)}, u32[]{:S(2)}) collective-permute-start(bf16[192,2304]{1,0:T(8,128)(2,1)} %collective-permute-done.30.refs_16_.refs_11_.refs_20_), channel_id=1, source_target_pairs={{0,4},{8,0},{16,8},{24,16},{28,24},{20,28},{12,20},{4,12},{1,5},{9... | collective-permute-start | bytes 2654216 | tf_op jit(solution)/shard_map/ppermute | solution.py:61
  175.2 32.5 %collective-permute-start.31 = (bf16[256,1536]{1,0:T(8,128)(2,1)}, bf16[256,1536]{1,0:T(8,128)(2,1)}, u32[]{:S(2)}, u32[]{:S(2)}) collective-permute-start(bf16[256,1536]{1,0:T(8,128)(2,1)} %multiply_convert_fusion.refs_0_), channel_id=1, source_target_pairs={{0,1},{1,0},{2,3},{3,2},{4,5},{5,4},{6,7},{7,6},{8,9},{9,8},{10,11... | collective-permute-start | bytes 2359304 | tf_op jit(solution)/shard_map/ppermute | solution.py:22
  199.3 33.9 %collective-permute-start.38 = (bf16[256,1536]{1,0:T(8,128)(2,1)}, bf16[256,1536]{1,0:T(8,128)(2,1)}, u32[]{:S(2)}, u32[]{:S(2)}) collective-permute-start(bf16[256,1536]{1,0:T(8,128)(2,1)} %refs_3_.1), channel_id=1, source_target_pairs={{0,1},{1,0},{2,3},{3,2},{4,5},{5,4},{6,7},{7,6},{8,9},{9,8},{10,11... | collective-permute-start | bytes 2359304 | tf_op jit(solution)/shard_map/ppermute | solution.py:22
  207.8 25.5 %collective-permute-start.39 = (bf16[256,1536]{1,0:T(8,128)(2,1)}, bf16[256,1536]{1,0:T(8,128)(2,1)S(1)}, u32[]{:S(2)}, u32[]{:S(2)}) collective-permute-start(bf16[256,1536]{1,0:T(8,128)(2,1)} %copy-done.35), channel_id=1, source_target_pairs={{0,1},{1,0},{2,3},{3,2},{4,5},{5,4},{6,7},{7,6},{8,9},{9,8},{10,11... | collective-permute-start | bytes 2359304 | tf_op jit(solution)/shard_map/ppermute | solution.py:22
  256.7 37.7 %collective-permute-start.40 = (bf16[2,256,1536]{2,1,0:T(8,128)(2,1)}, bf16[2,256,1536]{2,1,0:T(8,128)(2,1)S(1)}, u32[]{:S(2)}, u32[]{:S(2)}) collective-permute-start(bf16[2,256,1536]{2,1,0:T(8,128)(2,1)} %get-tuple-element.264), channel_id=1, source_target_pairs={{0,1},{1,0},{2,3},{3,2},{4,5},{5,4},{6,7},{7,6},{8,9},{9,8},{10,11... | collective-permute-start | bytes 4718600 | tf_op jit(solution)/shard_map/ppermute | solution.py:22
  280.9 31.3 %collective-permute-start.43 = (bf16[192,768]{1,0:T(8,128)(2,1)}, bf16[192,768]{1,0:T(8,128)(2,1)S(1)}, u32[]{:S(2)}, u32[]{:S(2)}) collective-permute-start(bf16[192,768]{1,0:T(8,128)(2,1)} %get-tuple-element.273), channel_id=1, source_target_pairs={{0,8},{8,16},{16,24},{24,28},{28,20},{20,12},{12,4},{4,0},{1,9},{9... | collective-permute-start | bytes 884744 | tf_op jit(solution)/shard_map/ppermute | solution.py:61
  281.9 30.3 %collective-permute-start.44 = (bf16[192,768]{1,0:T(8,128)(2,1)}, bf16[192,768]{1,0:T(8,128)(2,1)S(1)}, u32[]{:S(2)}, u32[]{:S(2)}) collective-permute-start(bf16[192,768]{1,0:T(8,128)(2,1)} %get-tuple-element.274), channel_id=1, source_target_pairs={{0,4},{8,0},{16,8},{24,16},{28,24},{20,28},{12,20},{4,12},{1,5},{9... | collective-permute-start | bytes 884744 | tf_op jit(solution)/shard_map/ppermute | solution.py:61
  294.6 40.1 %collective-permute-start.47 = (bf16[256,1536]{1,0:T(8,128)(2,1)S(1)}, bf16[256,1536]{1,0:T(8,128)(2,1)S(1)}, u32[]{:S(2)}, u32[]{:S(2)}) collective-permute-start(bf16[256,1536]{1,0:T(8,128)(2,1)S(1)} %fusion.14), channel_id=1, source_target_pairs={{0,2},{1,3},{2,0},{3,1},{4,6},{5,7},{6,4},{7,5},{8,10},{9,11},{10,... | collective-permute-start | bytes 2359304 | tf_op jit(solution)/shard_map/ppermute | solution.py:22
  357.1 23.9 %collective-permute-start.51 = (bf16[256,1536]{1,0:T(8,128)(2,1)}, bf16[256,1536]{1,0:T(8,128)(2,1)S(1)}, u32[]{:S(2)}, u32[]{:S(2)}) collective-permute-start(bf16[256,1536]{1,0:T(8,128)(2,1)} %fusion.15), channel_id=1, source_target_pairs={{0,2},{1,3},{2,0},{3,1},{4,6},{5,7},{6,4},{7,5},{8,10},{9,11},{10,... | collective-permute-start | bytes 2359304 | tf_op jit(solution)/shard_map/ppermute | solution.py:22
  395.1 36.5 %collective-permute-start.52 = (bf16[256,1664]{1,0:T(8,128)(2,1)S(1)}, bf16[256,1664]{1,0:T(8,128)(2,1)S(1)}, u32[]{:S(2)}, u32[]{:S(2)}) collective-permute-start(bf16[256,1664]{1,0:T(8,128)(2,1)S(1)} %fusion.11.refs_3_), channel_id=1, source_target_pairs={{0,1},{1,0},{2,3},{3,2},{4,5},{5,4},{6,7},{7,6},{8,9},{9,8},{10,11... | collective-permute-start | bytes 2555912 | tf_op jit(solution)/shard_map/ppermute | solution.py:22
  407.2 24.3 %collective-permute-start.58 = (bf16[256,1664]{1,0:T(8,128)(2,1)S(1)}, bf16[256,1664]{1,0:T(8,128)(2,1)S(1)}, u32[]{:S(2)}, u32[]{:S(2)}) collective-permute-start(bf16[256,1664]{1,0:T(8,128)(2,1)S(1)} %collective-permute-done.57.refs_5_), channel_id=1, source_target_pairs={{0,1},{1,0},{2,3},{3,2},{4,5},{5,4},{6,7},{7,6},{8,9},{9,8},{10,11... | collective-permute-start | bytes 2555912 | tf_op jit(solution)/shard_map/ppermute | solution.py:22
  429.5 21.4 %collective-permute-start.59 = (bf16[192,768]{1,0:T(8,128)(2,1)}, bf16[192,768]{1,0:T(8,128)(2,1)S(1)}, u32[]{:S(2)}, u32[]{:S(2)}) collective-permute-start(bf16[192,768]{1,0:T(8,128)(2,1)} %get-tuple-element.333), channel_id=1, source_target_pairs={{0,8},{8,16},{16,24},{24,28},{28,20},{20,12},{12,4},{4,0},{1,9},{9... | collective-permute-start | bytes 884744 | tf_op jit(solution)/shard_map/ppermute | solution.py:61
  548.7 22.0 %collective-permute-start.68 = (bf16[576,768]{1,0:T(8,128)(2,1)}, bf16[576,768]{1,0:T(8,128)(2,1)S(1)}, u32[]{:S(2)}, u32[]{:S(2)}) collective-permute-start(bf16[576,768]{1,0:T(8,128)(2,1)} %get-tuple-element.382), channel_id=1, source_target_pairs={{0,8},{8,16},{16,24},{24,28},{28,20},{20,12},{12,4},{4,0},{1,9},{9... | collective-permute-start | bytes 2654216 | tf_op jit(solution)/shard_map/ppermute | solution.py:61
  550.3 21.8 %collective-permute-start.69 = (bf16[576,768]{1,0:T(8,128)(2,1)}, bf16[576,768]{1,0:T(8,128)(2,1)}, u32[]{:S(2)}, u32[]{:S(2)}) collective-permute-start(bf16[576,768]{1,0:T(8,128)(2,1)} %get-tuple-element.383), channel_id=1, source_target_pairs={{0,4},{8,0},{16,8},{24,16},{28,24},{20,28},{12,20},{4,12},{1,5},{9... | collective-permute-start | bytes 2654216 | tf_op jit(solution)/shard_map/ppermute | solution.py:61
  (158 other events, 1602.8 us)
Sparse Core Ops, SparseCore 0:
  148.3 53.3 all-gather.2

commit v3 on v2

--- a/solution.py
+++ b/solution.py
@@ -72,23 +72,23 @@
     return step_ring(behind[:half], 1), step_ring(ahead[half:], -1)
 
 
-def walk_weight(own, steps):
+def walk_weight(own, steps, lack=0):
     arrays = [own]
     rows = own.shape[0]
-    meta = [(0, 0, rows, 0, 0, True)]
+    meta = [(0, 0, rows, 0, 0, True, 0)]
     for at, (behind, ahead) in enumerate(steps):
         arrays += [behind, ahead]
         if at < 3:
-            meta.append((len(arrays) - 2, 0, rows, 7 - at, 0, True))
-            meta.append((len(arrays) - 1, 0, rows, 1 + at, 0, True))
+            meta.append((len(arrays) - 2, 0, rows, 7 - at, 0, True, 0))
+            meta.append((len(arrays) - 1, 0, rows, 1 + at, 0, True, 0))
         else:
-            meta.append((len(arrays) - 2, 0, rows // 2, 4, 0, True))
-            meta.append((len(arrays) - 1, 0, rows // 2, 4, rows // 2, True))
+            meta.append((len(arrays) - 2, 0, rows // 2, 4, 0, True, lack))
+            meta.append((len(arrays) - 1, 0, rows // 2, 4, rows // 2, True, lack))
     return arrays, tuple(meta)
 
 
 def natural_weight(array, count, deep, stride):
-    return [array], tuple((0, at * stride, deep, at, 0, False) for at in range(count))
+    return [array], tuple((0, at * stride, deep, at, 0, False, 0) for at in range(count))
 
 
 def after(value, *earlier):
@@ -240,16 +240,20 @@
 def ring_final(firsts, which, t_ref, *refs):
     del t_ref
     count = len(firsts)
-    terms, outs = refs[:count], refs[-count:]
-    arrived = refs[count:-count]
+    terms, (zx_ref, out_ref) = refs[:count], refs[-2:]
+    arrived = refs[count:-2]
+    deep = out_ref.shape[1]
     for at in range(count):
-        deep = outs[at].shape[0]
         span = pl.ds(firsts[at], deep)
-        outs[at][...] = (
+        total = (
             terms[at][0].astype(F32)
             + arrived[2 * which[at]][span, :].astype(F32)
             + arrived[2 * which[at] + 1][span, :].astype(F32)
         )
+        if at % 3 == 0:
+            out_ref[at // 3] = total
+        else:
+            zx_ref[at // 3, :, at % 3 - 1, :] = total
 
 
 def term_spec(terms, slot):
@@ -316,16 +320,23 @@
 
 
 def ring_results(rings):
+    layers = len(rings) // 3
+    deep, width = rings[0].terms.shape[1:]
     if not is_walk():
-        return [
+        sums = [
             lax.psum_scatter(ring.terms, "fsdp", scatter_dimension=0, tiled=False).astype(F32)
             for ring in rings
         ]
+        zx = [jnp.stack(sums[3 * k + 1 : 3 * k + 3], 1) for k in range(layers)]
+        return jnp.stack(zx), jnp.stack(sums[::3])
     arrived, which = arrivals(rings)
     ins = [ring.terms for ring in rings] + arrived
     in_specs = [term_spec(ring.terms, 0) for ring in rings]
     in_specs += [whole_spec(item.shape) for item in arrived]
-    outs = [jax.ShapeDtypeStruct(ring.terms.shape[1:], F32) for ring in rings]
+    outs = [
+        jax.ShapeDtypeStruct((layers, deep, 2, width), F32),
+        jax.ShapeDtypeStruct((layers, deep, width), F32),
+    ]
     out_specs = [whole_spec(item.shape) for item in outs]
     body = partial(ring_final, tuple(ring.first for ring in rings), which)
     return call(body, rings[0].table, 1, ins, in_specs, outs, out_specs, [], 10**6, "ring_final")
@@ -396,20 +407,30 @@
     return lane < 64, lane >= 64
 
 
-def start_weight(arrays, meta, column, width, deep, table, goal, sems):
+def weight_copies(arrays, meta, column, width, deep, table, goal, sems):
     copies = []
-    for at, (array, source, rows, slot, first, by_walk) in enumerate(meta):
+    for at, (array, source, rows, slot, first, by_walk, lack) in enumerate(meta):
         row = slot * deep + first
         if by_walk:
             row = pl.multiple_of(table[1 + slot] * deep + first, 32)
         copy = pltpu.make_async_copy(
-            arrays[array].at[pl.ds(source, rows), pl.ds(column * width, width)],
+            arrays[array].at[pl.ds(source, rows), pl.ds(column * width - lack, width)],
             goal.at[pl.ds(row, rows)],
             sems.at[at],
         )
-        copy.start()
         copies.append(copy)
     return copies
+
+
+def start_weight(*where):
+    copies = weight_copies(*where)
+    for copy in copies:
+        copy.start()
+    return copies
+
+
+def wait_weight(*where):
+    wait_all(weight_copies(*where))
 
 
 def wait_all(copies):
@@ -593,8 +614,8 @@
 
     @pl.when(step == 0)
     def _():
-        copies = start_weight(x_parts, meta_x, cols_xz[0], width, deep, t_ref, wx, sem_x)
-        copies += start_weight(z_parts, meta_z, cols_xz[1], width, deep, t_ref, wz, sem_z)
+        copies = start_weight(z_parts, meta_z, cols_xz[1], width, deep, t_ref, wz, sem_z)
+        start_weight(x_parts, meta_x, cols_xz[0], width, deep, t_ref, wx, sem_x)
         wait_all(copies)
         gdt_ref[...] = jnp.zeros_like(gdt_ref)
         gn_ref[...] = jnp.zeros_like(gn_ref)
@@ -602,7 +623,13 @@
     normed = rows_ref[0]
     du = du_ref[0]
     gdt_ref[...] += dot(du.astype(BF16), normed)
-    total = dot_t(dz_ref[0], wz[...]) + dot_t(dx_ref[0], wx[...]) + dot_t(dbc_ref[0], wbc_ref[...])
+    total = dot_t(dz_ref[0], wz[...]) + dot_t(dbc_ref[0], wbc_ref[...])
+
+    @pl.when(step == 0)
+    def _():
+        wait_weight(x_parts, meta_x, cols_xz[0], width, deep, t_ref, wx, sem_x)
+
+    total = total + dot_t(dx_ref[0], wx[...])
     du_cols = jnp.concatenate([du, jnp.zeros((128 - du.shape[0], du.shape[1]), F32)], 0).T
     total = total + dot(du_cols.astype(BF16), wdt_ref[...])
     gn_ref[...] += jnp.sum(total * normed.astype(F32), 0, keepdims=True)
@@ -706,10 +733,15 @@
     @pl.when(step == 0)
     def _():
         copies = start_weight(z_parts, meta_z, cols_zo[0], width, deep, t_ref, wz, sem_z)
-        copies += start_weight(o_parts, meta_o, cols_zo[1], width, deep, t_ref, wo, sem_o)
+        start_weight(o_parts, meta_o, cols_zo[1], width, deep, t_ref, wo, sem_o)
         wait_all(copies)
 
     z = dot(rows_ref[0], wz[...]).astype(BF16)
+
+    @pl.when(step == 0)
+    def _():
+        wait_weight(o_parts, meta_o, cols_zo[1], width, deep, t_ref, wo, sem_o)
+
     z_ref[0] = z
     z = z.astype(F32)
     v = y_ref[0] * (z * jax.nn.sigmoid(z))
@@ -1162,6 +1194,7 @@
         bias_bc = tiny[:, :, shared * taps : shared * (taps + 1)].reshape(1, wide).astype(F32)
         bc_params.append(jnp.pad(jnp.concatenate([taps_bc.T, bias_bc], 0), ((0, 3), (0, 0))))
 
+    unpack(0)
     running = hidden.astype(F32)
     saved = []
     for k in range(layers):
@@ -1172,10 +1205,16 @@
             if walk:
                 ring_all.step(normed)
                 over, *ring_all.steps[2] = lax.optimization_barrier((over,) + tuple(ring_all.steps[2]))
-                ring_all.step()
+                behind, ahead = ring_all.steps[2]
+                last_x = ring_last(behind[:, :width], ahead[:, :width])
+                last_zo = ring_last(behind[:, width:], ahead[:, width:])
             slots = [normed, beside, over, permute(over, "tp", 1)]
-        unpack(k)
-        w_x = ring_x.weight() if k == 0 else ring_all.weight()
+        if k == 0:
+            w_x = ring_x.weight()
+        elif walk:
+            w_x = walk_weight(ring_all.own, ring_all.steps[:3] + [last_x])
+        else:
+            w_x = ring_all.weight()
         rows, x, bc, u, y, state = run_project(
             k, table, slots, gains[k], w_bc[k], w_dt[k], lines_of, params, bc_params[k], spread, w_x, 0, k == 0
         )
@@ -1186,6 +1225,9 @@
             w_zo, cols_zo = ring_zo.weight(), (0, 1)
         else:
             w_zo, cols_zo = w_x, (1, 2)
+            if walk:
+                y, *last_zo = lax.optimization_barrier((y,) + tuple(last_zo))
+                w_zo = walk_weight(ring_all.own, ring_all.steps[:3] + [tuple(last_zo)], width)
         weights.append((w_x, w_zo, cols_zo))
         entry = dict(rows=rows, x=x, bc=bc, u=u, y=y, state=state, h=running)
         is_last = k == layers - 1
@@ -1196,13 +1238,17 @@
             k, table, rows, y, chan, cots_last if is_last else None, w_zo, w_zo, cols_zo
         )
         if not is_last and walk:
-            send, z, *next_ring.steps[0] = lax.optimization_barrier((send, z) + tuple(next_ring.steps[0]))
+            send, z, packs[k + 1], *next_ring.steps[0] = lax.optimization_barrier(
+                (send, z, packs[k + 1]) + tuple(next_ring.steps[0])
+            )
         entry["z"] = z
         entry["near"] = near = permute(send, "tp", 1)
         if not is_last:
             ring_all = next_ring
             going = plus(keep[1], near[1])
             far = permute(going, "tp", 2)
+            unpack(k + 1)
+            far = after(far, w_bc[k + 1], w_dt[k + 1], bc_params[k + 1])
             if walk:
                 ring_all.step(going)
                 far, *ring_all.steps[1] = lax.optimization_barrier((far,) + tuple(ring_all.steps[1]))
@@ -1253,15 +1299,13 @@
             extra = three_parts(item["scale"]) + three_parts(cross)
             extra = jnp.concatenate(extra, 1).astype(BF16)
             low = jnp.concatenate([low, jnp.pad(extra, ((0, 0), (0, 128 - 6)))], 1)
-            cots = tp_gather(low)
+            over, beside = permute(low, "tp", 2), permute(low, "tp", 1)
             if walk:
-                later_rings = sums_of[k + 1]
-                (low_now,) = ring_pin(later_rings, low)
-                sums_of[k + 1] = later_rings[:2] + (ring_results(later_rings[:2]), later_rings[2])
-                last_x = later_rings[2]
-                ring_step([last_x], low_now)
-                (cots[2],) = ring_pin([last_x], cots[2])
-                ring_step([last_x])
+                last_x = sums_of[k + 1][2]
+                over = after(over, *ring_step(sums_of[k + 1], low))
+                (over,) = ring_pin(sums_of[k + 1], over)
+                ring_step([last_x], over)
+            cots = [low, beside, over, permute(over, "tp", 1)]
             dy, dz, gated, g_gain, cot = run_gate_backward(
                 k, table, z, y, chan, None, cots, w_zo, cols_zo[1], inner
             )
@@ -1277,10 +1321,11 @@
         ring_o = RingSum(weight_grad(cot, gated).reshape(count, deep, width), table)
         ring_z = RingSum(weight_grad(rows, dz).reshape(count, deep, width), table)
         early = [ring_o, ring_z]
-        dy = after(dy, *ring_step(early, dy), ring_o.terms, ring_z.terms)
+        rounds = early + ([last_x] if k < layers - 1 and walk else [])
+        dy = after(dy, *ring_step(rounds, dy), ring_o.terms, ring_z.terms)
         if k == layers - 1:
             dy = after(dy, saved[k]["near"])
-        splits = (tp_count // 2, tp_count - tp_count // 2)
+        splits = (tp_count,) if k else (tp_count // 2, tp_count - tp_count // 2)
         done, top = None, tp_count - 1
         for steps in splits:
             done = run_mix_backward(
@@ -1290,10 +1335,10 @@
             top -= steps
             if top >= 0:
                 done = list(done)
-                (done[6],) = ring_pin(early, done[6])
-                done[6] = after(done[6], *ring_step(early))
+                (done[6],) = ring_pin(rounds, done[6])
+                done[6] = after(done[6], *ring_step(rounds))
         dx, dbc, du, gx, gbc, gh = done[:6]
-        (dx,) = ring_pin(early, dx)
+        (dx,) = ring_pin(rounds, dx)
         if k == layers - 1:
             dx, far = lax.optimization_barrier((dx, item["far"]))
             scale = lax.rsqrt(item["sums"][0, 0] / inner + EPS)[:, None]
@@ -1305,41 +1350,38 @@
             sent = ring_step(every)
             dx_now = after(dx, *sent) if walk else dx
         else:
-            dx_now = dx
+            sent = ring_step(every)
+            dx_now = after(dx, *sent) if walk else dx
         send, keep, g_dt, g_norm = run_input_backward(
             table, dx_now, dz, dbc, du, rows, w_bc[k], w_dt[k], w_x, w_zo, (0, cols_zo[0])
         )
-        parts[k] = [weight_grad(rows, dbc), g_norm, gbc, g_dt, gx]
+        parts[k] = [weight_grad(rows, dbc) if k else None, g_norm, gbc, g_dt, gx]
         if k == 0:
             (send,) = ring_pin(every, send)
             near = permute(send, "tp", 1)
-            small = small_sum(parts)
-            near, small.terms = lax.optimization_barrier((near, small.terms))
             going = plus(keep[1], near[1])
             far = permute(going, "tp", 2)
             ring_step(every, going)
+            (far,) = ring_pin(every, far)
+            ring_step([ring_x], far)
+            parts[k][0] = weight_grad(rows, after(dbc, far))
+            small = small_sum(parts)
             got = small.over_core()
-            got, far = ring_pin(every, got, far)
-            ring_step([ring_x], far)
-            got = small.over_y(got)
             (got,) = ring_pin([ring_x], got)
-            ring_step([ring_x])
-            got = small.over_x(got)
+            last_sent = ring_step([ring_x])
             if walk:
-                (got,) = ring_pin([ring_x], got)
-            got = small.over_z(got)
+                got = after(got, *last_sent)
+                far = after(far, *last_sent)
+            got = small.over_z(small.over_x(small.over_y(got)))
         else:
+            (send,) = ring_pin(every, send)
             near = permute(send, "tp", 1)
-            ring_x = RingSum(weight_grad(rows, dx).reshape(count, deep, width), table)
-            every.append(ring_x)
-            going, ring_x.terms = lax.optimization_barrier((plus(keep[1], near[1]), ring_x.terms))
+            going = plus(keep[1], near[1])
             far = permute(going, "tp", 2)
             ring_step(every, going)
-            (far,) = ring_pin(every, far)
-            ring_step(every, far)
+            ring_x = RingSum(weight_grad(rows, after(dx, going)).reshape(count, deep, width), table)
+            far, ring_x.terms, parts[k][0] = ring_pin(every, far, ring_x.terms, parts[k][0])
         sums_of[k] = (ring_o, ring_z, ring_x)
-        if k == 0 or not walk:
-            sums_of[k] = (ring_o, ring_z, ring_results([ring_o, ring_z]), ring_x)
         d_normed = keep[0].astype(F32) + near[0].astype(F32) + far.astype(F32)
         h = item["h"]
         inv = norm_scale_of(h)
@@ -1356,16 +1398,12 @@
     vector = vector.reshape(layers, 8, width)
     tiny = d_pack[:, bc_deep]
     conv = tiny[:, bc_deep : bc_deep + (taps + 1) * shared].reshape(layers, taps + 1, shared)
-    zx, out = [], []
-    for k in range(layers):
-        _, _, (sum_o, sum_z), last_x = sums_of[k]
-        zx.append(jnp.stack([sum_z, ring_results([last_x])[0]], 1))
-        out.append(sum_o)
+    zx, out = ring_results([ring for rings in sums_of for ring in rings])
     return (
         running,
         grad_run,
         tiny[:, :bc_deep],
-        jnp.stack(zx),
+        zx,
         d_dt.reshape(layers, heads, deep).swapaxes(1, 2),
         d_pack[:, :bc_deep],
         vector[:, :taps].swapaxes(1, 2),
@@ -1376,7 +1414,7 @@
         vector[:, 7, HEAD_ROWS : HEAD_ROWS + heads],
         jnp.sum(vector[:, 5].reshape(layers, heads, -1), 2),
         vector[:, 6],
-        jnp.stack(out),
+        out,
     )
 
 

time: 636 us -> 608 us (0.956); the launches traced: 632 us -> 597 us
  waiting for transfers between devices: 163 us -> 139 us
  Pallas kernels: 246 us -> 234 us
  local copies, waits for them, and re-layouts: 40.7 us -> 52.5 us
  starting transfers between devices: 88 us -> 77.2 us
    ppermute x48, waiting for transfers between devices: 78.3 us -> 66 us  [step_ring(): lax.ppermute(value, 'fsdp', [(WALK[at], WALK[(at + by) % size]) for at in...]
    ppermute x48, starting transfers between devices: 63.1 us -> 51.3 us  [step_ring(): lax.ppermute(value, 'fsdp', [(WALK[at], WALK[(at + by) % size]) for at in...]
    pallas_call x28 -> x23, Pallas kernels: 246 us -> 234 us  [call(): pl.pallas_call(body, grid_spec=pltpu.PrefetchScalarGridSpec(num_scalar_pr...]
    ppermute x33, waiting for transfers between devices: 82.6 us -> 72.9 us  [permute(): return lax.ppermute(value, axis, [(at, at ^ mask) for at in range(size)])]
    unnamed x209 -> x202, local copies, waits for them, and re-layouts: 14.6 us -> 14.5 us
  transfers between devices with their start and end apart: 82 -> 82, of which waited for: 38 -> 39; matrix products, arithmetic and copies ran while one was open for 13% -> 13% of each run, Pallas kernels for 31% -> 34%
where the time goes in v3:
time: 608 us; the launch traced here: 597 us
  Pallas kernels  234 us (38%)
  waiting for transfers between devices  139 us (23%)
  starting transfers between devices  77.2 us (13%)
  local copies, waits for them, and re-layouts  52.5 us (9%)
  other arithmetic  40 us (7%)
  matrix products  38.2 us (6%)
  between operations  16 us (3%)
    pallas_call x23, Pallas kernels, call(): pl.pallas_call(body, grid_spec=pltpu.PrefetchScalarGridSpec(num_scalar_pr...  234 us
    ppermute x33, waiting for transfers between devices, permute(): return lax.ppermute(value, axis, [(at, at ^ mask) for at in range(size)])  72.9 us
    ppermute x48, waiting for transfers between devices, step_ring(): lax.ppermute(value, 'fsdp', [(WALK[at], WALK[(at + by) % size]) for at in...  66 us
    ppermute x48, starting transfers between devices, step_ring(): lax.ppermute(value, 'fsdp', [(WALK[at], WALK[(at + by) % size]) for at in...  51.3 us
    dot_general x8, matrix products, weight_grad(): lax.dot_general(left, right, (((0, 1), (0, 1)), ((), ())), preferred_elem...  38.2 us
    ppermute x33, starting transfers between devices, permute(): return lax.ppermute(value, axis, [(at, at ^ mask) for at in range(size)])  25.8 us
    unnamed x202, local copies, waits for them, and re-layouts  14.5 us
  transfers between devices with their start and end apart: 82, of which 39 were waited for; matrix products, arithmetic and copies ran while one was open for 13% of the time, Pallas kernels for 34%

profile of v3, /device:TPU:0, one launch (start us, length us, event | category | flops | bytes accessed | tf_op | source)
XLA Modules:
  0.0 597.2 jit_solution(15961493025684103400)
XLA Ops:
  46.4 6.0 collective-permute-done.9
  58.3 9.5 %collective-permute-done.13.refs_19_.refs_14_ = bf16[96,768]{1,0:T(8,128)(2,1)S(1)} collective-permute-done((bf16[96,768]{1,0:T(8,128)(2,1)S(1)}, bf16[96,768]{1,0:T(8,128)(2,1)S(1)}, u32[]{:S(2)}, u32[]{:S(2)}) %collective-permute-start.13) | collective-permute-done | bytes 147488 | tf_op jit(solution)/shard_map/ppermute | solution.py:61
  86.1 23.8 %project_scan.2 = (bf16[4,256,1536]{2,1,0:T(8,128)(2,1)}, bf16[4,256,768]{2,1,0:T(8,128)(2,1)}, f32[4,256,256]{2,1,0:T(8,128)}, f32[4,16,256]{2,1,0:T(8,128)}, f...) custom-call(s32[9]{0:T(128)} %pad_add_fusion.t_ref, bf16[256,1536]{1,0:T(8,128)(2,1)} %refs_0_.1, ...), custom_call_target="tpu_custom_call" | custom-call | flops 10000000000 | bytes 17741824 | tf_op jit(solution)/shard_map/project_scan/pallas_call | solution.py:847
  112.2 5.8 collective-permute-done.23.refs_10_.refs_19_.refs_14_.refs_23_
  121.9 14.7 %gate_forward.2 = (bf16[4,256,768]{2,1,0:T(8,128)(2,1)}, bf16[2,256,1664]{2,1,0:T(8,128)(2,1)}, bf16[2,256,1664]{2,1,0:T(8,128)(2,1)}) custom-call(s32[9]{0:T(128)} %pad_add_fusion.t_ref, bf16[4,256,1536]{2,1,0:T(8,128)(2,1)} %get-tuple-element.226.refs_0_.refs_4_, f32[4,256,768]{2,1,0:T(8,128)} %get-tuple-element.231.refs_1_.refs_6_, ...), custom_call_target="tpu_custom_call" | custom-call | flops 6000000000 | bytes 20758528 | tf_op jit(solution)/shard_map/gate_forward/pallas_call | solution.py:847
  178.1 16.4 %collective-permute-done.32.refs_2_ = bf16[256,1536]{1,0:T(8,128)(2,1)} collective-permute-done((bf16[256,1536]{1,0:T(8,128)(2,1)}, bf16[256,1536]{1,0:T(8,128)(2,1)}, u32[]{:S(2)}, u32[]{:S(2)}) %collective-permute-start.32) | collective-permute-done | bytes 786464 | tf_op jit(solution)/shard_map/ppermute | solution.py:22
  204.6 23.1 %project_scan.3 = (bf16[4,256,1536]{2,1,0:T(8,128)(2,1)}, bf16[4,256,768]{2,1,0:T(8,128)(2,1)}, f32[4,256,256]{2,1,0:T(8,128)}, f32[4,16,256]{2,1,0:T(8,128)}, f...) custom-call(s32[9]{0:T(128)} %pad_add_fusion.t_ref, bf16[256,1536]{1,0:T(8,128)(2,1)} %multiply_convert_fusion.refs_0_, ...), custom_call_target="tpu_custom_call" | custom-call | flops 10000000000 | bytes 21870592 | tf_op jit(solution)/shard_map/project_scan/pallas_call | solution.py:847
  228.8 19.2 %gate_forward.3 = (bf16[4,256,768]{2,1,0:T(8,128)(2,1)}, bf16[2,256,1536]{2,1,0:T(8,128)(2,1)}, bf16[2,256,1536]{2,1,0:T(8,128)(2,1)}, bf16[4,256,1536]{2,1,0:T(...) custom-call(s32[9]{0:T(128)} %pad_add_fusion.t_ref, ...), custom_call_target="tpu_custom_call" | custom-call | flops 6000000000 | bytes 32522240 | tf_op jit(solution)/shard_map/gate_forward/pallas_call | solution.py:847
  255.6 8.0 %gate_backward.2 = (bf16[4,256,768]{2,1,0:T(8,128)(2,1)}, bf16[4,256,768]{2,1,0:T(8,128)(2,1)}, bf16[4,256,768]{2,1,0:T(8,128)(2,1)}, f32[8,768]{1,0:T(8,128)}) custom-call(s32[9]{0:T(128)} %pad_add_fusion.t_ref, bf16[4,256,768]{2,1,0:T(8,128)(2,1)} %get-tuple-element.262.refs_0_, f32[4,256,768]{2,1,0:T(8,128)} %get-tuple-element.256.refs_1_.refs_6_, ...), custom_call_target="tpu_custom_call" | custom-call | flops 3000000000 | bytes 11116544 | tf_op jit(solution)/shard_map/gate_backward/pallas_call | solution.py:847
  281.0 28.8 %mix_backward.3 = (bf16[4,256,768]{2,1,0:T(8,128)(2,1)}, bf16[4,256,256]{2,1,0:T(8,128)(2,1)}, f32[4,16,256]{2,1,0:T(8,128)}, f32[8,768]{1,0:T(8,128)}, f32[8,25...) custom-call(s32[9]{0:T(128)} %pad_add_fusion.t_ref, ...), custom_call_target="tpu_custom_call" | custom-call | flops 8000000000 | bytes 14852096 | tf_op jit(solution)/shard_map/mix_backward/pallas_call | solution.py:847
  315.9 15.0 %input_backward.2 = (bf16[2,256,1536]{2,1,0:T(8,128)(2,1)}, bf16[2,256,1536]{2,1,0:T(8,128)(2,1)}, f32[16,1536]{1,0:T(8,128)}, f32[1,1536]{1,0:T(1,128)}) custom-call(s32[9]{0:T(128)} %pad_add_fusion.t_ref, bf16[4,256,768]{2,1,0:T(8,128)(2,1)} %get-tuple-element.299.refs_0_, bf16[4,256,768]{2,1,0:T(8,128)(2,1)} %get-tuple-element.269.refs_1_, ...), custom_call_target="tpu_custom_call" | custom-call | flops 7000000000 | bytes 24582144 | tf_op jit(solution)/shard_map/input_backward/pallas_call | solution.py:847
  347.0 6.5 %bitcast_convert_fusion.3 = bf16[1536,768]{1,0:T(8,128)(2,1)} fusion(bf16[4,256,1536]{2,1,0:T(8,128)(2,1)} %get-tuple-element.254.refs_0_.refs_4_, bf16[4,256,768]{2,1,0:T(8,128)(2,1)} %get-tuple-element.299.refs_0_), kind=kOutput, calls=%fused_computation.3 | convolution fusion | flops 2417098752 | bytes 7077888 | tf_op jit(solution)/shard_map/dot_general | solution.py:1316
  353.6 6.4 %collective-permute-done.51.refs_6_ = bf16[384,768]{1,0:T(8,128)(2,1)S(1)} collective-permute-done((bf16[384,768]{1,0:T(8,128)(2,1)}, bf16[384,768]{1,0:T(8,128)(2,1)S(1)}, u32[]{:S(2)}, u32[]{:S(2)}) %collective-permute-start.51) | collective-permute-done | bytes 589856 | tf_op jit(solution)/shard_map/ppermute | solution.py:61
  375.5 12.3 %collective-permute-done.57.refs_5_ = bf16[256,1664]{1,0:T(8,128)(2,1)S(1)} collective-permute-done((bf16[256,1664]{1,0:T(8,128)(2,1)S(1)}, bf16[256,1664]{1,0:T(8,128)(2,1)S(1)}, u32[]{:S(2)}, u32[]{:S(2)}) %collective-permute-start.57) | collective-permute-done | bytes 852000 | tf_op jit(solution)/shard_map/ppermute | solution.py:22
  399.1 10.9 %gate_backward.3 = (bf16[4,256,768]{2,1,0:T(8,128)(2,1)}, bf16[4,256,768]{2,1,0:T(8,128)(2,1)}, bf16[4,256,768]{2,1,0:T(8,128)(2,1)}, f32[8,768]{1,0:T(8,128)}, bf16[4,256,1536]{2,1,0:T(8,128)(2,1)}) custom-call(s32[9]{0:T(128)} %pad_add_fusion.t_ref, bf16[4,256,768]{2,1,0:T(8,128)(2,1)} %get-tuple-element.301.refs_0_, ...), custom_call_target="tpu_custom_call" | custom-call | flops 3000000000 | bytes 20783104 | tf_op jit(solution)/shard_map/gate_backward/pallas_call | solution.py:847
  425.2 15.9 %mix_backward.4 = (bf16[4,256,768]{2,1,0:T(8,128)(2,1)}, bf16[4,256,256]{2,1,0:T(8,128)(2,1)}, f32[4,16,256]{2,1,0:T(8,128)}, f32[8,768]{1,0:T(8,128)}, f32[8,25...) custom-call(s32[9]{0:T(128)} %pad_add_fusion.t_ref, ...), custom_call_target="tpu_custom_call" | custom-call | flops 4000000000 | bytes 14852096 | tf_op jit(solution)/shard_map/mix_backward/pallas_call | solution.py:847
  448.0 16.2 %mix_backward.5 = (bf16[4,256,768]{2,1,0:T(8,128)(2,1)}, bf16[4,256,256]{2,1,0:T(8,128)(2,1)}, f32[4,16,256]{2,1,0:T(8,128)}, f32[8,768]{1,0:T(8,128)}, f32[8,25...) custom-call(s32[9]{0:T(128)} %pad_add_fusion.t_ref, ...), custom_call_target="tpu_custom_call", output_to_operand_aliasing={{0}: (15, {}), {1}: (16, {}), {2}: (17, {})} | custom-call | flops 4000000000 | bytes 17530880 | tf_op jit(solution)/shard_map/mix_backward/pallas_call | solution.py:847
  467.0 5.7 bitcast_convert_fusion
  478.7 15.1 %input_backward.3 = (bf16[2,256,1536]{2,1,0:T(8,128)(2,1)}, bf16[2,256,1536]{2,1,0:T(8,128)(2,1)}, f32[16,1536]{1,0:T(8,128)}, f32[1,1536]{1,0:T(1,128)}) custom-call(s32[9]{0:T(128)} %pad_add_fusion.t_ref, bf16[4,256,768]{2,1,0:T(8,128)(2,1)} %get-tuple-element.355.refs_0_, bf16[4,256,768]{2,1,0:T(8,128)(2,1)} %get-tuple-element.313.refs_1_, ...), custom_call_target="tpu_custom_call" | custom-call | flops 7000000000 | bytes 18388992 | tf_op jit(solution)/shard_map/input_backward/pallas_call | solution.py:847
  510.2 9.9 %collective-permute-done.70 = bf16[256,1536]{1,0:T(8,128)(2,1)} collective-permute-done((bf16[256,1536]{1,0:T(8,128)(2,1)}, bf16[256,1536]{1,0:T(8,128)(2,1)}, u32[]{:S(2)}, u32[]{:S(2)}) %collective-permute-start.70) | collective-permute-done | bytes 786464 | tf_op jit(solution)/shard_map/ppermute | solution.py:22
  520.2 6.3 %collective-permute-done.68.refs_2_.refs_6_ = bf16[576,768]{1,0:T(8,128)(2,1)S(1)} collective-permute-done((bf16[576,768]{1,0:T(8,128)(2,1)}, bf16[576,768]{1,0:T(8,128)(2,1)S(1)}, u32[]{:S(2)}, u32[]{:S(2)}) %collective-permute-start.68) | collective-permute-done | bytes 884768 | tf_op jit(solution)/shard_map/ppermute | solution.py:61
  538.1 7.0 %collective-permute-done.71.refs_2_ = bf16[192,768]{1,0:T(8,128)(2,1)} collective-permute-done((bf16[192,768]{1,0:T(8,128)(2,1)}, bf16[192,768]{1,0:T(8,128)(2,1)}, u32[]{:S(2)}, u32[]{:S(2)}) %collective-permute-start.71) | collective-permute-done | bytes 294944 | tf_op jit(solution)/shard_map/ppermute | solution.py:61
  552.9 5.9 collective-permute-done.74
  575.3 6.1 %ring_final.1 = (f32[2,192,2,768]{3,2,1,0:T(2,128)}, f32[2,192,768]{2,1,0:T(8,128)}) custom-call(s32[9]{0:T(128)} %pad_add_fusion.t_ref, bf16[8,192,768]{2,1,0:T(8,128)(2,1)} %bitcast.244, bf16[8,192,768]{2,1,0:T(8,128)(2,1)} %bitcast.235, bf16[8,192,768]{2,1,0:T(8,128)(2,1)} %bitcast.226, bf16[8,192,768]{2,1,0:T(8,128)(2,1)} %bitcast.262, ...), custom_call_target="tpu_custom_call" | custom-call | flops 1000000 | bytes 23298048 | tf_op jit(solution)/shard_map/ring_final/pallas_call | solution.py:847
  (573 shorter events, 286.8 us)
Async XLA Ops:
  7.3 129.3 %all-gather.3.cloned.1.call-start = ((), (), s32[]{:S(2)}) async-start(), calls=%async_computation | async-start | bytes 1081344 | tf_op jit(solution)/shard_map/all_gather | solution.py:1140
  15.1 39.7 %collective-permute-start.18 = (bf16[256,1536]{1,0:T(8,128)(2,1)S(1)}, bf16[256,1536]{1,0:T(8,128)(2,1)}, u32[]{:S(2)}, u32[]{:S(2)}) collective-permute-start(bf16[256,1536]{1,0:T(8,128)(2,1)S(1)} %copy-done.1), channel_id=1, source_target_pairs={{0,2},{1,3},{2,0},{3,1},{4,6},{5,7},{6,4},{7,5},{8,10},{9,11},{10,... | collective-permute-start | bytes 2359304 | tf_op jit(solution)/shard_map/ppermute | solution.py:22
  44.4 23.9 %collective-permute-start.11 = (bf16[192,1536]{1,0:T(8,128)(2,1)S(1)}, bf16[192,1536]{1,0:T(8,128)(2,1)}, u32[]{:S(2)}, u32[]{:S(2)}) collective-permute-start(bf16[192,1536]{1,0:T(8,128)(2,1)S(1)} %pad_maximum_fusion.3.refs_3_.refs_12_.refs_7_.refs_16_), channel_id=1, source_target_pairs={{0,8},{8,16},{16,24},{24,28},{28,20},{20,12},{12,4},{4,0},{1,9},{9... | collective-permute-start | bytes 1769480 | tf_op jit(solution)/shard_map/ppermute | solution.py:61
  46.0 22.3 %collective-permute-start.12 = (bf16[192,1536]{1,0:T(8,128)(2,1)S(1)}, bf16[192,1536]{1,0:T(8,128)(2,1)}, u32[]{:S(2)}, u32[]{:S(2)}) collective-permute-start(bf16[192,1536]{1,0:T(8,128)(2,1)S(1)} %pad_maximum_fusion.3.refs_3_.refs_12_.refs_7_.refs_16_), channel_id=1, source_target_pairs={{0,4},{8,0},{16,8},{24,16},{28,24},{20,28},{12,20},{4,12},{1,5},{9... | collective-permute-start | bytes 1769480 | tf_op jit(solution)/shard_map/ppermute | solution.py:61
  76.1 33.8 %collective-permute-start.20 = (bf16[256,1536]{1,0:T(8,128)(2,1)}, bf16[256,1536]{1,0:T(8,128)(2,1)S(1)}, u32[]{:S(2)}, u32[]{:S(2)}) collective-permute-start(bf16[256,1536]{1,0:T(8,128)(2,1)} %refs_3_.1), channel_id=1, source_target_pairs={{0,2},{1,3},{2,0},{3,1},{4,6},{5,7},{6,4},{7,5},{8,10},{9,11},{10,... | collective-permute-start | bytes 2359304 | tf_op jit(solution)/shard_map/ppermute | solution.py:22
  84.1 25.9 %collective-permute-start.21 = (bf16[192,1536]{1,0:T(8,128)(2,1)}, bf16[192,1536]{1,0:T(8,128)(2,1)S(1)}, u32[]{:S(2)}, u32[]{:S(2)}) collective-permute-start(bf16[192,1536]{1,0:T(8,128)(2,1)} %collective-permute-done.15.refs_6_.refs_15_.refs_10_.refs_19_), channel_id=1, source_target_pairs={{0,8},{8,16},{16,24},{24,28},{28,20},{20,12},{12,4},{4,0},{1,9},{9... | collective-permute-start | bytes 1769480 | tf_op jit(solution)/shard_map/ppermute | solution.py:61
  85.7 24.2 %collective-permute-start.22 = (bf16[192,1536]{1,0:T(8,128)(2,1)}, bf16[192,1536]{1,0:T(8,128)(2,1)S(1)}, u32[]{:S(2)}, u32[]{:S(2)}) collective-permute-start(bf16[192,1536]{1,0:T(8,128)(2,1)} %collective-permute-done.16.refs_7_.refs_16_.refs_11_.refs_20_), channel_id=1, source_target_pairs={{0,4},{8,0},{16,8},{24,16},{28,24},{20,28},{12,20},{4,12},{1,5},{9... | collective-permute-start | bytes 1769480 | tf_op jit(solution)/shard_map/ppermute | solution.py:61
  146.8 22.8 %collective-permute-start.29 = (bf16[192,2304]{1,0:T(8,128)(2,1)S(1)}, bf16[192,2304]{1,0:T(8,128)(2,1)S(1)}, u32[]{:S(2)}, u32[]{:S(2)}) collective-permute-start(bf16[192,2304]{1,0:T(8,128)(2,1)S(1)} %collective-permute-done.25.refs_13_.refs_8_.refs_17_), channel_id=1, source_target_pairs={{0,8},{8,16},{16,24},{24,28},{28,20},{20,12},{12,4},{4,0},{1,9},{9... | collective-permute-start | bytes 2654216 | tf_op jit(solution)/shard_map/ppermute | solution.py:61
  147.5 23.0 %collective-permute-start.30 = (bf16[192,2304]{1,0:T(8,128)(2,1)S(1)}, bf16[192,2304]{1,0:T(8,128)(2,1)S(1)}, u32[]{:S(2)}, u32[]{:S(2)}) collective-permute-start(bf16[192,2304]{1,0:T(8,128)(2,1)S(1)} %collective-permute-done.26.refs_14_.refs_9_.refs_18_), channel_id=1, source_target_pairs={{0,4},{8,0},{16,8},{24,16},{28,24},{20,28},{12,20},{4,12},{1,5},{9... | collective-permute-start | bytes 2654216 | tf_op jit(solution)/shard_map/ppermute | solution.py:61
  178.1 23.0 %collective-permute-start.31 = (bf16[256,1536]{1,0:T(8,128)(2,1)}, bf16[256,1536]{1,0:T(8,128)(2,1)}, u32[]{:S(2)}, u32[]{:S(2)}) collective-permute-start(bf16[256,1536]{1,0:T(8,128)(2,1)} %multiply_convert_fusion.refs_0_), channel_id=1, source_target_pairs={{0,1},{1,0},{2,3},{3,2},{4,5},{5,4},{6,7},{7,6},{8,9},{9,8},{10,11... | collective-permute-start | bytes 2359304 | tf_op jit(solution)/shard_map/ppermute | solution.py:22
  198.5 29.3 %collective-permute-start.40 = (bf16[256,1536]{1,0:T(8,128)(2,1)}, bf16[256,1536]{1,0:T(8,128)(2,1)}, u32[]{:S(2)}, u32[]{:S(2)}) collective-permute-start(bf16[256,1536]{1,0:T(8,128)(2,1)} %refs_3_.1), channel_id=1, source_target_pairs={{0,1},{1,0},{2,3},{3,2},{4,5},{5,4},{6,7},{7,6},{8,9},{9,8},{10,11... | collective-permute-start | bytes 2359304 | tf_op jit(solution)/shard_map/ppermute | solution.py:22
  201.1 26.6 %collective-permute-start.41 = (bf16[256,1536]{1,0:T(8,128)(2,1)}, bf16[256,1536]{1,0:T(8,128)(2,1)S(1)}, u32[]{:S(2)}, u32[]{:S(2)}) collective-permute-start(bf16[256,1536]{1,0:T(8,128)(2,1)} %copy-done.37), channel_id=1, source_target_pairs={{0,1},{1,0},{2,3},{3,2},{4,5},{5,4},{6,7},{7,6},{8,9},{9,8},{10,11... | collective-permute-start | bytes 2359304 | tf_op jit(solution)/shard_map/ppermute | solution.py:22
  202.6 25.1 %collective-permute-start.38 = (bf16[96,1536]{1,0:T(8,128)(2,1)S(1)}, bf16[96,1536]{1,0:T(8,128)(2,1)S(1)}, u32[]{:S(2)}, u32[]{:S(2)}) collective-permute-start(bf16[96,1536]{1,0:T(8,128)(2,1)S(1)} %slice.358), channel_id=1, source_target_pairs={{0,8},{8,16},{16,24},{24,28},{28,20},{20,12},{12,4},{4,0},{1,9},{9... | collective-permute-start | bytes 884744 | tf_op jit(solution)/shard_map/ppermute | solution.py:61
  203.4 24.3 %collective-permute-start.39 = (bf16[96,1536]{1,0:T(8,128)(2,1)S(1)}, bf16[96,1536]{1,0:T(8,128)(2,1)S(1)}, u32[]{:S(2)}, u32[]{:S(2)}) collective-permute-start(bf16[96,1536]{1,0:T(8,128)(2,1)S(1)} %slice.359), channel_id=1, source_target_pairs={{0,4},{8,0},{16,8},{24,16},{28,24},{20,28},{12,20},{4,12},{1,5},{9... | collective-permute-start | bytes 884744 | tf_op jit(solution)/shard_map/ppermute | solution.py:61
  248.1 21.0 %collective-permute-start.42 = (bf16[2,256,1536]{2,1,0:T(8,128)(2,1)}, bf16[2,256,1536]{2,1,0:T(8,128)(2,1)}, u32[]{:S(2)}, u32[]{:S(2)}) collective-permute-start(bf16[2,256,1536]{2,1,0:T(8,128)(2,1)} %get-tuple-element.261), channel_id=1, source_target_pairs={{0,1},{1,0},{2,3},{3,2},{4,5},{5,4},{6,7},{7,6},{8,9},{9,8},{10,11... | collective-permute-start | bytes 4718600 | tf_op jit(solution)/shard_map/ppermute | solution.py:22
  270.6 45.4 %collective-permute-start.47 = (bf16[256,1536]{1,0:T(8,128)(2,1)S(1)}, bf16[256,1536]{1,0:T(8,128)(2,1)S(1)}, u32[]{:S(2)}, u32[]{:S(2)}) collective-permute-start(bf16[256,1536]{1,0:T(8,128)(2,1)S(1)} %fusion.14), channel_id=1, source_target_pairs={{0,2},{1,3},{2,0},{3,1},{4,6},{5,7},{6,4},{7,5},{8,10},{9,11},{10,... | collective-permute-start | bytes 2359304 | tf_op jit(solution)/shard_map/ppermute | solution.py:22
  278.8 31.0 %collective-permute-start.45 = (bf16[192,768]{1,0:T(8,128)(2,1)}, bf16[192,768]{1,0:T(8,128)(2,1)S(1)}, u32[]{:S(2)}, u32[]{:S(2)}) collective-permute-start(bf16[192,768]{1,0:T(8,128)(2,1)} %get-tuple-element.270), channel_id=1, source_target_pairs={{0,8},{8,16},{16,24},{24,28},{28,20},{20,12},{12,4},{4,0},{1,9},{9... | collective-permute-start | bytes 884744 | tf_op jit(solution)/shard_map/ppermute | solution.py:61
  279.6 30.3 %collective-permute-start.46 = (bf16[192,768]{1,0:T(8,128)(2,1)}, bf16[192,768]{1,0:T(8,128)(2,1)S(1)}, u32[]{:S(2)}, u32[]{:S(2)}) collective-permute-start(bf16[192,768]{1,0:T(8,128)(2,1)} %get-tuple-element.271), channel_id=1, source_target_pairs={{0,4},{8,0},{16,8},{24,16},{28,24},{20,28},{12,20},{4,12},{1,5},{9... | collective-permute-start | bytes 884744 | tf_op jit(solution)/shard_map/ppermute | solution.py:61
  336.8 24.1 %collective-permute-start.53 = (bf16[256,1536]{1,0:T(8,128)(2,1)}, bf16[256,1536]{1,0:T(8,128)(2,1)S(1)}, u32[]{:S(2)}, u32[]{:S(2)}) collective-permute-start(bf16[256,1536]{1,0:T(8,128)(2,1)} %fusion.15), channel_id=1, source_target_pairs={{0,2},{1,3},{2,0},{3,1},{4,6},{5,7},{6,4},{7,5},{8,10},{9,11},{10,... | collective-permute-start | bytes 2359304 | tf_op jit(solution)/shard_map/ppermute | solution.py:22
  375.5 21.8 %collective-permute-start.54 = (bf16[256,1664]{1,0:T(8,128)(2,1)S(1)}, bf16[256,1664]{1,0:T(8,128)(2,1)S(1)}, u32[]{:S(2)}, u32[]{:S(2)}) collective-permute-start(bf16[256,1664]{1,0:T(8,128)(2,1)S(1)} %fusion.11.refs_3_), channel_id=1, source_target_pairs={{0,1},{1,0},{2,3},{3,2},{4,5},{5,4},{6,7},{7,6},{8,9},{9,8},{10,11... | collective-permute-start | bytes 2555912 | tf_op jit(solution)/shard_map/ppermute | solution.py:22
  504.8 21.7 %collective-permute-start.68 = (bf16[576,768]{1,0:T(8,128)(2,1)}, bf16[576,768]{1,0:T(8,128)(2,1)S(1)}, u32[]{:S(2)}, u32[]{:S(2)}) collective-permute-start(bf16[576,768]{1,0:T(8,128)(2,1)} %get-tuple-element.365), channel_id=1, source_target_pairs={{0,8},{8,16},{16,24},{24,28},{28,20},{20,12},{12,4},{4,0},{1,9},{9... | collective-permute-start | bytes 2654216 | tf_op jit(solution)/shard_map/ppermute | solution.py:61
  505.7 21.5 %collective-permute-start.69 = (bf16[576,768]{1,0:T(8,128)(2,1)}, bf16[576,768]{1,0:T(8,128)(2,1)S(1)}, u32[]{:S(2)}, u32[]{:S(2)}) collective-permute-start(bf16[576,768]{1,0:T(8,128)(2,1)} %get-tuple-element.366), channel_id=1, source_target_pairs={{0,4},{8,0},{16,8},{24,16},{28,24},{20,28},{12,20},{4,12},{1,5},{9... | collective-permute-start | bytes 2654216 | tf_op jit(solution)/shard_map/ppermute | solution.py:61
  550.8 24.5 %collective-permute-start.79 = (bf16[192,768]{1,0:T(8,128)(2,1)}, bf16[192,768]{1,0:T(8,128)(2,1)}, u32[]{:S(2)}, u32[]{:S(2)}) collective-permute-start(bf16[192,768]{1,0:T(8,128)(2,1)} %get-tuple-element.382), channel_id=1, source_target_pairs={{0,8},{8,16},{16,24},{24,28},{28,20},{20,12},{12,4},{4,0},{1,9},{9... | collective-permute-start | bytes 884744 | tf_op jit(solution)/shard_map/ppermute | solution.py:61
  552.4 22.9 %collective-permute-start.80 = (bf16[192,768]{1,0:T(8,128)(2,1)}, bf16[192,768]{1,0:T(8,128)(2,1)}, u32[]{:S(2)}, u32[]{:S(2)}) collective-permute-start(bf16[192,768]{1,0:T(8,128)(2,1)} %get-tuple-element.383), channel_id=1, source_target_pairs={{0,4},{8,0},{16,8},{24,16},{28,24},{20,28},{12,20},{4,12},{1,5},{9... | collective-permute-start | bytes 884744 | tf_op jit(solution)/shard_map/ppermute | solution.py:61
  (155 other events, 1443.5 us)
Sparse Core Ops, SparseCore 0:
  16.1 57.6 all-gather.2

commit v4 on v3

--- a/solution.py
+++ b/solution.py
@@ -14,7 +14,7 @@
 BF16 = jnp.bfloat16
 WALK = (0, 2, 4, 6, 7, 5, 3, 1)
 HEAD_ROWS = 16
-VMEM = 56 * 1024 * 1024
+VMEM = 48 * 1024 * 1024
 
 
 def permute(value, axis, mask):
@@ -464,6 +464,7 @@
     state = held[...]
     state_ref[0] = state
     entering = dot(c_rows, state.astype(BF16)) * enter_x
+    half = rows // 2
     xl = xc.astype(BF16)
     low_mask, high_mask = pair_masks(rows)
     zero = jnp.zeros((rows, 128), BF16)
@@ -471,10 +472,16 @@
         span = slice(pair * 128, pair * 128 + 128)
         part = xl[:, span]
         acc = entering[:, span] + xc[:, span] * cp[5:6, span]
+        early, late = acc[:half], acc[half:]
         for side, mask in ((0, low_mask), (1, high_mask)):
             head = 2 * pair + side
-            weights = jnp.exp(cols[:, head : head + 1] - less[head : head + 1] + bar) * scores
-            acc = acc + dot(weights.astype(BF16), jnp.where(mask, part, zero))
+            column, line = cols[:, head : head + 1], less[head : head + 1]
+            own = jnp.where(mask, part, zero)
+            first = jnp.exp(column[:half] - line[:, :half] + bar[:half, :half]) * scores[:half, :half]
+            second = jnp.exp(column[half:] - line + bar[half:]) * scores[half:]
+            early = early + dot(first.astype(BF16), own[:half])
+            late = late + dot(second.astype(BF16), own)
+        acc = jnp.concatenate([early, late], 0)
         y_ref[0, :, span] = acc
     keep = enter_x[rows - 1 : rows]
     held[...] = state * keep + dot(
@@ -545,19 +552,28 @@
 
     low_mask, high_mask = pair_masks(rows)
     zero = jnp.zeros((rows, 128), BF16)
-    d_scores = jnp.zeros((rows, rows), F32)
+    half = rows // 2
+    d_first = jnp.zeros((half, rows), F32)
+    d_second = jnp.zeros((half, half), F32)
     d_scan = []
     for pair in range(pairs):
         span = slice(pair * 128, pair * 128 + 128)
         part, grad = xl[:, span], dyl[:, span]
         acc = dx_tail[:, span]
+        early, late = acc[:half], acc[half:]
         for side, mask in ((0, low_mask), (1, high_mask)):
             head = 2 * pair + side
-            decay = jnp.exp(total[head : head + 1] - cols[:, head : head + 1] + bar)
-            weights = (decay * scores).astype(BF16)
-            d_scores = d_scores + decay * dot_t(jnp.where(mask, part, zero), grad)
-            acc = acc + dot(weights, jnp.where(mask, grad, zero))
-        d_scan.append(acc)
+            column, line = cols[:, head : head + 1], total[head : head + 1]
+            own, own_grad = jnp.where(mask, part, zero), jnp.where(mask, grad, zero)
+            first = jnp.exp(line - column[:half] + bar[:half])
+            second = jnp.exp(line[:, half:] - column[half:] + bar[half:, half:])
+            d_first = d_first + first * dot_t(own[:half], grad)
+            d_second = d_second + second * dot_t(own[half:], grad[half:])
+            early = early + dot((first * scores[:half]).astype(BF16), own_grad)
+            late = late + dot((second * scores[half:, half:]).astype(BF16), own_grad[half:])
+        d_scan.append(jnp.concatenate([early, late], 0))
+    d_scores = jnp.concatenate([jnp.zeros((half, half), F32), d_second], 1)
+    d_scores = jnp.concatenate([d_first, d_scores], 0)
     d_scan = jnp.concatenate(d_scan, 1)
     db = db + dot(d_scores.astype(BF16), c_rows)
     dc = dc + dot(d_scores.T.astype(BF16), b_rows)

time: 608 us -> 595 us (0.979)
  Pallas kernels: 234 us -> 200 us
  waiting for transfers between devices: 139 us -> 154 us
  local copies, waits for them, and re-layouts: 52.5 us -> 65.3 us
    pallas_call x23, Pallas kernels: 234 us -> 200 us  [call(): pl.pallas_call(body, grid_spec=pltpu.PrefetchScalarGridSpec(num_scalar_pr...]
    unnamed x202 -> x346, local copies, waits for them, and re-layouts: 14.5 us -> 29.9 us
    ppermute x33, waiting for transfers between devices: 72.9 us -> 86.9 us  [permute(): return lax.ppermute(value, axis, [(at, at ^ mask) for at in range(size)])]
  transfers between devices with their start and end apart: 82 -> 82, of which waited for: 39 -> 40; matrix products, arithmetic and copies ran while one was open for 13% -> 11% of each run, Pallas kernels for 34% -> 30%
where the time goes in v4:
time: 595 us; the launch traced here: 585 us
  Pallas kernels  200 us (34%)
  waiting for transfers between devices  154 us (26%)
  starting transfers between devices  77 us (13%)
  local copies, waits for them, and re-layouts  65.3 us (11%)
  other arithmetic  36.3 us (6%)
  matrix products  35 us (6%)
  between operations  16.8 us (3%)
    pallas_call x23, Pallas kernels, call(): pl.pallas_call(body, grid_spec=pltpu.PrefetchScalarGridSpec(num_scalar_pr...  200 us
    ppermute x33, waiting for transfers between devices, permute(): return lax.ppermute(value, axis, [(at, at ^ mask) for at in range(size)])  86.9 us
    ppermute x48, waiting for transfers between devices, step_ring(): lax.ppermute(value, 'fsdp', [(WALK[at], WALK[(at + by) % size]) for at in...  67.4 us
    ppermute x48, starting transfers between devices, step_ring(): lax.ppermute(value, 'fsdp', [(WALK[at], WALK[(at + by) % size]) for at in...  51.6 us
    dot_general x8, matrix products, weight_grad(): lax.dot_general(left, right, (((0, 1), (0, 1)), ((), ())), preferred_elem...  35 us
    unnamed x346, local copies, waits for them, and re-layouts  29.9 us
    ppermute x33, starting transfers between devices, permute(): return lax.ppermute(value, axis, [(at, at ^ mask) for at in range(size)])  25.4 us
  transfers between devices with their start and end apart: 82, of which 40 were waited for; matrix products, arithmetic and copies ran while one was open for 11% of the time, Pallas kernels for 30%

profile of v4, /device:TPU:0, one launch (start us, length us, event | category | flops | bytes accessed | tf_op | source)
XLA Modules:
  0.0 584.8 jit_solution(15634521352407326077)
XLA Ops:
  47.1 5.9 %collective-permute-done.9 = bf16[2,2,1,2,1,64,256]{6,5,4,3,2,1,0:T(8,128)(2,1)S(1)} collective-permute-done((bf16[2,2,1,2,1,64,256]{6,5,4,3,2,1,0:T(8,128)(2,1)S(1)}, bf16[2,2,1,2,1,64,256]{6,5,4,3,2,1,0:T(8,128)(2,1)S(1)}, u32[]{:S(2)}, u32[]{:S(2)}) %collective-permute-start.9) | collective-permute-done | bytes 262176 | tf_op jit(solution)/shard_map/ppermute | solution.py:22
  57.8 11.1 %collective-permute-done.13.refs_19_.refs_14_ = bf16[96,768]{1,0:T(8,128)(2,1)S(1)} collective-permute-done((bf16[96,768]{1,0:T(8,128)(2,1)}, bf16[96,768]{1,0:T(8,128)(2,1)S(1)}, u32[]{:S(2)}, u32[]{:S(2)}) %collective-permute-start.13) | collective-permute-done | bytes 147488 | tf_op jit(solution)/shard_map/ppermute | solution.py:61
  95.7 22.3 %project_scan.2 = (bf16[4,256,1536]{2,1,0:T(8,128)(2,1)}, bf16[4,256,768]{2,1,0:T(8,128)(2,1)}, f32[4,256,256]{2,1,0:T(8,128)}, f32[4,16,256]{2,1,0:T(8,128)S(1)...) custom-call(s32[9]{0:T(128)S(1)} %pad_add_fusion.t_ref, bf16[256,1536]{1,0:T(8,128)(2,1)S(1)} %copy-done.6, ...), custom_call_target="tpu_custom_call" | custom-call | flops 10000000000 | bytes 17741824 | tf_op jit(solution)/shard_map/project_scan/pallas_call | solution.py:863
  120.3 5.7 collective-permute-done.23.refs_10_.refs_19_.refs_14_.refs_23_
  130.0 13.4 %gate_forward.2 = (bf16[4,256,768]{2,1,0:T(8,128)(2,1)}, bf16[2,256,1664]{2,1,0:T(8,128)(2,1)}, bf16[2,256,1664]{2,1,0:T(8,128)(2,1)}) custom-call(s32[9]{0:T(128)S(1)} %pad_add_fusion.t_ref, bf16[4,256,1536]{2,1,0:T(8,128)(2,1)} %get-tuple-element.226.refs_0_.refs_4_, f32[4,256,768]{2,1,0:T(8,128)} %get-tuple-element.231.refs_1_.refs_6_, ...), custom_call_target="tpu_custom_call" | custom-call | flops 6000000000 | bytes 20758528 | tf_op jit(solution)/shard_map/gate_forward/pallas_call | solution.py:863
  164.7 13.7 %collective-permute-done.28 = bf16[256,1664]{1,0:T(8,128)(2,1)} collective-permute-done((bf16[256,1664]{1,0:T(8,128)(2,1)}, bf16[256,1664]{1,0:T(8,128)(2,1)}, u32[]{:S(2)}, u32[]{:S(2)}) %collective-permute-start.28) | collective-permute-done | bytes 852000 | tf_op jit(solution)/shard_map/ppermute | solution.py:22
  186.2 16.4 %collective-permute-done.32.refs_2_ = bf16[256,1536]{1,0:T(8,128)(2,1)} collective-permute-done((bf16[256,1536]{1,0:T(8,128)(2,1)}, bf16[256,1536]{1,0:T(8,128)(2,1)}, u32[]{:S(2)}, u32[]{:S(2)}) %collective-permute-start.32) | collective-permute-done | bytes 786464 | tf_op jit(solution)/shard_map/ppermute | solution.py:22
  218.0 21.7 %project_scan.3 = (bf16[4,256,1536]{2,1,0:T(8,128)(2,1)}, bf16[4,256,768]{2,1,0:T(8,128)(2,1)}, f32[4,256,256]{2,1,0:T(8,128)}, f32[4,16,256]{2,1,0:T(8,128)S(1)...) custom-call(s32[9]{0:T(128)S(1)} %pad_add_fusion.t_ref, bf16[256,1536]{1,0:T(8,128)(2,1)} %multiply_convert_fusion.refs_0_, ...), custom_call_target="tpu_custom_call" | custom-call | flops 10000000000 | bytes 21870592 | tf_op jit(solution)/shard_map/project_scan/pallas_call | solution.py:863
  239.8 16.5 %gate_forward.3 = (bf16[4,256,768]{2,1,0:T(8,128)(2,1)}, bf16[2,256,1536]{2,1,0:T(8,128)(2,1)}, bf16[2,256,1536]{2,1,0:T(8,128)(2,1)}, bf16[4,256,1536]{2,1,0:T(...) custom-call(s32[9]{0:T(128)S(1)} %pad_add_fusion.t_ref, ...), custom_call_target="tpu_custom_call" | custom-call | flops 6000000000 | bytes 32522240 | tf_op jit(solution)/shard_map/gate_forward/pallas_call | solution.py:863
  261.6 6.2 %gate_backward.2 = (bf16[4,256,768]{2,1,0:T(8,128)(2,1)S(1)}, bf16[4,256,768]{2,1,0:T(8,128)(2,1)S(1)}, bf16[4,256,768]{2,1,0:T(8,128)(2,1)S(1)}, f32[8,768]{1,0:T(8,128)S(1)}) custom-call(s32[9]{0:T(128)S(1)} %pad_add_fusion.t_ref, bf16[4,256,768]{2,1,0:T(8,128)(2,1)} %get-tuple-element.262.refs_0_, f32[4,256,768]{2,1,0:T(8,128)} %get-tuple-element.256.refs_1_.refs_6_, ...), custom_call_target="tpu_custom_call" | custom-call | flops 3000000000 | bytes 11116544 | tf_op jit(solution)/shard_map/gate_backward/pallas_call | solution.py:863
  281.4 27.5 %mix_backward.3 = (bf16[4,256,768]{2,1,0:T(8,128)(2,1)S(1)}, bf16[4,256,256]{2,1,0:T(8,128)(2,1)S(1)}, f32[4,16,256]{2,1,0:T(8,128)S(1)}, f32[8,768]{1,0:T(8,128...) custom-call(s32[9]{0:T(128)S(1)} %pad_add_fusion.t_ref, ...), custom_call_target="tpu_custom_call" | custom-call | flops 8000000000 | bytes 14852096 | tf_op jit(solution)/shard_map/mix_backward/pallas_call | solution.py:863
  313.9 13.4 %input_backward.2 = (bf16[2,256,1536]{2,1,0:T(8,128)(2,1)}, bf16[2,256,1536]{2,1,0:T(8,128)(2,1)}, f32[16,1536]{1,0:T(8,128)S(1)}, f32[1,1536]{1,0:T(1,128)S(1)}) custom-call(s32[9]{0:T(128)S(1)} %pad_add_fusion.t_ref, bf16[4,256,768]{2,1,0:T(8,128)(2,1)} %copy-done.103, bf16[4,256,768]{2,1,0:T(8,128)(2,1)} %copy-done.105, ...), custom_call_target="tpu_custom_call" | custom-call | flops 7000000000 | bytes 24582144 | tf_op jit(solution)/shard_map/input_backward/pallas_call | solution.py:863
  341.2 6.1 %bitcast_convert_fusion.3 = bf16[1536,768]{1,0:T(8,128)(2,1)} fusion(bf16[4,256,1536]{2,1,0:T(8,128)(2,1)} %get-tuple-element.254.refs_0_.refs_4_, bf16[4,256,768]{2,1,0:T(8,128)(2,1)S(1)} %copy-done.104), kind=kOutput, calls=%fused_computation.3 | convolution fusion | flops 2417098752 | bytes 7077888 | tf_op jit(solution)/shard_map/dot_general | solution.py:1332
  347.3 6.6 %collective-permute-done.51.refs_6_ = bf16[384,768]{1,0:T(8,128)(2,1)S(1)} collective-permute-done((bf16[384,768]{1,0:T(8,128)(2,1)S(1)}, bf16[384,768]{1,0:T(8,128)(2,1)S(1)}, u32[]{:S(2)}, u32[]{:S(2)}) %collective-permute-start.51) | collective-permute-done | bytes 589856 | tf_op jit(solution)/shard_map/ppermute | solution.py:61
  368.2 13.6 %collective-permute-done.57.refs_5_ = bf16[256,1664]{1,0:T(8,128)(2,1)S(1)} collective-permute-done((bf16[256,1664]{1,0:T(8,128)(2,1)S(1)}, bf16[256,1664]{1,0:T(8,128)(2,1)S(1)}, u32[]{:S(2)}, u32[]{:S(2)}) %collective-permute-start.57) | collective-permute-done | bytes 852000 | tf_op jit(solution)/shard_map/ppermute | solution.py:22
  388.7 10.3 %gate_backward.3 = (bf16[4,256,768]{2,1,0:T(8,128)(2,1)}, bf16[4,256,768]{2,1,0:T(8,128)(2,1)}, bf16[4,256,768]{2,1,0:T(8,128)(2,1)}, f32[8,768]{1,0:T(8,128)S(1)}, bf16[4,256,1536]{2,1,0:T(8,128)(2,1)}) custom-call(s32[9]{0:T(128)S(1)} %pad_add_fusion.t_ref, bf16[4,256,768]{2,1,0:T(8,128)(2,1)} %get-tuple-element.301.refs_0_, ...), custom_call_target="tpu_custom_call" | custom-call | flops 3000000000 | bytes 20783104 | tf_op jit(solution)/shard_map/gate_backward/pallas_call | solution.py:863
  399.0 6.6 %bitcast_convert_fusion.1 = bf16[1536,768]{1,0:T(8,128)(2,1)} fusion(bf16[4,256,1536]{2,1,0:T(8,128)(2,1)} %get-tuple-element.226.refs_0_.refs_4_, bf16[4,256,768]{2,1,0:T(8,128)(2,1)} %get-tuple-element.313.refs_1_), kind=kOutput, calls=%fused_computation.1 | convolution fusion | flops 2417098752 | bytes 7077888 | tf_op jit(solution)/shard_map/dot_general | solution.py:1332
  414.0 14.5 %mix_backward.4 = (bf16[4,256,768]{2,1,0:T(8,128)(2,1)S(1)}, bf16[4,256,256]{2,1,0:T(8,128)(2,1)S(1)}, f32[4,16,256]{2,1,0:T(8,128)S(1)}, f32[8,768]{1,0:T(8,128...) custom-call(s32[9]{0:T(128)S(1)} %pad_add_fusion.t_ref, ...), custom_call_target="tpu_custom_call" | custom-call | flops 4000000000 | bytes 14852096 | tf_op jit(solution)/shard_map/mix_backward/pallas_call | solution.py:863
  432.7 15.1 %mix_backward.5 = (bf16[4,256,768]{2,1,0:T(8,128)(2,1)S(1)}, bf16[4,256,256]{2,1,0:T(8,128)(2,1)S(1)}, f32[4,16,256]{2,1,0:T(8,128)S(1)}, f32[8,768]{1,0:T(8,128...) custom-call(s32[9]{0:T(128)S(1)} %pad_add_fusion.t_ref, ...), custom_call_target="tpu_custom_call", output_to_operand_aliasing={{0}: (15, {}), {1}: (16, {}), {2}: (17, {})} | custom-call | flops 4000000000 | bytes 17530880 | tf_op jit(solution)/shard_map/mix_backward/pallas_call | solution.py:863
  451.9 6.4 %bitcast_convert_fusion = bf16[1536,768]{1,0:T(8,128)(2,1)} fusion(bf16[4,256,1536]{2,1,0:T(8,128)(2,1)} %get-tuple-element.226.refs_0_.refs_4_, bf16[4,256,768]{2,1,0:T(8,128)(2,1)S(1)} %get-tuple-element.355.refs_0_), kind=kOutput, calls=%fused_computation | convolution fusion | flops 2417098752 | bytes 7077888 | tf_op jit(solution)/shard_map/dot_general | solution.py:1332
  463.0 13.8 %input_backward.3 = (bf16[2,256,1536]{2,1,0:T(8,128)(2,1)}, bf16[2,256,1536]{2,1,0:T(8,128)(2,1)}, f32[16,1536]{1,0:T(8,128)S(1)}, f32[1,1536]{1,0:T(1,128)S(1)}) custom-call(s32[9]{0:T(128)S(1)} %pad_add_fusion.t_ref, bf16[4,256,768]{2,1,0:T(8,128)(2,1)} %copy-done.28, bf16[4,256,768]{2,1,0:T(8,128)(2,1)} %get-tuple-element.313.refs_1_, ...), custom_call_target="tpu_custom_call" | custom-call | flops 7000000000 | bytes 18388992 | tf_op jit(solution)/shard_map/input_backward/pallas_call | solution.py:863
  495.0 10.7 %collective-permute-done.70 = bf16[256,1536]{1,0:T(8,128)(2,1)} collective-permute-done((bf16[256,1536]{1,0:T(8,128)(2,1)}, bf16[256,1536]{1,0:T(8,128)(2,1)}, u32[]{:S(2)}, u32[]{:S(2)}) %collective-permute-start.70) | collective-permute-done | bytes 786464 | tf_op jit(solution)/shard_map/ppermute | solution.py:22
  505.7 5.5 collective-permute-done.68.refs_2_.refs_6_
  540.9 6.5 %collective-permute-done.74 = bf16[8,98,256]{2,0,1:T(8,128)(2,1)S(1)} collective-permute-done((bf16[8,98,256]{2,0,1:T(8,128)(2,1)S(1)}, bf16[8,98,256]{2,0,1:T(8,128)(2,1)S(1)}, u32[]{:S(2)}, u32[]{:S(2)}) %collective-permute-start.74) | collective-permute-done | bytes 401440 | tf_op jit(solution)/shard_map/ppermute | solution.py:22
  (718 shorter events, 278.6 us)
Async XLA Ops:
  7.3 137.6 %all-gather.3.cloned.1.call-start = ((), (), s32[]{:S(2)}) async-start(), calls=%async_computation | async-start | bytes 1081344 | tf_op jit(solution)/shard_map/all_gather | solution.py:1156
  15.0 40.3 %collective-permute-start.18 = (bf16[256,1536]{1,0:T(8,128)(2,1)S(1)}, bf16[256,1536]{1,0:T(8,128)(2,1)}, u32[]{:S(2)}, u32[]{:S(2)}) collective-permute-start(bf16[256,1536]{1,0:T(8,128)(2,1)S(1)} %copy-done.6), channel_id=1, source_target_pairs={{0,2},{1,3},{2,0},{3,1},{4,6},{5,7},{6,4},{7,5},{8,10},{9,11},{10,... | collective-permute-start | bytes 2359304 | tf_op jit(solution)/shard_map/ppermute | solution.py:22
  45.0 24.3 %collective-permute-start.11 = (bf16[192,1536]{1,0:T(8,128)(2,1)S(1)}, bf16[192,1536]{1,0:T(8,128)(2,1)S(1)}, u32[]{:S(2)}, u32[]{:S(2)}) collective-permute-start(bf16[192,1536]{1,0:T(8,128)(2,1)S(1)} %pad_maximum_fusion.3.refs_3_.refs_12_.refs_7_.refs_16_), channel_id=1, source_target_pairs={{0,8},{8,16},{16,24},{24,28},{28,20},{20,12},{12,4},{4,0},{1,9},{9... | collective-permute-start | bytes 1769480 | tf_op jit(solution)/shard_map/ppermute | solution.py:61
  46.6 22.8 %collective-permute-start.12 = (bf16[192,1536]{1,0:T(8,128)(2,1)S(1)}, bf16[192,1536]{1,0:T(8,128)(2,1)}, u32[]{:S(2)}, u32[]{:S(2)}) collective-permute-start(bf16[192,1536]{1,0:T(8,128)(2,1)S(1)} %pad_maximum_fusion.3.refs_3_.refs_12_.refs_7_.refs_16_), channel_id=1, source_target_pairs={{0,4},{8,0},{16,8},{24,16},{28,24},{20,28},{12,20},{4,12},{1,5},{9... | collective-permute-start | bytes 1769480 | tf_op jit(solution)/shard_map/ppermute | solution.py:61
  79.0 39.1 %collective-permute-start.20 = (bf16[256,1536]{1,0:T(8,128)(2,1)S(1)}, bf16[256,1536]{1,0:T(8,128)(2,1)S(1)}, u32[]{:S(2)}, u32[]{:S(2)}) collective-permute-start(bf16[256,1536]{1,0:T(8,128)(2,1)S(1)} %copy-done.19), channel_id=1, source_target_pairs={{0,2},{1,3},{2,0},{3,1},{4,6},{5,7},{6,4},{7,5},{8,10},{9,11},{10,... | collective-permute-start | bytes 2359304 | tf_op jit(solution)/shard_map/ppermute | solution.py:22
  85.1 32.9 %collective-permute-start.21 = (bf16[192,1536]{1,0:T(8,128)(2,1)}, bf16[192,1536]{1,0:T(8,128)(2,1)S(1)}, u32[]{:S(2)}, u32[]{:S(2)}) collective-permute-start(bf16[192,1536]{1,0:T(8,128)(2,1)} %collective-permute-done.15.refs_6_.refs_15_.refs_10_.refs_19_), channel_id=1, source_target_pairs={{0,8},{8,16},{16,24},{24,28},{28,20},{20,12},{12,4},{4,0},{1,9},{9... | collective-permute-start | bytes 1769480 | tf_op jit(solution)/shard_map/ppermute | solution.py:61
  86.7 31.3 %collective-permute-start.22 = (bf16[192,1536]{1,0:T(8,128)(2,1)}, bf16[192,1536]{1,0:T(8,128)(2,1)S(1)}, u32[]{:S(2)}, u32[]{:S(2)}) collective-permute-start(bf16[192,1536]{1,0:T(8,128)(2,1)} %collective-permute-done.16.refs_7_.refs_16_.refs_11_.refs_20_), channel_id=1, source_target_pairs={{0,4},{8,0},{16,8},{24,16},{28,24},{20,28},{12,20},{4,12},{1,5},{9... | collective-permute-start | bytes 1769480 | tf_op jit(solution)/shard_map/ppermute | solution.py:61
  155.6 22.8 %collective-permute-start.29 = (bf16[192,2304]{1,0:T(8,128)(2,1)S(1)}, bf16[192,2304]{1,0:T(8,128)(2,1)}, u32[]{:S(2)}, u32[]{:S(2)}) collective-permute-start(bf16[192,2304]{1,0:T(8,128)(2,1)S(1)} %collective-permute-done.25.refs_13_.refs_8_.refs_17_), channel_id=1, source_target_pairs={{0,8},{8,16},{16,24},{24,28},{28,20},{20,12},{12,4},{4,0},{1,9},{9... | collective-permute-start | bytes 2654216 | tf_op jit(solution)/shard_map/ppermute | solution.py:61
  156.1 22.3 %collective-permute-start.30 = (bf16[192,2304]{1,0:T(8,128)(2,1)}, bf16[192,2304]{1,0:T(8,128)(2,1)}, u32[]{:S(2)}, u32[]{:S(2)}) collective-permute-start(bf16[192,2304]{1,0:T(8,128)(2,1)} %collective-permute-done.26.refs_14_.refs_9_.refs_18_), channel_id=1, source_target_pairs={{0,4},{8,0},{16,8},{24,16},{28,24},{20,28},{12,20},{4,12},{1,5},{9... | collective-permute-start | bytes 2654216 | tf_op jit(solution)/shard_map/ppermute | solution.py:61
  186.2 24.5 %collective-permute-start.31 = (bf16[256,1536]{1,0:T(8,128)(2,1)}, bf16[256,1536]{1,0:T(8,128)(2,1)}, u32[]{:S(2)}, u32[]{:S(2)}) collective-permute-start(bf16[256,1536]{1,0:T(8,128)(2,1)} %multiply_convert_fusion.refs_0_), channel_id=1, source_target_pairs={{0,1},{1,0},{2,3},{3,2},{4,5},{5,4},{6,7},{7,6},{8,9},{9,8},{10,11... | collective-permute-start | bytes 2359304 | tf_op jit(solution)/shard_map/ppermute | solution.py:22
  208.6 31.2 %collective-permute-start.40 = (bf16[256,1536]{1,0:T(8,128)(2,1)S(1)}, bf16[256,1536]{1,0:T(8,128)(2,1)S(1)}, u32[]{:S(2)}, u32[]{:S(2)}) collective-permute-start(bf16[256,1536]{1,0:T(8,128)(2,1)S(1)} %copy-done.20), channel_id=1, source_target_pairs={{0,1},{1,0},{2,3},{3,2},{4,5},{5,4},{6,7},{7,6},{8,9},{9,8},{10,11... | collective-permute-start | bytes 2359304 | tf_op jit(solution)/shard_map/ppermute | solution.py:22
  210.7 29.0 %collective-permute-start.41 = (bf16[256,1536]{1,0:T(8,128)(2,1)S(1)}, bf16[256,1536]{1,0:T(8,128)(2,1)S(1)}, u32[]{:S(2)}, u32[]{:S(2)}) collective-permute-start(bf16[256,1536]{1,0:T(8,128)(2,1)S(1)} %copy-done.34), channel_id=1, source_target_pairs={{0,1},{1,0},{2,3},{3,2},{4,5},{5,4},{6,7},{7,6},{8,9},{9,8},{10,11... | collective-permute-start | bytes 2359304 | tf_op jit(solution)/shard_map/ppermute | solution.py:22
  211.6 28.2 %collective-permute-start.38 = (bf16[96,1536]{1,0:T(8,128)(2,1)S(1)}, bf16[96,1536]{1,0:T(8,128)(2,1)S(1)}, u32[]{:S(2)}, u32[]{:S(2)}) collective-permute-start(bf16[96,1536]{1,0:T(8,128)(2,1)S(1)} %slice.358), channel_id=1, source_target_pairs={{0,8},{8,16},{16,24},{24,28},{28,20},{20,12},{12,4},{4,0},{1,9},{9... | collective-permute-start | bytes 884744 | tf_op jit(solution)/shard_map/ppermute | solution.py:61
  213.3 26.5 %collective-permute-start.39 = (bf16[96,1536]{1,0:T(8,128)(2,1)S(1)}, bf16[96,1536]{1,0:T(8,128)(2,1)S(1)}, u32[]{:S(2)}, u32[]{:S(2)}) collective-permute-start(bf16[96,1536]{1,0:T(8,128)(2,1)S(1)} %slice.359), channel_id=1, source_target_pairs={{0,4},{8,0},{16,8},{24,16},{28,24},{20,28},{12,20},{4,12},{1,5},{9... | collective-permute-start | bytes 884744 | tf_op jit(solution)/shard_map/ppermute | solution.py:61
  274.0 40.0 %collective-permute-start.47 = (bf16[256,1536]{1,0:T(8,128)(2,1)S(1)}, bf16[256,1536]{1,0:T(8,128)(2,1)S(1)}, u32[]{:S(2)}, u32[]{:S(2)}) collective-permute-start(bf16[256,1536]{1,0:T(8,128)(2,1)S(1)} %fusion.14), channel_id=1, source_target_pairs={{0,2},{1,3},{2,0},{3,1},{4,6},{5,7},{6,4},{7,5},{8,10},{9,11},{10,... | collective-permute-start | bytes 2359304 | tf_op jit(solution)/shard_map/ppermute | solution.py:22
  279.1 30.9 %collective-permute-start.45 = (bf16[192,768]{1,0:T(8,128)(2,1)S(1)}, bf16[192,768]{1,0:T(8,128)(2,1)S(1)}, u32[]{:S(2)}, u32[]{:S(2)}) collective-permute-start(bf16[192,768]{1,0:T(8,128)(2,1)S(1)} %get-tuple-element.270), channel_id=1, source_target_pairs={{0,8},{8,16},{16,24},{24,28},{28,20},{20,12},{12,4},{4,0},{1,9},{9... | collective-permute-start | bytes 884744 | tf_op jit(solution)/shard_map/ppermute | solution.py:61
  279.6 30.4 %collective-permute-start.46 = (bf16[192,768]{1,0:T(8,128)(2,1)S(1)}, bf16[192,768]{1,0:T(8,128)(2,1)S(1)}, u32[]{:S(2)}, u32[]{:S(2)}) collective-permute-start(bf16[192,768]{1,0:T(8,128)(2,1)S(1)} %get-tuple-element.271), channel_id=1, source_target_pairs={{0,4},{8,0},{16,8},{24,16},{28,24},{20,28},{12,20},{4,12},{1,5},{9... | collective-permute-start | bytes 884744 | tf_op jit(solution)/shard_map/ppermute | solution.py:61
  332.4 21.9 %collective-permute-start.53 = (bf16[256,1536]{1,0:T(8,128)(2,1)S(1)}, bf16[256,1536]{1,0:T(8,128)(2,1)S(1)}, u32[]{:S(2)}, u32[]{:S(2)}) collective-permute-start(bf16[256,1536]{1,0:T(8,128)(2,1)S(1)} %fusion.15), channel_id=1, source_target_pairs={{0,2},{1,3},{2,0},{3,1},{4,6},{5,7},{6,4},{7,5},{8,10},{9,11},{10,... | collective-permute-start | bytes 2359304 | tf_op jit(solution)/shard_map/ppermute | solution.py:22
  384.7 20.8 %collective-permute-start.59 = (bf16[192,768]{1,0:T(8,128)(2,1)S(1)}, bf16[192,768]{1,0:T(8,128)(2,1)S(1)}, u32[]{:S(2)}, u32[]{:S(2)}) collective-permute-start(bf16[192,768]{1,0:T(8,128)(2,1)S(1)} %get-tuple-element.318), channel_id=1, source_target_pairs={{0,8},{8,16},{16,24},{24,28},{28,20},{20,12},{12,4},{4,0},{1,9},{9... | collective-permute-start | bytes 884744 | tf_op jit(solution)/shard_map/ppermute | solution.py:61
  430.6 20.8 %collective-permute-start.63 = (bf16[576,768]{1,0:T(8,128)(2,1)S(1)}, bf16[576,768]{1,0:T(8,128)(2,1)S(1)}, u32[]{:S(2)}, u32[]{:S(2)}) collective-permute-start(bf16[576,768]{1,0:T(8,128)(2,1)S(1)} %get-tuple-element.337), channel_id=1, source_target_pairs={{0,8},{8,16},{16,24},{24,28},{28,20},{20,12},{12,4},{4,0},{1,9},{9... | collective-permute-start | bytes 2654216 | tf_op jit(solution)/shard_map/ppermute | solution.py:61
  489.6 21.6 %collective-permute-start.68 = (bf16[576,768]{1,0:T(8,128)(2,1)}, bf16[576,768]{1,0:T(8,128)(2,1)S(1)}, u32[]{:S(2)}, u32[]{:S(2)}) collective-permute-start(bf16[576,768]{1,0:T(8,128)(2,1)} %get-tuple-element.365), channel_id=1, source_target_pairs={{0,8},{8,16},{16,24},{24,28},{28,20},{20,12},{12,4},{4,0},{1,9},{9... | collective-permute-start | bytes 2654216 | tf_op jit(solution)/shard_map/ppermute | solution.py:61
  491.2 21.5 %collective-permute-start.69 = (bf16[576,768]{1,0:T(8,128)(2,1)}, bf16[576,768]{1,0:T(8,128)(2,1)S(1)}, u32[]{:S(2)}, u32[]{:S(2)}) collective-permute-start(bf16[576,768]{1,0:T(8,128)(2,1)} %get-tuple-element.366), channel_id=1, source_target_pairs={{0,4},{8,0},{16,8},{24,16},{28,24},{20,28},{12,20},{4,12},{1,5},{9... | collective-permute-start | bytes 2654216 | tf_op jit(solution)/shard_map/ppermute | solution.py:61
  538.8 26.1 %collective-permute-start.79 = (bf16[192,768]{1,0:T(8,128)(2,1)}, bf16[192,768]{1,0:T(8,128)(2,1)S(1)}, u32[]{:S(2)}, u32[]{:S(2)}) collective-permute-start(bf16[192,768]{1,0:T(8,128)(2,1)} %copy-done.96), channel_id=1, source_target_pairs={{0,8},{8,16},{16,24},{24,28},{28,20},{20,12},{12,4},{4,0},{1,9},{9... | collective-permute-start | bytes 884744 | tf_op jit(solution)/shard_map/ppermute | solution.py:61
  539.7 25.2 %collective-permute-start.80 = (bf16[192,768]{1,0:T(8,128)(2,1)}, bf16[192,768]{1,0:T(8,128)(2,1)S(1)}, u32[]{:S(2)}, u32[]{:S(2)}) collective-permute-start(bf16[192,768]{1,0:T(8,128)(2,1)} %copy-done.95), channel_id=1, source_target_pairs={{0,4},{8,0},{16,8},{24,16},{28,24},{20,28},{12,20},{4,12},{1,5},{9... | collective-permute-start | bytes 884744 | tf_op jit(solution)/shard_map/ppermute | solution.py:61
  (228 other events, 2262.6 us)
Sparse Core Ops, SparseCore 0:
  16.0 57.4 all-gather.2

commit v5 on v4

--- a/solution.py
+++ b/solution.py
@@ -15,6 +15,7 @@
 WALK = (0, 2, 4, 6, 7, 5, 3, 1)
 HEAD_ROWS = 16
 VMEM = 48 * 1024 * 1024
+SMALL = 24 * 1024 * 1024
 
 
 def permute(value, axis, mask):
@@ -871,7 +872,7 @@
         ),
         out_shape=outs,
         compiler_params=pltpu.CompilerParams(
-            dimension_semantics=("arbitrary",), vmem_limit_bytes=VMEM
+            dimension_semantics=("arbitrary",), vmem_limit_bytes=SMALL if grid == 1 else VMEM
         ),
         cost_estimate=pl.CostEstimate(flops=flops, bytes_accessed=size, transcendentals=0),
         name=name,

time: 595 us -> 614 us (1.032)
  local copies, waits for them, and re-layouts: 65.3 us -> 90 us
  starting transfers between devices: 77 us -> 87.2 us
  Pallas kernels: 200 us -> 191 us
    unnamed x346 -> x360, local copies, waits for them, and re-layouts: 29.9 us -> 48.1 us
    ppermute x48, starting transfers between devices: 51.6 us -> 62.5 us  [step_ring(): lax.ppermute(value, 'fsdp', [(WALK[at], WALK[(at + by) % size]) for at in...]
    pallas_call x23, Pallas kernels: 200 us -> 191 us  [call(): pl.pallas_call(body, grid_spec=pltpu.PrefetchScalarGridSpec(num_scalar_pr...]
    ppermute x33, waiting for transfers between devices: 86.9 us -> 80.3 us  [permute(): return lax.ppermute(value, axis, [(at, at ^ mask) for at in range(size)])]
  transfers between devices with their start and end apart: 82 -> 82, of which waited for: 40 -> 38; matrix products, arithmetic and copies ran while one was open for 11% -> 12% of each run, Pallas kernels for 30% -> 28%
where the time goes in v5:
time: 614 us; the launch traced here: 608 us
  Pallas kernels  191 us (31%)
  waiting for transfers between devices  153 us (25%)
  local copies, waits for them, and re-layouts  90 us (15%)
  starting transfers between devices  87.2 us (14%)
  other arithmetic  40.6 us (7%)
  matrix products  29.7 us (5%)
  between operations  16.6 us (3%)
    pallas_call x23, Pallas kernels, call(): pl.pallas_call(body, grid_spec=pltpu.PrefetchScalarGridSpec(num_scalar_pr...  191 us
    ppermute x33, waiting for transfers between devices, permute(): return lax.ppermute(value, axis, [(at, at ^ mask) for at in range(size)])  80.3 us
    ppermute x48, waiting for transfers between devices, step_ring(): lax.ppermute(value, 'fsdp', [(WALK[at], WALK[(at + by) % size]) for at in...  72.9 us
    ppermute x48, starting transfers between devices, step_ring(): lax.ppermute(value, 'fsdp', [(WALK[at], WALK[(at + by) % size]) for at in...  62.5 us
    unnamed x360, local copies, waits for them, and re-layouts  48.1 us
    dot_general x8, matrix products, weight_grad(): lax.dot_general(left, right, (((0, 1), (0, 1)), ((), ())), preferred_elem...  29.7 us
    ppermute x33, starting transfers between devices, permute(): return lax.ppermute(value, axis, [(at, at ^ mask) for at in range(size)])  24.7 us
  transfers between devices with their start and end apart: 82, of which 38 were waited for; matrix products, arithmetic and copies ran while one was open for 12% of the time, Pallas kernels for 28%

profile of v5, /device:TPU:0, one launch (start us, length us, event | category | flops | bytes accessed | tf_op | source)
XLA Modules:
  0.0 608.4 jit_solution(17419267464626308139)
XLA Ops:
  47.1 5.9 collective-permute-done.9
  58.4 10.5 %collective-permute-done.13.refs_19_.refs_14_ = bf16[96,768]{1,0:T(8,128)(2,1)S(1)} collective-permute-done((bf16[96,768]{1,0:T(8,128)(2,1)}, bf16[96,768]{1,0:T(8,128)(2,1)S(1)}, u32[]{:S(2)}, u32[]{:S(2)}) %collective-permute-start.13) | collective-permute-done | bytes 147488 | tf_op jit(solution)/shard_map/ppermute | solution.py:62
  95.7 22.2 %project_scan.2 = (bf16[4,256,1536]{2,1,0:T(8,128)(2,1)}, bf16[4,256,768]{2,1,0:T(8,128)(2,1)}, f32[4,256,256]{2,1,0:T(8,128)}, f32[4,16,256]{2,1,0:T(8,128)S(1)...) custom-call(s32[9]{0:T(128)S(1)} %pad_add_fusion.t_ref, bf16[256,1536]{1,0:T(8,128)(2,1)S(1)} %copy-done.14, ...), custom_call_target="tpu_custom_call" | custom-call | flops 10000000000 | bytes 17741824 | tf_op jit(solution)/shard_map/project_scan/pallas_call | solution.py:864
  120.3 5.7 collective-permute-done.23.refs_10_.refs_19_.refs_14_.refs_23_
  129.0 11.7 %collective-permute-start.26 = (bf16[192,2304]{1,0:T(8,128)(2,1)S(1)}, bf16[192,2304]{1,0:T(8,128)(2,1)}, u32[]{:S(2)}, u32[]{:S(2)}) collective-permute-start(bf16[192,2304]{1,0:T(8,128)(2,1)S(1)} %pad_maximum_fusion.2.refs_12_.refs_7_.refs_16_), channel_id=1, source_target_pairs={{0,4},{8,0},{16,8},{24,16},{28,24},{20,28},{12,20},{4,12},{1,5},{9... | collective-permute-start | bytes 2654216 | tf_op jit(solution)/shard_map/ppermute | solution.py:62
  140.7 13.4 %gate_forward.2 = (bf16[4,256,768]{2,1,0:T(8,128)(2,1)}, bf16[2,256,1664]{2,1,0:T(8,128)(2,1)}, bf16[2,256,1664]{2,1,0:T(8,128)(2,1)}) custom-call(s32[9]{0:T(128)S(1)} %pad_add_fusion.t_ref, bf16[4,256,1536]{2,1,0:T(8,128)(2,1)} %get-tuple-element.226.refs_0_.refs_4_, f32[4,256,768]{2,1,0:T(8,128)} %get-tuple-element.231.refs_1_.refs_6_, ...), custom_call_target="tpu_custom_call" | custom-call | flops 6000000000 | bytes 20758528 | tf_op jit(solution)/shard_map/gate_forward/pallas_call | solution.py:864
  175.5 13.7 %collective-permute-done.28 = bf16[256,1664]{1,0:T(8,128)(2,1)} collective-permute-done((bf16[256,1664]{1,0:T(8,128)(2,1)}, bf16[256,1664]{1,0:T(8,128)(2,1)}, u32[]{:S(2)}, u32[]{:S(2)}) %collective-permute-start.28) | collective-permute-done | bytes 852000 | tf_op jit(solution)/shard_map/ppermute | solution.py:23
  196.9 16.4 %collective-permute-done.32.refs_2_ = bf16[256,1536]{1,0:T(8,128)(2,1)} collective-permute-done((bf16[256,1536]{1,0:T(8,128)(2,1)}, bf16[256,1536]{1,0:T(8,128)(2,1)}, u32[]{:S(2)}, u32[]{:S(2)}) %collective-permute-start.32) | collective-permute-done | bytes 786464 | tf_op jit(solution)/shard_map/ppermute | solution.py:23
  227.8 21.7 %project_scan.3 = (bf16[4,256,1536]{2,1,0:T(8,128)(2,1)}, bf16[4,256,768]{2,1,0:T(8,128)(2,1)}, f32[4,256,256]{2,1,0:T(8,128)}, f32[4,16,256]{2,1,0:T(8,128)S(1)...) custom-call(s32[9]{0:T(128)S(1)} %pad_add_fusion.t_ref, bf16[256,1536]{1,0:T(8,128)(2,1)} %multiply_convert_fusion.refs_0_, ...), custom_call_target="tpu_custom_call" | custom-call | flops 10000000000 | bytes 21870592 | tf_op jit(solution)/shard_map/project_scan/pallas_call | solution.py:864
  249.5 16.5 %gate_forward.3 = (bf16[4,256,768]{2,1,0:T(8,128)(2,1)}, bf16[2,256,1536]{2,1,0:T(8,128)(2,1)}, bf16[2,256,1536]{2,1,0:T(8,128)(2,1)}, bf16[4,256,1536]{2,1,0:T(...) custom-call(s32[9]{0:T(128)S(1)} %pad_add_fusion.t_ref, ...), custom_call_target="tpu_custom_call" | custom-call | flops 6000000000 | bytes 32522240 | tf_op jit(solution)/shard_map/gate_forward/pallas_call | solution.py:864
  271.3 6.2 %gate_backward.2 = (bf16[4,256,768]{2,1,0:T(8,128)(2,1)S(1)}, bf16[4,256,768]{2,1,0:T(8,128)(2,1)S(1)}, bf16[4,256,768]{2,1,0:T(8,128)(2,1)S(1)}, f32[8,768]{1,0:T(8,128)S(1)}) custom-call(s32[9]{0:T(128)S(1)} %pad_add_fusion.t_ref, bf16[4,256,768]{2,1,0:T(8,128)(2,1)} %get-tuple-element.262.refs_0_, f32[4,256,768]{2,1,0:T(8,128)} %get-tuple-element.256.refs_1_.refs_6_, ...), custom_call_target="tpu_custom_call" | custom-call | flops 3000000000 | bytes 11116544 | tf_op jit(solution)/shard_map/gate_backward/pallas_call | solution.py:864
  291.3 27.5 %mix_backward.3 = (bf16[4,256,768]{2,1,0:T(8,128)(2,1)S(1)}, bf16[4,256,256]{2,1,0:T(8,128)(2,1)S(1)}, f32[4,16,256]{2,1,0:T(8,128)S(1)}, f32[8,768]{1,0:T(8,128...) custom-call(s32[9]{0:T(128)S(1)} %pad_add_fusion.t_ref, ...), custom_call_target="tpu_custom_call" | custom-call | flops 8000000000 | bytes 14852096 | tf_op jit(solution)/shard_map/mix_backward/pallas_call | solution.py:864
  322.0 13.4 %input_backward.2 = (bf16[2,256,1536]{2,1,0:T(8,128)(2,1)}, bf16[2,256,1536]{2,1,0:T(8,128)(2,1)}, f32[16,1536]{1,0:T(8,128)S(1)}, f32[1,1536]{1,0:T(1,128)S(1)}) custom-call(s32[9]{0:T(128)S(1)} %pad_add_fusion.t_ref, bf16[4,256,768]{2,1,0:T(8,128)(2,1)} %copy-done.114, bf16[4,256,768]{2,1,0:T(8,128)(2,1)} %copy-done.116, ...), custom_call_target="tpu_custom_call" | custom-call | flops 7000000000 | bytes 24582144 | tf_op jit(solution)/shard_map/input_backward/pallas_call | solution.py:864
  351.9 8.9 %collective-permute-done.51.refs_6_ = bf16[384,768]{1,0:T(8,128)(2,1)S(1)} collective-permute-done((bf16[384,768]{1,0:T(8,128)(2,1)S(1)}, bf16[384,768]{1,0:T(8,128)(2,1)S(1)}, u32[]{:S(2)}, u32[]{:S(2)}) %collective-permute-start.51) | collective-permute-done | bytes 589856 | tf_op jit(solution)/shard_map/ppermute | solution.py:62
  376.9 11.7 %collective-permute-done.57.refs_5_ = bf16[256,1664]{1,0:T(8,128)(2,1)S(1)} collective-permute-done((bf16[256,1664]{1,0:T(8,128)(2,1)S(1)}, bf16[256,1664]{1,0:T(8,128)(2,1)S(1)}, u32[]{:S(2)}, u32[]{:S(2)}) %collective-permute-start.57) | collective-permute-done | bytes 852000 | tf_op jit(solution)/shard_map/ppermute | solution.py:23
  397.2 10.3 %gate_backward.3 = (bf16[4,256,768]{2,1,0:T(8,128)(2,1)}, bf16[4,256,768]{2,1,0:T(8,128)(2,1)}, bf16[4,256,768]{2,1,0:T(8,128)(2,1)}, f32[8,768]{1,0:T(8,128)S(1)}, bf16[4,256,1536]{2,1,0:T(8,128)(2,1)}) custom-call(s32[9]{0:T(128)S(1)} %pad_add_fusion.t_ref, bf16[4,256,768]{2,1,0:T(8,128)(2,1)} %get-tuple-element.301.refs_0_, ...), custom_call_target="tpu_custom_call" | custom-call | flops 3000000000 | bytes 20783104 | tf_op jit(solution)/shard_map/gate_backward/pallas_call | solution.py:864
  407.5 5.2 bitcast_convert_fusion.1
  418.6 14.5 %mix_backward.4 = (bf16[4,256,768]{2,1,0:T(8,128)(2,1)S(1)}, bf16[4,256,256]{2,1,0:T(8,128)(2,1)S(1)}, f32[4,16,256]{2,1,0:T(8,128)S(1)}, f32[8,768]{1,0:T(8,128...) custom-call(s32[9]{0:T(128)S(1)} %pad_add_fusion.t_ref, ...), custom_call_target="tpu_custom_call" | custom-call | flops 4000000000 | bytes 14852096 | tf_op jit(solution)/shard_map/mix_backward/pallas_call | solution.py:864
  440.8 15.1 %mix_backward.5 = (bf16[4,256,768]{2,1,0:T(8,128)(2,1)S(1)}, bf16[4,256,256]{2,1,0:T(8,128)(2,1)S(1)}, f32[4,16,256]{2,1,0:T(8,128)S(1)}, f32[8,768]{1,0:T(8,128...) custom-call(s32[9]{0:T(128)S(1)} %pad_add_fusion.t_ref, ...), custom_call_target="tpu_custom_call", output_to_operand_aliasing={{0}: (15, {}), {1}: (16, {}), {2}: (17, {})} | custom-call | flops 4000000000 | bytes 17530880 | tf_op jit(solution)/shard_map/mix_backward/pallas_call | solution.py:864
  466.9 13.8 %input_backward.3 = (bf16[2,256,1536]{2,1,0:T(8,128)(2,1)}, bf16[2,256,1536]{2,1,0:T(8,128)(2,1)}, f32[16,1536]{1,0:T(8,128)S(1)}, f32[1,1536]{1,0:T(1,128)S(1)}) custom-call(s32[9]{0:T(128)S(1)} %pad_add_fusion.t_ref, bf16[4,256,768]{2,1,0:T(8,128)(2,1)} %copy-done.37, bf16[4,256,768]{2,1,0:T(8,128)(2,1)} %get-tuple-element.313.refs_1_, ...), custom_call_target="tpu_custom_call" | custom-call | flops 7000000000 | bytes 18388992 | tf_op jit(solution)/shard_map/input_backward/pallas_call | solution.py:864
  503.5 4.9 collective-permute-done.70
  508.5 8.2 %collective-permute-done.68.refs_2_.refs_6_ = bf16[576,768]{1,0:T(8,128)(2,1)S(1)} collective-permute-done((bf16[576,768]{1,0:T(8,128)(2,1)}, bf16[576,768]{1,0:T(8,128)(2,1)S(1)}, u32[]{:S(2)}, u32[]{:S(2)}) %collective-permute-start.68) | collective-permute-done | bytes 884768 | tf_op jit(solution)/shard_map/ppermute | solution.py:62
  530.9 6.9 %collective-permute-done.71.refs_2_ = bf16[192,768]{1,0:T(8,128)(2,1)S(1)} collective-permute-done((bf16[192,768]{1,0:T(8,128)(2,1)}, bf16[192,768]{1,0:T(8,128)(2,1)S(1)}, u32[]{:S(2)}, u32[]{:S(2)}) %collective-permute-start.71) | collective-permute-done | bytes 294944 | tf_op jit(solution)/shard_map/ppermute | solution.py:62
  546.4 6.8 %collective-permute-done.74 = bf16[8,98,256]{2,0,1:T(8,128)(2,1)S(1)} collective-permute-done((bf16[8,98,256]{2,0,1:T(8,128)(2,1)}, bf16[8,98,256]{2,0,1:T(8,128)(2,1)S(1)}, u32[]{:S(2)}, u32[]{:S(2)}) %collective-permute-start.74) | collective-permute-done | bytes 401440 | tf_op jit(solution)/shard_map/ppermute | solution.py:23
  (732 shorter events, 300.7 us)
Async XLA Ops:
  7.3 148.3 %all-gather.3.cloned.1.call-start = ((), (), s32[]{:S(2)}) async-start(), calls=%async_computation | async-start | bytes 1081344 | tf_op jit(solution)/shard_map/all_gather | solution.py:1157
  15.0 41.0 %collective-permute-start.18 = (bf16[256,1536]{1,0:T(8,128)(2,1)S(1)}, bf16[256,1536]{1,0:T(8,128)(2,1)}, u32[]{:S(2)}, u32[]{:S(2)}) collective-permute-start(bf16[256,1536]{1,0:T(8,128)(2,1)S(1)} %copy-done.14), channel_id=1, source_target_pairs={{0,2},{1,3},{2,0},{3,1},{4,6},{5,7},{6,4},{7,5},{8,10},{9,11},{10,... | collective-permute-start | bytes 2359304 | tf_op jit(solution)/shard_map/ppermute | solution.py:23
  45.1 24.3 %collective-permute-start.11 = (bf16[192,1536]{1,0:T(8,128)(2,1)S(1)}, bf16[192,1536]{1,0:T(8,128)(2,1)S(1)}, u32[]{:S(2)}, u32[]{:S(2)}) collective-permute-start(bf16[192,1536]{1,0:T(8,128)(2,1)S(1)} %pad_maximum_fusion.3.refs_3_.refs_12_.refs_7_.refs_16_), channel_id=1, source_target_pairs={{0,8},{8,16},{16,24},{24,28},{28,20},{20,12},{12,4},{4,0},{1,9},{9... | collective-permute-start | bytes 1769480 | tf_op jit(solution)/shard_map/ppermute | solution.py:62
  46.6 22.8 %collective-permute-start.12 = (bf16[192,1536]{1,0:T(8,128)(2,1)S(1)}, bf16[192,1536]{1,0:T(8,128)(2,1)}, u32[]{:S(2)}, u32[]{:S(2)}) collective-permute-start(bf16[192,1536]{1,0:T(8,128)(2,1)S(1)} %pad_maximum_fusion.3.refs_3_.refs_12_.refs_7_.refs_16_), channel_id=1, source_target_pairs={{0,4},{8,0},{16,8},{24,16},{28,24},{20,28},{12,20},{4,12},{1,5},{9... | collective-permute-start | bytes 1769480 | tf_op jit(solution)/shard_map/ppermute | solution.py:62
  78.4 39.7 %collective-permute-start.20 = (bf16[256,1536]{1,0:T(8,128)(2,1)S(1)}, bf16[256,1536]{1,0:T(8,128)(2,1)S(1)}, u32[]{:S(2)}, u32[]{:S(2)}) collective-permute-start(bf16[256,1536]{1,0:T(8,128)(2,1)S(1)} %copy-done.26), channel_id=1, source_target_pairs={{0,2},{1,3},{2,0},{3,1},{4,6},{5,7},{6,4},{7,5},{8,10},{9,11},{10,... | collective-permute-start | bytes 2359304 | tf_op jit(solution)/shard_map/ppermute | solution.py:23
  85.1 32.9 %collective-permute-start.21 = (bf16[192,1536]{1,0:T(8,128)(2,1)}, bf16[192,1536]{1,0:T(8,128)(2,1)S(1)}, u32[]{:S(2)}, u32[]{:S(2)}) collective-permute-start(bf16[192,1536]{1,0:T(8,128)(2,1)} %collective-permute-done.15.refs_6_.refs_15_.refs_10_.refs_19_), channel_id=1, source_target_pairs={{0,8},{8,16},{16,24},{24,28},{28,20},{20,12},{12,4},{4,0},{1,9},{9... | collective-permute-start | bytes 1769480 | tf_op jit(solution)/shard_map/ppermute | solution.py:62
  86.7 31.3 %collective-permute-start.22 = (bf16[192,1536]{1,0:T(8,128)(2,1)}, bf16[192,1536]{1,0:T(8,128)(2,1)S(1)}, u32[]{:S(2)}, u32[]{:S(2)}) collective-permute-start(bf16[192,1536]{1,0:T(8,128)(2,1)} %collective-permute-done.16.refs_7_.refs_16_.refs_11_.refs_20_), channel_id=1, source_target_pairs={{0,4},{8,0},{16,8},{24,16},{28,24},{20,28},{12,20},{4,12},{1,5},{9... | collective-permute-start | bytes 1769480 | tf_op jit(solution)/shard_map/ppermute | solution.py:62
  127.6 28.0 %collective-permute-start.25 = (bf16[192,2304]{1,0:T(8,128)(2,1)S(1)}, bf16[192,2304]{1,0:T(8,128)(2,1)S(1)}, u32[]{:S(2)}, u32[]{:S(2)}) collective-permute-start(bf16[192,2304]{1,0:T(8,128)(2,1)S(1)} %pad_maximum_fusion.2.refs_12_.refs_7_.refs_16_), channel_id=1, source_target_pairs={{0,8},{8,16},{16,24},{24,28},{28,20},{20,12},{12,4},{4,0},{1,9},{9... | collective-permute-start | bytes 2654216 | tf_op jit(solution)/shard_map/ppermute | solution.py:62
  129.0 30.1 %collective-permute-start.26 = (bf16[192,2304]{1,0:T(8,128)(2,1)S(1)}, bf16[192,2304]{1,0:T(8,128)(2,1)}, u32[]{:S(2)}, u32[]{:S(2)}) collective-permute-start(bf16[192,2304]{1,0:T(8,128)(2,1)S(1)} %pad_maximum_fusion.2.refs_12_.refs_7_.refs_16_), channel_id=1, source_target_pairs={{0,4},{8,0},{16,8},{24,16},{28,24},{20,28},{12,20},{4,12},{1,5},{9... | collective-permute-start | bytes 2654216 | tf_op jit(solution)/shard_map/ppermute | solution.py:62
  166.4 22.8 %collective-permute-start.29 = (bf16[192,2304]{1,0:T(8,128)(2,1)S(1)}, bf16[192,2304]{1,0:T(8,128)(2,1)}, u32[]{:S(2)}, u32[]{:S(2)}) collective-permute-start(bf16[192,2304]{1,0:T(8,128)(2,1)S(1)} %collective-permute-done.25.refs_13_.refs_8_.refs_17_), channel_id=1, source_target_pairs={{0,8},{8,16},{16,24},{24,28},{28,20},{20,12},{12,4},{4,0},{1,9},{9... | collective-permute-start | bytes 2654216 | tf_op jit(solution)/shard_map/ppermute | solution.py:62
  166.9 22.3 %collective-permute-start.30 = (bf16[192,2304]{1,0:T(8,128)(2,1)}, bf16[192,2304]{1,0:T(8,128)(2,1)}, u32[]{:S(2)}, u32[]{:S(2)}) collective-permute-start(bf16[192,2304]{1,0:T(8,128)(2,1)} %collective-permute-done.26.refs_14_.refs_9_.refs_18_), channel_id=1, source_target_pairs={{0,4},{8,0},{16,8},{24,16},{28,24},{20,28},{12,20},{4,12},{1,5},{9... | collective-permute-start | bytes 2654216 | tf_op jit(solution)/shard_map/ppermute | solution.py:62
  196.9 23.7 %collective-permute-start.31 = (bf16[256,1536]{1,0:T(8,128)(2,1)}, bf16[256,1536]{1,0:T(8,128)(2,1)}, u32[]{:S(2)}, u32[]{:S(2)}) collective-permute-start(bf16[256,1536]{1,0:T(8,128)(2,1)} %multiply_convert_fusion.refs_0_), channel_id=1, source_target_pairs={{0,1},{1,0},{2,3},{3,2},{4,5},{5,4},{6,7},{7,6},{8,9},{9,8},{10,11... | collective-permute-start | bytes 2359304 | tf_op jit(solution)/shard_map/ppermute | solution.py:23
  218.5 31.0 %collective-permute-start.40 = (bf16[256,1536]{1,0:T(8,128)(2,1)S(1)}, bf16[256,1536]{1,0:T(8,128)(2,1)S(1)}, u32[]{:S(2)}, u32[]{:S(2)}) collective-permute-start(bf16[256,1536]{1,0:T(8,128)(2,1)S(1)} %copy-done.27), channel_id=1, source_target_pairs={{0,1},{1,0},{2,3},{3,2},{4,5},{5,4},{6,7},{7,6},{8,9},{9,8},{10,11... | collective-permute-start | bytes 2359304 | tf_op jit(solution)/shard_map/ppermute | solution.py:23
  220.6 28.9 %collective-permute-start.41 = (bf16[256,1536]{1,0:T(8,128)(2,1)S(1)}, bf16[256,1536]{1,0:T(8,128)(2,1)S(1)}, u32[]{:S(2)}, u32[]{:S(2)}) collective-permute-start(bf16[256,1536]{1,0:T(8,128)(2,1)S(1)} %copy-done.43), channel_id=1, source_target_pairs={{0,1},{1,0},{2,3},{3,2},{4,5},{5,4},{6,7},{7,6},{8,9},{9,8},{10,11... | collective-permute-start | bytes 2359304 | tf_op jit(solution)/shard_map/ppermute | solution.py:23
  222.2 27.3 %collective-permute-start.38 = (bf16[96,1536]{1,0:T(8,128)(2,1)S(1)}, bf16[96,1536]{1,0:T(8,128)(2,1)S(1)}, u32[]{:S(2)}, u32[]{:S(2)}) collective-permute-start(bf16[96,1536]{1,0:T(8,128)(2,1)S(1)} %slice.358), channel_id=1, source_target_pairs={{0,8},{8,16},{16,24},{24,28},{28,20},{20,12},{12,4},{4,0},{1,9},{9... | collective-permute-start | bytes 884744 | tf_op jit(solution)/shard_map/ppermute | solution.py:62
  223.2 26.2 %collective-permute-start.39 = (bf16[96,1536]{1,0:T(8,128)(2,1)S(1)}, bf16[96,1536]{1,0:T(8,128)(2,1)S(1)}, u32[]{:S(2)}, u32[]{:S(2)}) collective-permute-start(bf16[96,1536]{1,0:T(8,128)(2,1)S(1)} %slice.359), channel_id=1, source_target_pairs={{0,4},{8,0},{16,8},{24,16},{28,24},{20,28},{12,20},{4,12},{1,5},{9... | collective-permute-start | bytes 884744 | tf_op jit(solution)/shard_map/ppermute | solution.py:62
  283.6 38.3 %collective-permute-start.47 = (bf16[256,1536]{1,0:T(8,128)(2,1)S(1)}, bf16[256,1536]{1,0:T(8,128)(2,1)S(1)}, u32[]{:S(2)}, u32[]{:S(2)}) collective-permute-start(bf16[256,1536]{1,0:T(8,128)(2,1)S(1)} %fusion.14), channel_id=1, source_target_pairs={{0,2},{1,3},{2,0},{3,1},{4,6},{5,7},{6,4},{7,5},{8,10},{9,11},{10,... | collective-permute-start | bytes 2359304 | tf_op jit(solution)/shard_map/ppermute | solution.py:23
  288.8 30.0 %collective-permute-start.45 = (bf16[192,768]{1,0:T(8,128)(2,1)S(1)}, bf16[192,768]{1,0:T(8,128)(2,1)S(1)}, u32[]{:S(2)}, u32[]{:S(2)}) collective-permute-start(bf16[192,768]{1,0:T(8,128)(2,1)S(1)} %get-tuple-element.270), channel_id=1, source_target_pairs={{0,8},{8,16},{16,24},{24,28},{28,20},{20,12},{12,4},{4,0},{1,9},{9... | collective-permute-start | bytes 884744 | tf_op jit(solution)/shard_map/ppermute | solution.py:62
  289.5 29.3 %collective-permute-start.46 = (bf16[192,768]{1,0:T(8,128)(2,1)S(1)}, bf16[192,768]{1,0:T(8,128)(2,1)S(1)}, u32[]{:S(2)}, u32[]{:S(2)}) collective-permute-start(bf16[192,768]{1,0:T(8,128)(2,1)S(1)} %get-tuple-element.271), channel_id=1, source_target_pairs={{0,4},{8,0},{16,8},{24,16},{28,24},{20,28},{12,20},{4,12},{1,5},{9... | collective-permute-start | bytes 884744 | tf_op jit(solution)/shard_map/ppermute | solution.py:62
  434.9 21.4 %collective-permute-start.63 = (bf16[576,768]{1,0:T(8,128)(2,1)}, bf16[576,768]{1,0:T(8,128)(2,1)S(1)}, u32[]{:S(2)}, u32[]{:S(2)}) collective-permute-start(bf16[576,768]{1,0:T(8,128)(2,1)} %get-tuple-element.337), channel_id=1, source_target_pairs={{0,8},{8,16},{16,24},{24,28},{28,20},{20,12},{12,4},{4,0},{1,9},{9... | collective-permute-start | bytes 2654216 | tf_op jit(solution)/shard_map/ppermute | solution.py:62
  495.1 21.6 %collective-permute-start.68 = (bf16[576,768]{1,0:T(8,128)(2,1)}, bf16[576,768]{1,0:T(8,128)(2,1)S(1)}, u32[]{:S(2)}, u32[]{:S(2)}) collective-permute-start(bf16[576,768]{1,0:T(8,128)(2,1)} %get-tuple-element.365), channel_id=1, source_target_pairs={{0,8},{8,16},{16,24},{24,28},{28,20},{20,12},{12,4},{4,0},{1,9},{9... | collective-permute-start | bytes 2654216 | tf_op jit(solution)/shard_map/ppermute | solution.py:62
  496.7 21.6 %collective-permute-start.69 = (bf16[576,768]{1,0:T(8,128)(2,1)}, bf16[576,768]{1,0:T(8,128)(2,1)}, u32[]{:S(2)}, u32[]{:S(2)}) collective-permute-start(bf16[576,768]{1,0:T(8,128)(2,1)} %get-tuple-element.366), channel_id=1, source_target_pairs={{0,4},{8,0},{16,8},{24,16},{28,24},{20,28},{12,20},{4,12},{1,5},{9... | collective-permute-start | bytes 2654216 | tf_op jit(solution)/shard_map/ppermute | solution.py:62
  544.4 36.2 %collective-permute-start.79 = (bf16[192,768]{1,0:T(8,128)(2,1)}, bf16[192,768]{1,0:T(8,128)(2,1)S(1)}, u32[]{:S(2)}, u32[]{:S(2)}) collective-permute-start(bf16[192,768]{1,0:T(8,128)(2,1)} %copy-done.107), channel_id=1, source_target_pairs={{0,8},{8,16},{16,24},{24,28},{28,20},{20,12},{12,4},{4,0},{1,9},{9... | collective-permute-start | bytes 884744 | tf_op jit(solution)/shard_map/ppermute | solution.py:62
  545.5 35.0 %collective-permute-start.80 = (bf16[192,768]{1,0:T(8,128)(2,1)}, bf16[192,768]{1,0:T(8,128)(2,1)}, u32[]{:S(2)}, u32[]{:S(2)}) collective-permute-start(bf16[192,768]{1,0:T(8,128)(2,1)} %copy-done.106), channel_id=1, source_target_pairs={{0,4},{8,0},{16,8},{24,16},{28,24},{20,28},{12,20},{4,12},{1,5},{9... | collective-permute-start | bytes 884744 | tf_op jit(solution)/shard_map/ppermute | solution.py:62
  (235 other events, 2296.3 us)
Sparse Core Ops, SparseCore 0:
  16.0 57.4 all-gather.2
